TPU v7x, 256 devices: a whole 4x4x8 slice. The times are simulated.
256 devices in a mesh: dp: 16 (over y, z_hi, core), ctx: 16 (over z_lo, x).
Axes of the slice: x: 4, y: 4, z: 8 (z_hi: 2, z_lo: 4; z = z_hi * 4 + z_lo), core: 2. Of those that a mesh axis runs over, the one named last changes fastest.
Arguments:
- layer_input: bfloat16 [16, 4096, 8192], P('dp', 'ctx'), may hold values from -6 to 6
- kv_weight: bfloat16 [8192, 256], P('dp'), may hold values from -0.0625 to 0.0625
- kv_stored: bfloat16 [16, 4096, 256], P('dp', 'ctx'), may hold values from -4.5 to 4.5
- queries: bfloat16 [16, 4096, 2048], P('dp', 'ctx'), may hold values from -145 to 145
- grad_out: bfloat16 [16, 4096, 2048], P('dp', 'ctx'), may hold values from -6 to 6
- positions: int32 [4096], P('ctx'), may hold values from 0 to 4095, as said below
Outputs:
- query_grad: bfloat16 [16, 4096, 2048], P('dp', 'ctx')
- input_grad: bfloat16 [16, 4096, 8192], P('dp', 'ctx')
- weight_grad: float32 [8192, 256], P(('dp', 'ctx'))
Inputs may be any that keep to these rules, and one draw needn't show every extreme that they name: A permutation of the positions; the 256 slots of index c of ctx hold two blocks of 128 consecutive ascending positions, blocks p and 31 - p of the sequence for some p, in either order.
All inputs are finite; a program needn't handle non-finite values.
Results may differ from a plain program's by a relative error of at most 0.022.
Values may be sent and summed in bfloat16 or wider, within the bound.
No kernel may reach another device: no remote copies, remote signals or barrier semaphores. Data moves between devices by JAX's collectives and lax.ppermute only.
A program may use at most 128 MiB of HBM per device.

v0:
```python
import math

import jax
import jax.numpy as jnp
from jax import lax
from jax.sharding import PartitionSpec as P

masked_score = -1e30


def block_scores(query_block, key_block, query_pos, key_pos, scale):
    scores = (
        jnp.einsum("thd,kd->thk", query_block, key_block, preferred_element_type=jnp.float32)
        * scale
    )
    visible = key_pos[None, None, :] <= query_pos[:, None, None]
    return (scores, visible)


def keep_state(inner):
    return inner


def body(layer_input, kv_weight, kv_stored, queries, grad_out, positions):
    head_dim = kv_weight.shape[1] // 2
    tok_rows = queries.shape[1]
    head_count = queries.shape[2] // head_dim
    block_rows = tok_rows // 2
    ctx_size = lax.axis_size("ctx")
    data_size = lax.axis_size("dp")
    seq_rows = tok_rows * ctx_size
    scale = 1.0 / math.sqrt(head_dim)
    query_parts = queries[0].reshape(2, block_rows, head_count, head_dim)
    grad_parts = grad_out[0].reshape(2, block_rows, head_count, head_dim)
    query_pos = positions.reshape(2, block_rows)
    last_pos = jnp.max(query_pos, axis=1)
    stat_one = (
        jnp.full((block_rows, head_count), masked_score, jnp.float32),
        jnp.zeros((block_rows, head_count), jnp.float32),
        jnp.zeros((block_rows, head_count, head_dim), jnp.float32),
    )
    stats_init = (stat_one, stat_one)
    acc_zero = jnp.zeros((block_rows, head_count, head_dim), jnp.float32)
    grads_init = ((acc_zero, acc_zero), jnp.zeros((seq_rows, 2 * head_dim), jnp.float32))
    kv_piece = lax.all_gather(kv_stored[0], "ctx", axis=0, tiled=True)
    pos_piece = lax.all_gather(positions, "ctx", axis=0, tiled=True)
    blocks = kv_piece.shape[0] // block_rows

    def stats_step(block_index, state):
        key_block = lax.dynamic_slice_in_dim(kv_piece, block_index * block_rows, block_rows, 0)
        key_pos = lax.dynamic_slice_in_dim(pos_piece, block_index * block_rows, block_rows, 0)
        first_key = jnp.min(key_pos)
        updated = []
        for side in range(2):

            def stats_update(inner, side=side):
                running, total, accum = inner
                scores, visible = block_scores(
                    query_parts[side], key_block[:, :head_dim], query_pos[side], key_pos, scale
                )
                new_top = jnp.maximum(
                    running, jnp.max(jnp.where(visible, scores, masked_score), axis=-1)
                )
                weights = jnp.where(visible, jnp.exp(scores - new_top[..., None]), 0.0)
                factor = jnp.exp(running - new_top)
                weights_low = weights.astype(jnp.bfloat16)
                accum = accum * factor[..., None] + jnp.einsum(
                    "thk,kd->thd",
                    weights_low,
                    key_block[:, head_dim:],
                    preferred_element_type=jnp.float32,
                )
                return (new_top, total * factor + jnp.sum(weights, axis=-1), accum)

            updated.append(
                lax.cond(first_key <= last_pos[side], stats_update, keep_state, state[side])
            )
        return tuple(updated)

    stats = lax.fori_loop(0, blocks, stats_step, stats_init)
    finish_lse_parts = jnp.stack([stats[side][0] + jnp.log(stats[side][1]) for side in range(2)])
    out_parts = jnp.stack([stats[side][2] / stats[side][1][..., None] for side in range(2)])
    finish_dvec = jnp.sum(grad_parts.astype(jnp.float32) * out_parts, axis=-1)
    grads_kv_piece = lax.all_gather(kv_stored[0], "ctx", axis=0, tiled=True)
    grads_pos_piece = lax.all_gather(positions, "ctx", axis=0, tiled=True)
    blocks = grads_kv_piece.shape[0] // block_rows

    def grads_step(block_index, state):
        query_acc, key_grads = state
        key_block = lax.dynamic_slice_in_dim(
            grads_kv_piece, block_index * block_rows, block_rows, 0
        )
        key_pos = lax.dynamic_slice_in_dim(grads_pos_piece, block_index * block_rows, block_rows, 0)
        first_key = jnp.min(key_pos)
        row_start = block_index * block_rows
        new_acc = []
        for side in range(2):

            def grads_update(inner, side=side):
                acc_side, grads_all = inner
                scores, visible = block_scores(
                    query_parts[side], key_block[:, :head_dim], query_pos[side], key_pos, scale
                )
                prob = jnp.where(visible, jnp.exp(scores - finish_lse_parts[side][..., None]), 0.0)
                dprob = jnp.einsum(
                    "thd,kd->thk",
                    grad_parts[side],
                    key_block[:, head_dim:],
                    preferred_element_type=jnp.float32,
                )
                dscore = (prob * (dprob - finish_dvec[side][..., None]) * scale).astype(
                    jnp.bfloat16
                )
                prob_low = prob.astype(jnp.bfloat16)
                acc_side = acc_side + jnp.einsum(
                    "thk,kd->thd",
                    dscore,
                    key_block[:, :head_dim],
                    preferred_element_type=jnp.float32,
                )
                key_part = jnp.einsum(
                    "thk,thd->kd", dscore, query_parts[side], preferred_element_type=jnp.float32
                )
                value_part = jnp.einsum(
                    "thk,thd->kd", prob_low, grad_parts[side], preferred_element_type=jnp.float32
                )
                previous = lax.dynamic_slice_in_dim(grads_all, row_start, block_rows, 0)
                fresh = previous + jnp.concatenate([key_part, value_part], axis=1)
                grads_all = lax.dynamic_update_slice_in_dim(grads_all, fresh, row_start, 0)
                return (acc_side, grads_all)

            acc_side, key_grads = lax.cond(
                first_key <= last_pos[side], grads_update, keep_state, (query_acc[side], key_grads)
            )
            new_acc.append(acc_side)
        return (tuple(new_acc), key_grads)

    query_acc, key_grads = lax.fori_loop(0, blocks, grads_step, grads_init)
    owned = lax.psum_scatter(key_grads.astype(jnp.bfloat16), "ctx", scatter_dimension=0, tiled=True)
    query_grad = jnp.concatenate([query_acc[0], query_acc[1]], axis=0)
    query_grad = query_grad.reshape(1, tok_rows, head_count * head_dim).astype(jnp.bfloat16)
    input_grad = lax.dot_general(
        owned,
        lax.all_gather(kv_weight, "dp", axis=0, tiled=True),
        (((1,), (1,)), ((), ())),
        preferred_element_type=jnp.float32,
    ).astype(jnp.bfloat16)[None]
    grad_scale = 1.0 / math.sqrt(data_size * seq_rows)
    features = layer_input[0]
    weight_grad = lax.psum_scatter(
        lax.dot_general(
            features, owned, (((0,), (0,)), ((), ())), preferred_element_type=jnp.float32
        )
        * grad_scale,
        ("dp", "ctx"),
        scatter_dimension=0,
        tiled=True,
    )
    return (query_grad, input_grad, weight_grad)


def solution(mesh):
    placed = (
        P("dp", "ctx", None),
        P("dp", None),
        P("dp", "ctx", None),
        P("dp", "ctx", None),
        P("dp", "ctx", None),
        P("ctx"),
    )
    return jax.shard_map(
        body,
        mesh=mesh,
        in_specs=placed,
        out_specs=(P("dp", "ctx", None), P("dp", "ctx", None), P(("dp", "ctx"), None)),
        check_vma=False,
    )
```

profile of v0, /device:TPU:0, one launch (start us, length us, event | category | flops | bytes accessed | tf_op | source)
XLA Modules:
  0.0 2155.3 jit_solution(2700628055875318978)
XLA Ops:
  13.0 41.8 %all-gather.1 = s32[16,1,256]{2,1,0:T(1,128)S(1)} all-gather(s32[1,1,256]{2,1,0:T(1,128)S(1)} %bitcast.135), channel_id=1, replica_groups=mesh['dp'=16,'ctx'=16] {'ctx'}, dimensions={0}, use_global_device_ids=true | all-gather | bytes 17408 | tf_op jit(solution)/shard_map/all_gather | solution.py:85
  54.9 40.4 %all-gather.7.cloned.1.call-done = bf16[1,4096,256]{2,1,0:T(8,128)(2,1)} async-done(((bf16[1,256,256]{2,1,0:T(8,128)(2,1)}), bf16[1,4096,256]{2,1,0:T(8,128)(2,1)}) %all-gather.7.cloned.1.call-update) | async-done | bytes 2097168 | tf_op jit(solution)/shard_map/all_gather | solution.py:84
  95.6 232.0 %while.40 = (s32[]{:T(128)}, f32[128,16]{0,1:T(8,128)S(1)}, f32[128,16]{0,1:T(8,128)S(1)}, f32[128,16,128]{2,0,1:T(8,128)S(1)}, f32[128,16]{0,1:T(8,128)S(1)}, /...) while((s32[]{:T(128)}, f32[128,16]{0,1:T(8,128)S(1)}, ...), condition=%wide.region_11.12_spmd, body=%wide.region_1.11_spmd.sunk | while | flops 274243712 | bytes 12195291 | solution.py:80
  334.5 405.6 %while.41 = (s32[]{:T(128)}, f32[128,16,128]{2,0,1:T(8,128)}, f32[128,16,128]{2,0,1:T(8,128)}, f32[4096,256]{0,1:T(8,128)}, s32[4096]{0:T(1024)S(1)}, /*index=5*...) while((s32[]{:T(128)}, f32[128,16,128]{2,0,1:T(8,128)}, ...), condition=%wide.region_19.20_spmd, body=%wide.region_13.19_spmd.sunk | while | flops 675971200 | bytes 19338816 | solution.py:138
  337.8 7.8 conditional.10
  350.3 7.8 conditional.10
  359.3 7.8 conditional.11
  370.5 7.8 conditional.10
  379.5 7.8 conditional.11
  409.0 7.8 conditional.11
  424.9 7.8 conditional.10
  449.7 7.8 conditional.10
  469.9 7.8 conditional.10
  482.3 7.8 conditional.10
  494.8 7.8 conditional.10
  507.2 7.8 conditional.10
  519.7 7.8 conditional.10
  549.2 7.8 conditional.10
  569.4 7.8 conditional.10
  578.4 7.8 conditional.11
  594.3 7.8 conditional.10
  619.1 7.8 conditional.10
  644.0 7.8 conditional.10
  653.0 7.8 conditional.11
  673.5 7.8 conditional.10
  693.7 7.8 conditional.10
  706.1 7.8 conditional.10
  718.6 7.8 conditional.10
  731.0 7.8 conditional.10
  744.7 100.2 %reduce-scatter.5.cloned.1.call-done = bf16[256,256]{0,1:T(8,128)(2,1)} async-done(((bf16[4096,256]{0,1:T(8,128)(2,1)}), bf16[256,256]{0,1:T(8,128)(2,1)}) %reduce-scatter.5.cloned.1.call-update) | async-done | bytes 131088 | tf_op jit(solution)/shard_map/reduce_scatter | solution.py:139
  851.7 9.0 copy.54
  869.9 1278.2 %reduce-scatter.7.cloned.1.call-done = f32[32,256]{1,0:T(8,128)} async-done(((f32[8192,256]{1,0:T(8,128)}), f32[32,256]{1,0:T(8,128)}) %reduce-scatter.7.cloned.1.call-update) | async-done | bytes 32784
  (905 shorter events, 646.4 us)
Async XLA Ops:
  8.0 3.5 copy-start.3
  8.0 87.3 %all-gather.7.cloned.1.call-start = ((), (), s32[]{:S(2)}) async-start(), calls=%async_computation.4 | async-start | bytes 2228224 | tf_op jit(solution)/shard_map/all_gather | solution.py:84
  8.7 836.2 %reduce-scatter.5.cloned.1.call-start = ((), (), s32[]{:S(2)}) async-start(), calls=%async_computation.2 | async-start | bytes 2228224 | tf_op jit(solution)/shard_map/reduce_scatter | solution.py:139
  8.8 4.2 copy-start.5
  11.7 1.0 copy-start.1
  327.7 1.3 copy-start.2
  743.9 120.5 %all-gather.5.cloned.1.call-start = ((), (), s32[]{:S(2)}) async-start(), calls=%async_computation.3 | async-start | bytes 4456448 | tf_op jit(solution)/shard_map/all_gather | solution.py:144
  744.5 1403.7 %reduce-scatter.7.cloned.1.call-start = ((), (), s32[]{:S(2)}) async-start(), calls=%async_computation.5 | async-start | bytes 8421376
  860.7 1.5 copy-start
  862.1 2.3 copy-start.4
Sparse Core Ops, SparseCore 0:
  10.6 84.6 all-gather.6
  744.0 100.8 reduce-scatter.4
  860.8 1287.2 reduce-scatter.6
Sparse Core Ops, SparseCore 1:
  747.1 69.1 all-gather.4
where the time goes:
time: 2170 us; the launch traced here: 2160 us
  waiting for transfers between devices  1420 us (65%)
  matrix products  278 us (13%)
  loops' own time  166 us (8%)
  other arithmetic  119 us (5%)
  local copies, waits for them, and re-layouts  115 us (5%)
  blocking collectives  41.8 us (2%)
    unnamed x5, waiting for transfers between devices  1280 us
    reduce_scatter x1, waiting for transfers between devices, body(): lax.psum_scatter(key_grads.astype(jnp.bfloat16), 'ctx', scatter_dimension...  100 us
    dot_general x66, matrix products, block_scores(): jnp.einsum('thd,kd->thk', query_block, key_block, preferred_element_type=...  92.1 us
    dot_general x33, matrix products, grads_update(): jnp.einsum('thk,kd->thd', dscore, key_block[:, :head_dim], preferred_elem...  81.7 us
    another operation x1, loops' own time, body(): stats = lax.fori_loop(0, blocks, stats_step, stats_init)  81.7 us
    another operation x1, loops' own time, body(): query_acc, key_grads = lax.fori_loop(0, blocks, grads_step, grads_init)  78.4 us
    dynamic_update_slice x33, other arithmetic, grads_update(): grads_all = lax.dynamic_update_slice_in_dim(grads_all, fresh, row_start, 0)  52.2 us
    dot_general x33, matrix products, grads_update(): jnp.einsum('thk,thd->kd', dscore, query_parts[side], preferred_element_ty...  45.7 us
  transfers between devices with their start and end apart: 4, of which 3 were waited for; matrix products, arithmetic and copies ran while one was open for 1% of the time, Pallas kernels for 0%

commit v1 on v0

v1 whole, which is shorter than its diff:
```python
import functools
import math

import jax
import jax.numpy as jnp
from jax import lax
from jax.experimental import pallas as pl
from jax.experimental.pallas import tpu as pltpu
from jax.sharding import PartitionSpec as P

BLK = 128
TAG = 16
MASKED = -1e30


def mm(a, b):
    return lax.dot_general(a, b, (((1,), (0,)), ((), ())), preferred_element_type=jnp.float32)


def mm_nt(a, b):
    return lax.dot_general(a, b, (((1,), (1,)), ((), ())), preferred_element_type=jnp.float32)


def attn_kernel(
    G,
    KC,
    blocks,
    scale,
    q_ref,
    do_ref,
    near_ref,
    left_ref,
    right_ref,
    far_a_ref,
    far_b_ref,
    dq_ref,
    keep_ref,
    plus_ref,
    minus_ref,
    plus_late_ref,
    minus_late_ref,
    kvs,
    kT,
    s_scr,
    dp_scr,
    acc,
    dqT,
    qr,
    dor,
    p_even,
    d_even,
    p_odd,
    d_odd,
    first_ref,
):
    R = G * BLK
    c = scale * math.log2(math.e)
    side = pl.program_id(0)
    grp = pl.program_id(1)
    toks = 2 * BLK
    owners = blocks // 2

    @pl.when((side == 0) & (grp == 0))
    def _():
        acc[...] = jnp.zeros_like(acc)
        owner = 0
        for piece in (near_ref, left_ref, right_ref, far_a_ref, far_b_ref):
            for i in range(piece.shape[0] // (toks + TAG)):
                base = i * (toks + TAG)
                mark = piece[base + toks : base + toks + TAG, :BLK].astype(jnp.float32)
                first = jnp.max(mark).astype(jnp.int32)
                first_ref[owner] = first
                for half, place in ((0, first), (1, blocks - 1 - first)):
                    dst = pl.ds(pl.multiple_of(place * BLK, BLK), BLK)
                    blk = piece[base + half * BLK : base + (half + 1) * BLK, :]
                    kvs[dst, :] = blk
                    kT[:, dst] = blk[:, :BLK].T
                owner += 1

    for h in range(G):
        cols = slice(h * BLK, (h + 1) * BLK)
        qr[cols, :] = q_ref[:, cols]
        dor[cols, :] = do_ref[:, cols]
    dqT[...] = jnp.zeros_like(dqT)
    qb = jnp.where(side == 0, first_ref[0], blocks - 1 - first_ref[0])
    nk = (qb + KC // BLK) // (KC // BLK)

    def scores(kc, state, masked):
        m, l, d = state
        rows = pl.ds(pl.multiple_of(kc * KC, KC), KC)
        s = mm_nt(kvs[rows, :BLK], qr[...])
        dp = mm_nt(kvs[rows, BLK:], dor[...])
        if masked:
            kpos = kc * KC + lax.broadcasted_iota(jnp.int32, (KC, R), 0)
            qpos = qb * BLK + (lax.broadcasted_iota(jnp.int32, (KC, R), 1) & (BLK - 1))
            s = jnp.where(kpos <= qpos, s, MASKED)
        s_scr[rows, :] = s
        dp_scr[rows, :] = dp
        s3 = s.reshape(KC // 8, 8, R)
        new = jnp.maximum(m, jnp.max(s3, axis=0))
        p = jnp.exp2((s3 - new[None]) * c)
        f = jnp.exp2((m - new) * c)
        l = l * f + jnp.sum(p, axis=0)
        d = d * f + jnp.sum(p * dp.reshape(KC // 8, 8, R), axis=0)
        return new, l, d

    init = (
        jnp.full((8, R), MASKED, jnp.float32),
        jnp.zeros((8, R), jnp.float32),
        jnp.zeros((8, R), jnp.float32),
    )
    state = lax.fori_loop(0, nk - 1, lambda kc, st: scores(kc, st, False), init)
    m, l, d = scores(nk - 1, state, True)
    top = jnp.max(m, axis=0, keepdims=True)
    f = jnp.exp2((m - top) * c)
    total = jnp.sum(l * f, axis=0, keepdims=True)
    dvec = jnp.sum(d * f, axis=0, keepdims=True) / total
    lse = top * c + jnp.log2(total)

    def weigh(kc, p_buf, d_buf):
        rows = pl.ds(pl.multiple_of(kc * KC, KC), KC)
        p = jnp.exp2(s_scr[rows, :] * c - lse)
        d_buf[...] = (p * (dp_scr[rows, :] - dvec)).astype(jnp.bfloat16)
        p_buf[...] = p.astype(jnp.bfloat16)

    def spend(kc, p_buf, d_buf):
        rows = pl.ds(pl.multiple_of(kc * KC, KC), KC)
        dqT[...] += mm(kT[:, rows], d_buf[...])
        acc[rows, :BLK] += mm(d_buf[...], qr[...])
        acc[rows, BLK:] += mm(p_buf[...], dor[...])

    def pair(t, _):
        kc = 2 * t
        weigh(kc + 1, p_odd, d_odd)
        spend(kc, p_even, d_even)
        weigh(jnp.minimum(kc + 2, nk - 1), p_even, d_even)
        spend(kc + 1, p_odd, d_odd)
        return 0

    weigh(0, p_even, d_even)
    lax.fori_loop(0, nk // 2, pair, 0)

    @pl.when(nk % 2 == 1)
    def _():
        spend(nk - 1, p_even, d_even)

    for h in range(G):
        cols = slice(h * BLK, (h + 1) * BLK)
        dq_ref[:, cols] = (dqT[:, cols].T * scale).astype(jnp.bfloat16)

    @pl.when((side == pl.num_programs(0) - 1) & (grp == pl.num_programs(1) - 1))
    def _():
        span = owners // NX
        cut = span // 2
        for owner in range(owners):
            dx, dz = owner // span, owner % span
            late = dz >= cut
            if dx == 0:
                out, row = keep_ref, dz
            elif dx == 1:
                out, row = (minus_late_ref, dz - cut) if late else (minus_ref, dz)
            elif dx == 2:
                out, row = (plus_ref, dz) if late else (plus_late_ref, dz)
            else:
                out, row = (minus_ref, dz) if late else (plus_ref, dz)
            first = first_ref[owner]
            for half, place in ((0, first), (1, blocks - 1 - first)):
                src = pl.ds(pl.multiple_of(place * BLK, BLK), BLK)
                dst = slice(row * toks + half * BLK, row * toks + (half + 1) * BLK)
                out[dst, :BLK] = (acc[src, :BLK] * scale).astype(jnp.bfloat16)
                out[dst, BLK:] = acc[src, BLK:].astype(jnp.bfloat16)


def attention(q, do, pieces, seq, G=8, KC=256):
    toks, width = q.shape
    heads = width // BLK
    R = G * BLK
    part = pl.BlockSpec((BLK, R), lambda s, g: (s, g))
    quarter = seq // NX

    def whole(rows):
        return pl.BlockSpec((rows, 2 * BLK), lambda s, g: (0, 0), pipeline_mode=pl.Buffered(1))

    out_rows = (quarter, quarter, quarter, quarter // 2, quarter // 2)
    return pl.pallas_call(
        functools.partial(attn_kernel, G, KC, seq // BLK, 1.0 / math.sqrt(BLK)),
        grid=(2, heads // G),
        in_specs=[part, part, *(whole(piece.shape[0]) for piece in pieces)],
        out_specs=[part, *(whole(rows) for rows in out_rows)],
        scratch_shapes=[
            pltpu.VMEM((seq, 2 * BLK), jnp.bfloat16),
            pltpu.VMEM((BLK, seq), jnp.bfloat16),
            pltpu.VMEM((seq, R), jnp.float32),
            pltpu.VMEM((seq, R), jnp.float32),
            pltpu.VMEM((seq, 2 * BLK), jnp.float32),
            pltpu.VMEM((BLK, R), jnp.float32),
            pltpu.VMEM((R, BLK), jnp.bfloat16),
            pltpu.VMEM((R, BLK), jnp.bfloat16),
            *(pltpu.VMEM((KC, R), jnp.bfloat16) for _ in range(4)),
            pltpu.SMEM((seq // BLK // 2,), jnp.int32),
        ],
        out_shape=[
            jax.ShapeDtypeStruct((toks, width), jnp.bfloat16),
            *(jax.ShapeDtypeStruct((rows, 2 * BLK), jnp.bfloat16) for rows in out_rows),
        ],
        compiler_params=pltpu.CompilerParams(
            dimension_semantics=("arbitrary", "arbitrary"), vmem_limit_bytes=60 * 2**20
        ),
        cost_estimate=pl.CostEstimate(
            flops=40 * 10**9, bytes_accessed=8 * 2**20, transcendentals=2 * 10**7
        ),
    )(q, do, *pieces)


NZ, NX = 4, 4
NY, NH, NC = 4, 2, 2
CORE_PAIRS = [(i, i ^ 1) for i in range(NY * NH * NC)]
FAR_PAIRS = [(i, i ^ NC) for i in range(NY * NH * NC)]


def along_x(array, step):
    pairs = [
        (z * NX + x, z * NX + (x + step) % NX) for z in range(NZ) for x in range(NX)
    ]
    return lax.ppermute(array, "ctx", pairs)


def along_z(array, step):
    pairs = [
        (z * NX + x, (z + step) % NZ * NX + x) for z in range(NZ) for x in range(NX)
    ]
    return lax.ppermute(array, "ctx", pairs)


def along_y(array, step):
    rest = NH * NC
    pairs = [(i, (i + step * rest) % (NY * rest)) for i in range(NY * rest)]
    return lax.ppermute(array, "dp", pairs)


def cut_kernel(core_ref, a_ref, b_ref, mine_ref, theirs_ref):
    mine_ref[0] = a_ref[...].T
    theirs_ref[0] = b_ref[...].T


def cut_features(features, core):
    toks, model = features.shape
    piece = model // (NY * NH * NC)
    out = jax.ShapeDtypeStruct((NY * NH, piece, toks), features.dtype)
    gs = pltpu.PrefetchScalarGridSpec(
        num_scalar_prefetch=1,
        grid=(NY * NH,),
        in_specs=[
            pl.BlockSpec((toks, piece), lambda i, core: (0, NC * i + core[0])),
            pl.BlockSpec((toks, piece), lambda i, core: (0, NC * i + 1 - core[0])),
        ],
        out_specs=[pl.BlockSpec((1, piece, toks), lambda i, core: (i, 0, 0))] * 2,
    )
    return pl.pallas_call(
        cut_kernel,
        grid_spec=gs,
        out_shape=[out, out],
        cost_estimate=pl.CostEstimate(flops=0, bytes_accessed=8 * 2**20, transcendentals=0),
    )(core.reshape(1), features, features)


def project_kernel(factor, at_ref, mine_ref, theirs_ref, grad_ref, other_ref, out_ref):
    total = mm(mine_ref[0], grad_ref[...]) + mm(theirs_ref[0], other_ref[...])
    total = (total * factor).astype(out_ref.dtype)
    rows = total.shape[0] // (NZ * NX)
    for z in range(NZ):
        dz = (z + NZ - at_ref[0]) % NZ
        for x in range(NX):
            dx = (x + NX - at_ref[1]) % NX
            src = (z * NX + x) * rows
            to = pl.multiple_of((dx * NZ + dz) * rows, rows)
            out_ref[0, pl.ds(to, rows), :] = total[src : src + rows, :]


def project(mine, theirs, grad, other, at, start, count, factor):
    _, piece, toks = mine.shape
    width = grad.shape[1]
    features = pl.BlockSpec((1, piece, toks), lambda i, at: (at[2 + start + i], 0, 0))
    gs = pltpu.PrefetchScalarGridSpec(
        num_scalar_prefetch=1,
        grid=(count,),
        in_specs=[
            features,
            features,
            pl.BlockSpec((toks, width), lambda i, at: (0, 0)),
            pl.BlockSpec((toks, width), lambda i, at: (0, 0)),
        ],
        out_specs=pl.BlockSpec((1, piece, width), lambda i, at: (i, 0, 0)),
    )
    return pl.pallas_call(
        functools.partial(project_kernel, factor),
        grid_spec=gs,
        out_shape=jax.ShapeDtypeStruct((count, piece, width), jnp.bfloat16),
        cost_estimate=pl.CostEstimate(
            flops=2**28 * count, bytes_accessed=2**20 * count, transcendentals=0
        ),
    )(at, mine, theirs, grad, other)


def total_of(*parts):
    return sum(part.astype(jnp.float32) for part in parts)


def body(layer_input, kv_weight, kv_stored, queries, grad_out, positions):
    low = jnp.bfloat16
    tok_rows = queries.shape[1]
    width = kv_weight.shape[1]
    ctx_size = lax.axis_size("ctx")
    data_size = lax.axis_size("dp")
    seq_rows = tok_rows * ctx_size
    data_at, ctx_at = lax.axis_index("dp"), lax.axis_index("ctx")
    y_at, far_at, core_at = data_at // (NH * NC), data_at // NC % NH, data_at % NC
    z_at, x_at = ctx_at // NX, ctx_at % NX

    tag = jnp.full((TAG, width), (positions[0] // BLK).astype(low), low)
    tagged = jnp.concatenate([kv_stored[0], tag], axis=0)
    near = jnp.concatenate([tagged, *(along_z(tagged, step) for step in range(1, NZ))], axis=0)
    half = near.shape[0] // 2
    left, right = along_x(near, 1), along_x(near, -1)
    far_a, far_b = along_x(left[:half], 1), along_x(right[half:], -1)

    mine, theirs = cut_features(layer_input[0], core_at)
    query, mine, theirs = lax.optimization_barrier((queries[0], mine, theirs))
    theirs = lax.ppermute(theirs, "dp", CORE_PAIRS)

    query_grad, keep, plus, minus, plus_late, minus_late = attention(
        query, grad_out[0], (near, left, right, far_a, far_b), seq_rows
    )
    weight = lax.all_gather(kv_weight, "dp", axis=0, tiled=True)

    cut = plus_late.shape[0]
    from_left, from_right = along_x(plus, 1), along_x(minus, -1)
    plus_late = total_of(plus_late, from_left[:cut]).astype(low)
    minus_late = total_of(minus_late, from_right[cut:]).astype(low)
    late_left, late_right = along_x(plus_late, 1), along_x(minus_late, -1)
    early = total_of(keep[:cut], late_left, from_right[:cut]).astype(low)
    late = total_of(keep[cut:], from_left[cut:], late_right).astype(low)
    spans = [early[:tok_rows], early[tok_rows:], late[:tok_rows], late[tok_rows:]]
    spans = [spans[0], *(along_z(spans[step], -step) for step in range(1, NZ))]
    owned = total_of(*spans).astype(low)

    other = lax.ppermute(owned, "dp", CORE_PAIRS)

    steps = ((2, 0), (1, 1), (3, 0), (2, 1), (1, 0), (3, 1), (0, 0), (0, 1))
    chunks = [(y_at + dy) % NY * NH + (far_at + dh) % NH for dy, dh in steps]
    at = jnp.stack([z_at, x_at, *chunks]).astype(jnp.int32)

    def terms_for(start, count):
        factor = 1.0 / math.sqrt(data_size * seq_rows)
        return project(mine, theirs, owned, other, at, start, count, factor)

    from_plus = along_y(terms_for(0, 2), 1)
    from_minus = along_y(terms_for(2, 2), -1)
    rest = terms_for(4, 4)
    late_plus = along_y(total_of(rest[0], from_plus[0]).astype(low), 1)
    late_minus = along_y(total_of(rest[1], from_minus[1]).astype(low), -1)
    input_grad = lax.dot_general(
        owned, weight, (((1,), (1,)), ((), ())), preferred_element_type=jnp.float32
    ).astype(low)[None]
    late_plus, late_minus, input_grad = lax.optimization_barrier(
        (late_plus, late_minus, input_grad)
    )
    halves = (
        total_of(rest[2], late_plus, from_minus[0]).astype(low),
        total_of(rest[3], from_plus[1], late_minus).astype(low),
    )
    terms = jnp.stack([half.reshape(NX, -1, width) for half in halves], axis=1)
    terms = terms.reshape(NX, -1, width)
    terms = total_of(terms[0], *(along_x(terms[step], step) for step in range(1, NX))).astype(low)
    terms = terms.reshape(NH, NZ, -1, width)
    terms = total_of(terms[:, 0], *(along_z(terms[:, step], step) for step in range(1, NZ)))
    weight_grad = terms[0] + lax.ppermute(terms[1], "dp", FAR_PAIRS)

    return (query_grad[None], input_grad, weight_grad)


def solution(mesh):
    placed = (
        P("dp", "ctx", None),
        P("dp", None),
        P("dp", "ctx", None),
        P("dp", "ctx", None),
        P("dp", "ctx", None),
        P("ctx"),
    )
    return jax.shard_map(
        body,
        mesh=mesh,
        in_specs=placed,
        out_specs=(P("dp", "ctx", None), P("dp", "ctx", None), P(("dp", "ctx"), None)),
        check_vma=False,
    )
```

time: 2170 us -> 210 us (0.10)
  waiting for transfers between devices: 1420 us -> 67.4 us
  matrix products: 278 us -> 5.49 us
  loops' own time: 166 us -> 0 us
  other arithmetic: 119 us -> 5.44 us
  local copies, waits for them, and re-layouts: 115 us -> 6.64 us
  Pallas kernels: 0 us -> 60 us
  starting transfers between devices: 0.34 us -> 46.5 us
  blocking collectives: 41.8 us -> 0 us
    unnamed x5 -> x1, waiting for transfers between devices: 1280 us -> 0.02 us
    dot_general x233 -> x1, matrix products: 278 us -> 5.49 us  [body(): lax.dot_general(owned, weight, (((1,), (1,)), ((), ())), preferred_elemen...]
    another operation x130 -> x0, loops' own time: 166 us -> none  [the longest x1 81.7 us: body(): stats = lax.fori_loop(0, blocks, stats_step, stats_init)]
    reduce_scatter x1 -> x0, waiting for transfers between devices: 100 us -> none  [body(): lax.psum_scatter(key_grads.astype(jnp.bfloat16), 'ctx', scatter_dimension...]
    ppermute x0 -> x27, waiting for transfers between devices: none -> 67.4 us  [the longest x11 35.5 us: along_x(): return lax.ppermute(array, 'ctx', pairs)]
    pallas_call x0 -> x5, Pallas kernels: none -> 60 us  [the longest x1 41.8 us: attention(): pl.pallas_call(functools.partial(attn_kernel, G, KC, seq // BLK, 1.0 / ma...]
    dynamic_slice x64 -> x0, local copies, waits for them, and re-layouts: 54 us -> none  [the longest x32 27 us: grads_step(): lax.dynamic_slice_in_dim(grads_kv_piece, block_index * block_rows, block_...]
    dynamic_update_slice x33 -> x0, other arithmetic: 52.2 us -> none  [grads_update(): grads_all = lax.dynamic_update_slice_in_dim(grads_all, fresh, row_start, 0)]
  transfers between devices with their start and end apart: 4 -> 28, of which waited for: 3 -> 19; matrix products, arithmetic and copies ran while one was open for 1% -> 6% of each run, Pallas kernels for 0% -> 29%
where the time goes in v1:
time: 210 us; the launch traced here: 208 us
  waiting for transfers between devices  67.4 us (32%)
  Pallas kernels  60 us (29%)
  starting transfers between devices  46.5 us (22%)
  between operations  17 us (8%)
  local copies, waits for them, and re-layouts  6.64 us (3%)
  matrix products  5.49 us (3%)
  other arithmetic  5.44 us (3%)
    pallas_call x1, Pallas kernels, attention(): pl.pallas_call(functools.partial(attn_kernel, G, KC, seq // BLK, 1.0 / ma...  41.8 us
    ppermute x11, waiting for transfers between devices, along_x(): return lax.ppermute(array, 'ctx', pairs)  35.5 us
    ppermute x9, waiting for transfers between devices, along_z(): return lax.ppermute(array, 'ctx', pairs)  19.1 us
    ppermute x11, starting transfers between devices, along_x(): return lax.ppermute(array, 'ctx', pairs)  18.4 us
    ppermute x9, starting transfers between devices, along_z(): return lax.ppermute(array, 'ctx', pairs)  15.7 us
    pallas_call x3, Pallas kernels, project(): pl.pallas_call(functools.partial(project_kernel, factor), grid_spec=gs, o...  11.3 us
    ppermute x4, waiting for transfers between devices, along_y(): return lax.ppermute(array, 'dp', pairs)  10.1 us
    pallas_call x1, Pallas kernels, cut_features(): pl.pallas_call(cut_kernel, grid_spec=gs, out_shape=[out, out], cost_estim...  6.89 us
  transfers between devices with their start and end apart: 28, of which 19 were waited for; matrix products, arithmetic and copies ran while one was open for 6% of the time, Pallas kernels for 29%

profile of v1, /device:TPU:0, one launch (start us, length us, event | category | flops | bytes accessed | tf_op | source)
XLA Modules:
  0.0 208.5 jit_solution(11188381313734467640)
XLA Ops:
  12.2 3.3 %collective-permute-start.1 = (bf16[272,256]{1,0:T(8,128)(2,1)S(1)}, bf16[272,256]{1,0:T(8,128)(2,1)S(1)}, u32[]{:S(2)}, u32[]{:S(2)}) collective-permute-start(bf16[272,256]{1,0:T(8,128)(2,1)S(1)} %concatenate.7), channel_id=1, source_target_pairs={{0,8},{1,9},{2,10},{3,11},{4,12},{5,13},{6,14},{7,15},{8,0},{9,1},... | collective-permute-start | bytes 417800 | tf_op jit(solution)/shard_map/ppermute | solution.py:232
  17.4 3.1 %collective-permute-done = bf16[272,256]{1,0:T(8,128)(2,1)S(1)} collective-permute-done((bf16[272,256]{1,0:T(8,128)(2,1)S(1)}, bf16[272,256]{1,0:T(8,128)(2,1)S(1)}, u32[]{:S(2)}, u32[]{:S(2)}) %collective-permute-start) | collective-permute-done | bytes 139296 | tf_op jit(solution)/shard_map/ppermute | solution.py:232
  20.6 4.1 %collective-permute-done.1 = bf16[272,256]{1,0:T(8,128)(2,1)S(1)} collective-permute-done((bf16[272,256]{1,0:T(8,128)(2,1)S(1)}, bf16[272,256]{1,0:T(8,128)(2,1)S(1)}, u32[]{:S(2)}, u32[]{:S(2)}) %collective-permute-start.1) | collective-permute-done | bytes 139296 | tf_op jit(solution)/shard_map/ppermute | solution.py:232
  26.3 1.8 collective-permute-start.4
  28.0 12.4 %collective-permute-done.3.left_ref = bf16[1088,256]{1,0:T(8,128)(2,1)S(1)} collective-permute-done((bf16[1088,256]{1,0:T(8,128)(2,1)S(1)}, bf16[1088,256]{1,0:T(8,128)(2,1)S(1)}, u32[]{:S(2)}, u32[]{:S(2)}) %collective-permute-start.3) | collective-permute-done | bytes 557088 | tf_op jit(solution)/shard_map/ppermute | solution.py:225
  40.8 3.0 %collective-permute-start.6 = (bf16[544,256]{1,0:T(8,128)(2,1)S(1)}, bf16[544,256]{1,0:T(8,128)(2,1)S(1)}, u32[]{:S(2)}, u32[]{:S(2)}) collective-permute-start(bf16[544,256]{1,0:T(8,128)(2,1)S(1)} %slice.129), channel_id=1, source_target_pairs={{0,3},{1,0},{2,1},{3,2},{4,7},{5,4},{6,5},{7,6},{8,11},{9,8},{10,9... | collective-permute-start | bytes 835592 | tf_op jit(solution)/shard_map/ppermute | solution.py:225
  43.9 6.9 %shard_map.85 = (bf16[8,512,256]{2,1,0:T(8,128)(2,1)}, bf16[8,512,256]{2,1,0:T(8,128)(2,1)}) custom-call(s32[1]{0:T(128)} %bitcast.1.core_ref, bf16[256,8192]{1,0:T(8,128)(2,1)} %bitcast.72, bf16[256,8192]{1,0:T(8,128)(2,1)} %bitcast.73), custom_call_target="tpu_custom_call" | custom-call | bytes 8388608 | tf_op jit(solution)/shard_map/pallas_call | solution.py:259
  51.6 41.8 %shard_map.86 = (bf16[256,2048]{1,0:T(8,128)(2,1)}, bf16[1024,256]{1,0:T(8,128)(2,1)}, bf16[1024,256]{1,0:T(8,128)(2,1)}, bf16[1024,256]{1,0:T(8,128)(2,1)}, bf1...) custom-call(bf16[256,2048]{1,0:T(8,128)(2,1)} %bitcast.82, bf16[256,2048]{1,0:T(8,128)(2,1)} %bitcast.83, ...), custom_call_target="tpu_custom_call" | custom-call | flops 40000000000 | bytes 8388608 | tf_op jit(solution)/shard_map/pallas_call | solution.py:185
  93.6 3.1 %collective-permute-start.10 = (bf16[1024,256]{1,0:T(8,128)(2,1)}, bf16[1024,256]{1,0:T(8,128)(2,1)S(1)}, u32[]{:S(2)}, u32[]{:S(2)}) collective-permute-start(bf16[1024,256]{1,0:T(8,128)(2,1)} %get-tuple-element.26), channel_id=1, source_target_pairs={{0,3},{1,0},{2,1},{3,2},{4,7},{5,4},{6,5},{7,6},{8,11},{9,8},{10,9... | collective-permute-start | bytes 1572872 | tf_op jit(solution)/shard_map/ppermute | solution.py:225
  96.8 10.6 %collective-permute-done.8 = bf16[1024,256]{1,0:T(8,128)(2,1)S(1)} collective-permute-done((bf16[1024,256]{1,0:T(8,128)(2,1)}, bf16[1024,256]{1,0:T(8,128)(2,1)S(1)}, u32[]{:S(2)}, u32[]{:S(2)}) %collective-permute-start.8) | collective-permute-done | bytes 524320 | tf_op jit(solution)/shard_map/ppermute | solution.py:225
  109.9 3.7 %collective-permute-start.12 = (bf16[512,256]{1,0:T(8,128)(2,1)S(1)}, bf16[512,256]{1,0:T(8,128)(2,1)S(1)}, u32[]{:S(2)}, u32[]{:S(2)}) collective-permute-start(bf16[512,256]{1,0:T(8,128)(2,1)S(1)} %add_convert_fusion.3), channel_id=1, source_target_pairs={{0,3},{1,0},{2,1},{3,2},{4,7},{5,4},{6,5},{7,6},{8,11},{9,8},{10,9... | collective-permute-start | bytes 786440 | tf_op jit(solution)/shard_map/ppermute | solution.py:225
  113.6 2.4 %collective-permute-done.9 = bf16[512,256]{1,0:T(8,128)(2,1)S(1)} collective-permute-done((bf16[512,256]{1,0:T(8,128)(2,1)S(1)}, bf16[512,256]{1,0:T(8,128)(2,1)S(1)}, u32[]{:S(2)}, u32[]{:S(2)}) %collective-permute-start.9) | collective-permute-done | bytes 262176 | tf_op jit(solution)/shard_map/ppermute | solution.py:225
  116.0 3.1 %collective-permute-done.12 = bf16[512,256]{1,0:T(8,128)(2,1)S(1)} collective-permute-done((bf16[512,256]{1,0:T(8,128)(2,1)S(1)}, bf16[512,256]{1,0:T(8,128)(2,1)S(1)}, u32[]{:S(2)}, u32[]{:S(2)}) %collective-permute-start.12) | collective-permute-done | bytes 262176 | tf_op jit(solution)/shard_map/ppermute | solution.py:225
  120.3 3.6 %collective-permute-start.14 = (bf16[256,256]{1,0:T(8,128)(2,1)S(1)}, bf16[256,256]{1,0:T(8,128)(2,1)S(1)}, u32[]{:S(2)}, u32[]{:S(2)}) collective-permute-start(bf16[256,256]{1,0:T(8,128)(2,1)S(1)} %get-tuple-element.42), channel_id=1, source_target_pairs={{0,4},{1,5},{2,6},{3,7},{4,8},{5,9},{6,10},{7,11},{8,12},{9,13},{1... | collective-permute-start | bytes 393224 | tf_op jit(solution)/shard_map/ppermute | solution.py:232
  124.2 2.3 %collective-permute-start.11 = (bf16[256,256]{1,0:T(8,128)(2,1)S(1)}, bf16[256,256]{1,0:T(8,128)(2,1)S(1)}, u32[]{:S(2)}, u32[]{:S(2)}) collective-permute-start(bf16[256,256]{1,0:T(8,128)(2,1)S(1)} %slice.133), channel_id=1, source_target_pairs={{0,12},{1,13},{2,14},{3,15},{4,0},{5,1},{6,2},{7,3},{8,4},{9,5},{1... | collective-permute-start | bytes 393224 | tf_op jit(solution)/shard_map/ppermute | solution.py:232
  126.5 2.2 %collective-permute-done.14 = bf16[256,256]{1,0:T(8,128)(2,1)S(1)} collective-permute-done((bf16[256,256]{1,0:T(8,128)(2,1)S(1)}, bf16[256,256]{1,0:T(8,128)(2,1)S(1)}, u32[]{:S(2)}, u32[]{:S(2)}) %collective-permute-start.14) | collective-permute-done | bytes 131104 | tf_op jit(solution)/shard_map/ppermute | solution.py:232
  128.7 4.2 %collective-permute-done.13 = bf16[256,256]{1,0:T(8,128)(2,1)S(1)} collective-permute-done((bf16[256,256]{1,0:T(8,128)(2,1)S(1)}, bf16[256,256]{1,0:T(8,128)(2,1)S(1)}, u32[]{:S(2)}, u32[]{:S(2)}) %collective-permute-start.13) | collective-permute-done | bytes 131104 | tf_op jit(solution)/shard_map/ppermute | solution.py:232
  136.4 3.1 %shard_map.89 = bf16[2,512,256]{2,1,0:T(8,128)(2,1)} custom-call(s32[10]{0:T(128)} %stack.46.at_ref, bf16[8,512,256]{2,1,0:T(8,128)(2,1)} %get-tuple-element.21.mine_ref, bf16[8,512,256]{2,1,0:T(8,128)(2,1)} %copy-done, bf16[256,256]{1,0:T(8,128)(2,1)} %copy-done.2, bf16[256,256]{1,0:T(8,128)(2,1)} %copy-done.4), custom_call_target="tpu_custom_call" | custom-call | flops 536870912 | bytes 2097152 | tf_op jit(solution)/shard_map/pallas_call | solution.py:295
  139.6 3.0 %collective-permute-start.18 = (bf16[2,512,256]{2,1,0:T(8,128)(2,1)}, bf16[2,512,256]{2,1,0:T(8,128)(2,1)S(1)}, u32[]{:S(2)}, u32[]{:S(2)}) collective-permute-start(bf16[2,512,256]{2,1,0:T(8,128)(2,1)} %shard_map.89), channel_id=1, source_target_pairs={{0,192},{16,208},{32,224},{48,240},{64,0},{80,16},{96,32},{112,48}... | collective-permute-start | bytes 1572872 | tf_op jit(solution)/shard_map/ppermute | solution.py:238
  142.6 3.2 %shard_map.88 = bf16[2,512,256]{2,1,0:T(8,128)(2,1)} custom-call(s32[10]{0:T(128)} %stack.46.at_ref, bf16[8,512,256]{2,1,0:T(8,128)(2,1)} %get-tuple-element.21.mine_ref, bf16[8,512,256]{2,1,0:T(8,128)(2,1)} %copy-done, bf16[256,256]{1,0:T(8,128)(2,1)} %copy-done.2, bf16[256,256]{1,0:T(8,128)(2,1)} %copy-done.4), custom_call_target="tpu_custom_call" | custom-call | flops 536870912 | bytes 2097152 | tf_op jit(solution)/shard_map/pallas_call | solution.py:295
  145.7 5.0 %shard_map.87 = bf16[4,512,256]{2,1,0:T(8,128)(2,1)} custom-call(s32[10]{0:T(128)} %stack.46.at_ref, bf16[8,512,256]{2,1,0:T(8,128)(2,1)} %get-tuple-element.21.mine_ref, bf16[8,512,256]{2,1,0:T(8,128)(2,1)} %copy-done, bf16[256,256]{1,0:T(8,128)(2,1)} %copy-done.2, bf16[256,256]{1,0:T(8,128)(2,1)} %copy-done.4), custom_call_target="tpu_custom_call" | custom-call | flops 1073741824 | bytes 4194304 | tf_op jit(solution)/shard_map/pallas_call | solution.py:295
  150.7 3.6 %collective-permute-done.18 = bf16[2,512,256]{2,1,0:T(8,128)(2,1)S(1)} collective-permute-done((bf16[2,512,256]{2,1,0:T(8,128)(2,1)}, bf16[2,512,256]{2,1,0:T(8,128)(2,1)S(1)}, u32[]{:S(2)}, u32[]{:S(2)}) %collective-permute-start.18) | collective-permute-done | bytes 524320 | tf_op jit(solution)/shard_map/ppermute | solution.py:238
  154.4 6.5 %collective-permute-done.16 = bf16[2,512,256]{2,1,0:T(8,128)(2,1)S(1)} collective-permute-done((bf16[2,512,256]{2,1,0:T(8,128)(2,1)}, bf16[2,512,256]{2,1,0:T(8,128)(2,1)S(1)}, u32[]{:S(2)}, u32[]{:S(2)}) %collective-permute-start.16) | collective-permute-done | bytes 524320 | tf_op jit(solution)/shard_map/ppermute | solution.py:238
  162.1 3.2 %collective-permute-start.19 = (bf16[512,256]{1,0:T(8,128)(2,1)S(1)}, bf16[512,256]{1,0:T(8,128)(2,1)S(1)}, u32[]{:S(2)}, u32[]{:S(2)}) collective-permute-start(bf16[512,256]{1,0:T(8,128)(2,1)S(1)} %get-tuple-element.33), channel_id=1, source_target_pairs={{0,192},{16,208},{32,224},{48,240},{64,0},{80,16},{96,32},{112,48}... | collective-permute-start | bytes 786440 | tf_op jit(solution)/shard_map/ppermute | solution.py:238
  165.3 5.5 %fusion = bf16[1,256,8192]{2,1,0:T(8,128)(2,1)} fusion(bf16[256,256]{1,0:T(8,128)(2,1)S(1)} %copy-done.3, bf16[8192,256]{1,0:T(8,128)(2,1)} %all-gather.2.cloned.1.call-done), kind=kOutput, calls=%fused_computation.1 | convolution fusion | flops 1075838976 | bytes 8519680 | tf_op jit(solution)/shard_map/dot_general | solution.py:362
  171.1 3.8 %collective-permute-start.22 = (bf16[256,256]{1,0:T(8,128)(2,1)S(1)}, bf16[256,256]{1,0:T(8,128)(2,1)S(1)}, u32[]{:S(2)}, u32[]{:S(2)}) collective-permute-start(bf16[256,256]{1,0:T(8,128)(2,1)S(1)} %bitcast.81), channel_id=1, source_target_pairs={{0,3},{1,0},{2,1},{3,2},{4,7},{5,4},{6,5},{7,6},{8,11},{9,8},{10,9... | collective-permute-start | bytes 393224 | tf_op jit(solution)/shard_map/ppermute | solution.py:225
  175.8 3.3 %collective-permute-done.22 = bf16[256,256]{1,0:T(8,128)(2,1)S(1)} collective-permute-done((bf16[256,256]{1,0:T(8,128)(2,1)S(1)}, bf16[256,256]{1,0:T(8,128)(2,1)S(1)}, u32[]{:S(2)}, u32[]{:S(2)}) %collective-permute-start.22) | collective-permute-done | bytes 131104 | tf_op jit(solution)/shard_map/ppermute | solution.py:225
  179.1 2.4 %collective-permute-done.21 = bf16[256,256]{1,0:T(8,128)(2,1)S(1)} collective-permute-done((bf16[256,256]{1,0:T(8,128)(2,1)S(1)}, bf16[256,256]{1,0:T(8,128)(2,1)S(1)}, u32[]{:S(2)}, u32[]{:S(2)}) %collective-permute-start.21) | collective-permute-done | bytes 131104 | tf_op jit(solution)/shard_map/ppermute | solution.py:225
  182.5 4.4 %collective-permute-start.25 = (bf16[2,32,256]{2,1,0:T(8,128)(2,1)S(1)}, bf16[2,32,256]{2,1,0:T(8,128)(2,1)S(1)}, u32[]{:S(2)}, u32[]{:S(2)}) collective-permute-start(bf16[2,32,256]{2,1,0:T(8,128)(2,1)S(1)} %get-tuple-element.44), channel_id=1, source_target_pairs={{0,12},{1,13},{2,14},{3,15},{4,0},{5,1},{6,2},{7,3},{8,4},{9,5},{1... | collective-permute-start | bytes 98312 | tf_op jit(solution)/shard_map/ppermute | solution.py:232
  188.5 3.2 %collective-permute-done.24 = bf16[2,32,256]{2,1,0:T(8,128)(2,1)S(1)} collective-permute-done((bf16[2,32,256]{2,1,0:T(8,128)(2,1)S(1)}, bf16[2,32,256]{2,1,0:T(8,128)(2,1)S(1)}, u32[]{:S(2)}, u32[]{:S(2)}) %collective-permute-start.24) | collective-permute-done | bytes 32800 | tf_op jit(solution)/shard_map/ppermute | solution.py:232
  193.1 5.9 %collective-permute-start.26 = (f32[32,256]{1,0:T(8,128)S(1)}, f32[32,256]{1,0:T(8,128)S(1)}, u32[]{:S(2)}, u32[]{:S(2)}) collective-permute-start(f32[32,256]{1,0:T(8,128)S(1)} %slice_bitcast_fusion.2), channel_id=1, source_target_pairs={{0,32},{16,48},{32,0},{48,16},{64,96},{80,112},{96,64},{112,80},{1... | collective-permute-start | bytes 98312 | tf_op jit(solution)/shard_map/ppermute | solution.py:377
  199.0 2.0 collective-permute-done.26
  (75 shorter events, 21.9 us)
Async XLA Ops:
  7.2 158.2 %all-gather.2.cloned.1.call-start = ((), (), s32[]{:S(2)}) async-start(), calls=%async_computation | async-start | bytes 4456448 | tf_op jit(solution)/shard_map/all_gather | solution.py:334
  11.9 8.6 %collective-permute-start = (bf16[272,256]{1,0:T(8,128)(2,1)S(1)}, bf16[272,256]{1,0:T(8,128)(2,1)S(1)}, u32[]{:S(2)}, u32[]{:S(2)}) collective-permute-start(bf16[272,256]{1,0:T(8,128)(2,1)S(1)} %concatenate.7), channel_id=1, source_target_pairs={{0,4},{1,5},{2,6},{3,7},{4,8},{5,9},{6,10},{7,11},{8,12},{9,13},{1... | collective-permute-start | bytes 417800 | tf_op jit(solution)/shard_map/ppermute | solution.py:232
  12.2 12.4 %collective-permute-start.1 = (bf16[272,256]{1,0:T(8,128)(2,1)S(1)}, bf16[272,256]{1,0:T(8,128)(2,1)S(1)}, u32[]{:S(2)}, u32[]{:S(2)}) collective-permute-start(bf16[272,256]{1,0:T(8,128)(2,1)S(1)} %concatenate.7), channel_id=1, source_target_pairs={{0,8},{1,9},{2,10},{3,11},{4,12},{5,13},{6,14},{7,15},{8,0},{9,1},... | collective-permute-start | bytes 417800 | tf_op jit(solution)/shard_map/ppermute | solution.py:232
  15.5 9.2 %collective-permute-start.2 = (bf16[272,256]{1,0:T(8,128)(2,1)S(1)}, bf16[272,256]{1,0:T(8,128)(2,1)S(1)}, u32[]{:S(2)}, u32[]{:S(2)}) collective-permute-start(bf16[272,256]{1,0:T(8,128)(2,1)S(1)} %concatenate.7), channel_id=1, source_target_pairs={{0,12},{1,13},{2,14},{3,15},{4,0},{5,1},{6,2},{7,3},{8,4},{9,5},{1... | collective-permute-start | bytes 417800 | tf_op jit(solution)/shard_map/ppermute | solution.py:232
  24.7 26.1 %copy-start.7 = (bf16[1088,256]{1,0:T(8,128)(2,1)}, bf16[1088,256]{1,0:T(8,128)(2,1)S(1)}, u32[]{:S(2)}) copy-start(bf16[1088,256]{1,0:T(8,128)(2,1)S(1)} %constant_dynamic-update-slice_fusion.near_ref) | copy-start | bytes 1671172
  24.7 15.7 %collective-permute-start.3 = (bf16[1088,256]{1,0:T(8,128)(2,1)S(1)}, bf16[1088,256]{1,0:T(8,128)(2,1)S(1)}, u32[]{:S(2)}, u32[]{:S(2)}) collective-permute-start(bf16[1088,256]{1,0:T(8,128)(2,1)S(1)} %constant_dynamic-update-slice_fusion.near_ref), channel_id=1, source_target_pairs={{0,1},{1,2},{2,3},{3,0},{4,5},{5,6},{6,7},{7,4},{8,9},{9,10},{10,1... | collective-permute-start | bytes 1671176 | tf_op jit(solution)/shard_map/ppermute | solution.py:225
  26.3 14.6 %collective-permute-start.4 = (bf16[1088,256]{1,0:T(8,128)(2,1)S(1)}, bf16[1088,256]{1,0:T(8,128)(2,1)S(1)}, u32[]{:S(2)}, u32[]{:S(2)}) collective-permute-start(bf16[1088,256]{1,0:T(8,128)(2,1)S(1)} %constant_dynamic-update-slice_fusion.near_ref), channel_id=1, source_target_pairs={{0,3},{1,0},{2,1},{3,2},{4,7},{5,4},{6,5},{7,6},{8,11},{9,8},{10,9... | collective-permute-start | bytes 1671176 | tf_op jit(solution)/shard_map/ppermute | solution.py:225
  40.4 10.3 %copy-start.5 = (bf16[1088,256]{1,0:T(8,128)(2,1)}, bf16[1088,256]{1,0:T(8,128)(2,1)S(1)}, u32[]{:S(2)}) copy-start(bf16[1088,256]{1,0:T(8,128)(2,1)S(1)} %collective-permute-done.3.left_ref) | copy-start | bytes 1671172
  40.5 10.3 %collective-permute-start.5 = (bf16[544,256]{1,0:T(8,128)(2,1)S(1)}, bf16[544,256]{1,0:T(8,128)(2,1)S(1)}, u32[]{:S(2)}, u32[]{:S(2)}) collective-permute-start(bf16[544,256]{1,0:T(8,128)(2,1)S(1)} %slice.128), channel_id=1, source_target_pairs={{0,1},{1,2},{2,3},{3,0},{4,5},{5,6},{6,7},{7,4},{8,9},{9,10},{10,1... | collective-permute-start | bytes 835592 | tf_op jit(solution)/shard_map/ppermute | solution.py:225
  40.8 10.0 %copy-start.6 = (bf16[1088,256]{1,0:T(8,128)(2,1)}, bf16[1088,256]{1,0:T(8,128)(2,1)S(1)}, u32[]{:S(2)}) copy-start(bf16[1088,256]{1,0:T(8,128)(2,1)S(1)} %collective-permute-done.4.right_ref) | copy-start | bytes 1671172
  40.8 10.0 %collective-permute-start.6 = (bf16[544,256]{1,0:T(8,128)(2,1)S(1)}, bf16[544,256]{1,0:T(8,128)(2,1)S(1)}, u32[]{:S(2)}, u32[]{:S(2)}) collective-permute-start(bf16[544,256]{1,0:T(8,128)(2,1)S(1)} %slice.129), channel_id=1, source_target_pairs={{0,3},{1,0},{2,1},{3,2},{4,7},{5,4},{6,5},{7,6},{8,11},{9,8},{10,9... | collective-permute-start | bytes 835592 | tf_op jit(solution)/shard_map/ppermute | solution.py:225
  93.4 13.9 %collective-permute-start.8 = (bf16[1024,256]{1,0:T(8,128)(2,1)}, bf16[1024,256]{1,0:T(8,128)(2,1)S(1)}, u32[]{:S(2)}, u32[]{:S(2)}) collective-permute-start(bf16[1024,256]{1,0:T(8,128)(2,1)} %get-tuple-element.25), channel_id=1, source_target_pairs={{0,1},{1,2},{2,3},{3,0},{4,5},{5,6},{6,7},{7,4},{8,9},{9,10},{10,1... | collective-permute-start | bytes 1572872 | tf_op jit(solution)/shard_map/ppermute | solution.py:225
  93.5 40.9 %collective-permute-start.7 = (bf16[8,512,256]{2,1,0:T(8,128)(2,1)}, bf16[8,512,256]{2,1,0:T(8,128)(2,1)S(1)}, u32[]{:S(2)}, u32[]{:S(2)}) collective-permute-start(bf16[8,512,256]{2,1,0:T(8,128)(2,1)} %get-tuple-element.22), channel_id=1, source_target_pairs={{0,16},{16,0},{32,48},{48,32},{64,80},{80,64},{96,112},{112,96},{1... | collective-permute-start | bytes 6291464 | tf_op jit(solution)/shard_map/ppermute | solution.py:329
  93.6 15.3 %collective-permute-start.10 = (bf16[1024,256]{1,0:T(8,128)(2,1)}, bf16[1024,256]{1,0:T(8,128)(2,1)S(1)}, u32[]{:S(2)}, u32[]{:S(2)}) collective-permute-start(bf16[1024,256]{1,0:T(8,128)(2,1)} %get-tuple-element.26), channel_id=1, source_target_pairs={{0,3},{1,0},{2,1},{3,2},{4,7},{5,4},{6,5},{7,6},{8,11},{9,8},{10,9... | collective-permute-start | bytes 1572872 | tf_op jit(solution)/shard_map/ppermute | solution.py:225
  108.3 7.7 %collective-permute-start.9 = (bf16[512,256]{1,0:T(8,128)(2,1)S(1)}, bf16[512,256]{1,0:T(8,128)(2,1)S(1)}, u32[]{:S(2)}, u32[]{:S(2)}) collective-permute-start(bf16[512,256]{1,0:T(8,128)(2,1)S(1)} %add_convert_fusion.5), channel_id=1, source_target_pairs={{0,1},{1,2},{2,3},{3,0},{4,5},{5,6},{6,7},{7,4},{8,9},{9,10},{10,1... | collective-permute-start | bytes 786440 | tf_op jit(solution)/shard_map/ppermute | solution.py:225
  109.9 9.1 %collective-permute-start.12 = (bf16[512,256]{1,0:T(8,128)(2,1)S(1)}, bf16[512,256]{1,0:T(8,128)(2,1)S(1)}, u32[]{:S(2)}, u32[]{:S(2)}) collective-permute-start(bf16[512,256]{1,0:T(8,128)(2,1)S(1)} %add_convert_fusion.3), channel_id=1, source_target_pairs={{0,3},{1,0},{2,1},{3,2},{4,7},{5,4},{6,5},{7,6},{8,11},{9,8},{10,9... | collective-permute-start | bytes 786440 | tf_op jit(solution)/shard_map/ppermute | solution.py:225
  120.3 8.3 %collective-permute-start.14 = (bf16[256,256]{1,0:T(8,128)(2,1)S(1)}, bf16[256,256]{1,0:T(8,128)(2,1)S(1)}, u32[]{:S(2)}, u32[]{:S(2)}) collective-permute-start(bf16[256,256]{1,0:T(8,128)(2,1)S(1)} %get-tuple-element.42), channel_id=1, source_target_pairs={{0,4},{1,5},{2,6},{3,7},{4,8},{5,9},{6,10},{7,11},{8,12},{9,13},{1... | collective-permute-start | bytes 393224 | tf_op jit(solution)/shard_map/ppermute | solution.py:232
  123.9 9.0 %collective-permute-start.13 = (bf16[256,256]{1,0:T(8,128)(2,1)S(1)}, bf16[256,256]{1,0:T(8,128)(2,1)S(1)}, u32[]{:S(2)}, u32[]{:S(2)}) collective-permute-start(bf16[256,256]{1,0:T(8,128)(2,1)S(1)} %get-tuple-element.41), channel_id=1, source_target_pairs={{0,8},{1,9},{2,10},{3,11},{4,12},{5,13},{6,14},{7,15},{8,0},{9,1},... | collective-permute-start | bytes 393224 | tf_op jit(solution)/shard_map/ppermute | solution.py:232
  124.2 8.7 %collective-permute-start.11 = (bf16[256,256]{1,0:T(8,128)(2,1)S(1)}, bf16[256,256]{1,0:T(8,128)(2,1)S(1)}, u32[]{:S(2)}, u32[]{:S(2)}) collective-permute-start(bf16[256,256]{1,0:T(8,128)(2,1)S(1)} %slice.133), channel_id=1, source_target_pairs={{0,12},{1,13},{2,14},{3,15},{4,0},{5,1},{6,2},{7,3},{8,4},{9,5},{1... | collective-permute-start | bytes 393224 | tf_op jit(solution)/shard_map/ppermute | solution.py:232
  133.0 1.4 collective-permute-start.15
  139.6 14.8 %collective-permute-start.18 = (bf16[2,512,256]{2,1,0:T(8,128)(2,1)}, bf16[2,512,256]{2,1,0:T(8,128)(2,1)S(1)}, u32[]{:S(2)}, u32[]{:S(2)}) collective-permute-start(bf16[2,512,256]{2,1,0:T(8,128)(2,1)} %shard_map.89), channel_id=1, source_target_pairs={{0,192},{16,208},{32,224},{48,240},{64,0},{80,16},{96,32},{112,48}... | collective-permute-start | bytes 1572872 | tf_op jit(solution)/shard_map/ppermute | solution.py:238
  145.7 19.6 %copy-start.3 = (bf16[256,256]{1,0:T(8,128)(2,1)S(1)}, bf16[256,256]{1,0:T(8,128)(2,1)}, u32[]{:S(2)}) copy-start(bf16[256,256]{1,0:T(8,128)(2,1)} %copy-done.2) | copy-start | bytes 393220
  145.7 15.1 %collective-permute-start.16 = (bf16[2,512,256]{2,1,0:T(8,128)(2,1)}, bf16[2,512,256]{2,1,0:T(8,128)(2,1)S(1)}, u32[]{:S(2)}, u32[]{:S(2)}) collective-permute-start(bf16[2,512,256]{2,1,0:T(8,128)(2,1)} %shard_map.88), channel_id=1, source_target_pairs={{0,64},{16,80},{32,96},{48,112},{64,128},{80,144},{96,160},{112,17... | collective-permute-start | bytes 1572872 | tf_op jit(solution)/shard_map/ppermute | solution.py:238
  162.0 8.8 %collective-permute-start.17 = (bf16[512,256]{1,0:T(8,128)(2,1)S(1)}, bf16[512,256]{1,0:T(8,128)(2,1)S(1)}, u32[]{:S(2)}, u32[]{:S(2)}) collective-permute-start(bf16[512,256]{1,0:T(8,128)(2,1)S(1)} %get-tuple-element.34), channel_id=1, source_target_pairs={{0,64},{16,80},{32,96},{48,112},{64,128},{80,144},{96,160},{112,17... | collective-permute-start | bytes 786440 | tf_op jit(solution)/shard_map/ppermute | solution.py:238
  162.1 8.7 %collective-permute-start.19 = (bf16[512,256]{1,0:T(8,128)(2,1)S(1)}, bf16[512,256]{1,0:T(8,128)(2,1)S(1)}, u32[]{:S(2)}, u32[]{:S(2)}) collective-permute-start(bf16[512,256]{1,0:T(8,128)(2,1)S(1)} %get-tuple-element.33), channel_id=1, source_target_pairs={{0,192},{16,208},{32,224},{48,240},{64,0},{80,16},{96,32},{112,48}... | collective-permute-start | bytes 786440 | tf_op jit(solution)/shard_map/ppermute | solution.py:238
  171.1 8.0 %collective-permute-start.22 = (bf16[256,256]{1,0:T(8,128)(2,1)S(1)}, bf16[256,256]{1,0:T(8,128)(2,1)S(1)}, u32[]{:S(2)}, u32[]{:S(2)}) collective-permute-start(bf16[256,256]{1,0:T(8,128)(2,1)S(1)} %bitcast.81), channel_id=1, source_target_pairs={{0,3},{1,0},{2,1},{3,2},{4,7},{5,4},{6,5},{7,6},{8,11},{9,8},{10,9... | collective-permute-start | bytes 393224 | tf_op jit(solution)/shard_map/ppermute | solution.py:225
  174.9 6.6 %collective-permute-start.21 = (bf16[256,256]{1,0:T(8,128)(2,1)S(1)}, bf16[256,256]{1,0:T(8,128)(2,1)S(1)}, u32[]{:S(2)}, u32[]{:S(2)}) collective-permute-start(bf16[256,256]{1,0:T(8,128)(2,1)S(1)} %bitcast.80), channel_id=1, source_target_pairs={{0,2},{1,3},{2,0},{3,1},{4,6},{5,7},{6,4},{7,5},{8,10},{9,11},{10,... | collective-permute-start | bytes 393224 | tf_op jit(solution)/shard_map/ppermute | solution.py:225
  174.9 7.6 %collective-permute-start.20 = (bf16[256,256]{1,0:T(8,128)(2,1)S(1)}, bf16[256,256]{1,0:T(8,128)(2,1)S(1)}, u32[]{:S(2)}, u32[]{:S(2)}) collective-permute-start(bf16[256,256]{1,0:T(8,128)(2,1)S(1)} %bitcast.79), channel_id=1, source_target_pairs={{0,1},{1,2},{2,3},{3,0},{4,5},{5,6},{6,7},{7,4},{8,9},{9,10},{10,1... | collective-permute-start | bytes 393224 | tf_op jit(solution)/shard_map/ppermute | solution.py:225
  182.5 6.0 %collective-permute-start.25 = (bf16[2,32,256]{2,1,0:T(8,128)(2,1)S(1)}, bf16[2,32,256]{2,1,0:T(8,128)(2,1)S(1)}, u32[]{:S(2)}, u32[]{:S(2)}) collective-permute-start(bf16[2,32,256]{2,1,0:T(8,128)(2,1)S(1)} %get-tuple-element.44), channel_id=1, source_target_pairs={{0,12},{1,13},{2,14},{3,15},{4,0},{5,1},{6,2},{7,3},{8,4},{9,5},{1... | collective-permute-start | bytes 98312 | tf_op jit(solution)/shard_map/ppermute | solution.py:232
  186.9 4.8 %collective-permute-start.24 = (bf16[2,32,256]{2,1,0:T(8,128)(2,1)S(1)}, bf16[2,32,256]{2,1,0:T(8,128)(2,1)S(1)}, u32[]{:S(2)}, u32[]{:S(2)}) collective-permute-start(bf16[2,32,256]{2,1,0:T(8,128)(2,1)S(1)} %get-tuple-element.45), channel_id=1, source_target_pairs={{0,8},{1,9},{2,10},{3,11},{4,12},{5,13},{6,14},{7,15},{8,0},{9,1},... | collective-permute-start | bytes 98312 | tf_op jit(solution)/shard_map/ppermute | solution.py:232
  187.4 5.7 %collective-permute-start.23 = (bf16[2,32,256]{2,1,0:T(8,128)(2,1)S(1)}, bf16[2,32,256]{2,1,0:T(8,128)(2,1)S(1)}, u32[]{:S(2)}, u32[]{:S(2)}) collective-permute-start(bf16[2,32,256]{2,1,0:T(8,128)(2,1)S(1)} %get-tuple-element.43), channel_id=1, source_target_pairs={{0,4},{1,5},{2,6},{3,7},{4,8},{5,9},{6,10},{7,11},{8,12},{9,13},{1... | collective-permute-start | bytes 98312 | tf_op jit(solution)/shard_map/ppermute | solution.py:232
  193.1 7.9 %collective-permute-start.26 = (f32[32,256]{1,0:T(8,128)S(1)}, f32[32,256]{1,0:T(8,128)S(1)}, u32[]{:S(2)}, u32[]{:S(2)}) collective-permute-start(f32[32,256]{1,0:T(8,128)S(1)} %slice_bitcast_fusion.2), channel_id=1, source_target_pairs={{0,32},{16,48},{32,0},{48,16},{64,96},{80,112},{96,64},{112,80},{1... | collective-permute-start | bytes 98312 | tf_op jit(solution)/shard_map/ppermute | solution.py:377
  (6 other events, 13.7 us)
Sparse Core Ops, SparseCore 0:
  16.6 81.1 all-gather.1

commit v2 on v1

v2 whole, which is shorter than its diff:
```python
import functools
import math

import jax
import jax.numpy as jnp
from jax import lax
from jax.experimental import pallas as pl
from jax.experimental.pallas import tpu as pltpu
from jax.sharding import PartitionSpec as P

BLK = 128
TAG = 16
MASKED = -1e30
LONG = 4


def mm(a, b):
    return lax.dot_general(a, b, (((1,), (0,)), ((), ())), preferred_element_type=jnp.float32)


def mm_tn(a, b):
    return lax.dot_general(a, b, (((0,), (0,)), ((), ())), preferred_element_type=jnp.float32)


def mm_nt(a, b):
    return lax.dot_general(a, b, (((1,), (1,)), ((), ())), preferred_element_type=jnp.float32)


def attn_kernel(
    G,
    KC,
    blocks,
    scale,
    q_ref,
    do_ref,
    near_ref,
    left_ref,
    right_ref,
    far_a_ref,
    far_b_ref,
    dq_ref,
    keep_ref,
    plus_ref,
    minus_ref,
    plus_late_ref,
    minus_late_ref,
    kvs,
    s_scr,
    dp_scr,
    acc,
    dq_acc,
    qr,
    dor,
    p_even,
    d_even,
    p_odd,
    d_odd,
    first_ref,
):
    R = G * BLK
    c = scale * math.log2(math.e)
    side = pl.program_id(0)
    grp = pl.program_id(1)
    toks = 2 * BLK
    owners = blocks // 2

    @pl.when((side == 0) & (grp == 0))
    def _():
        acc[...] = jnp.zeros_like(acc)
        owner = 0
        for piece in (near_ref, left_ref, right_ref, far_a_ref, far_b_ref):
            for i in range(piece.shape[0] // (toks + TAG)):
                base = i * (toks + TAG)
                mark = piece[base + toks : base + toks + TAG, :BLK].astype(jnp.float32)
                first = jnp.max(mark).astype(jnp.int32)
                first_ref[owner] = first
                for half, place in ((0, first), (1, blocks - 1 - first)):
                    dst = pl.ds(pl.multiple_of(place * BLK, BLK), BLK)
                    kvs[dst, :] = piece[base + half * BLK : base + (half + 1) * BLK, :]
                owner += 1

    for h in range(G):
        cols = slice(h * BLK, (h + 1) * BLK)
        qr[cols, :] = q_ref[:, cols]
        dor[cols, :] = do_ref[:, cols]
    dq_acc[...] = jnp.zeros_like(dq_acc)
    qb = jnp.where(side == 0, first_ref[0], blocks - 1 - first_ref[0])
    nk = (qb + KC // BLK) // (KC // BLK)

    def scores(start, size, state, masked):
        m, l, d = state
        rows = pl.ds(pl.multiple_of(start, KC), size)
        s = mm_nt(kvs[rows, :BLK], qr[...])
        dp = mm_nt(kvs[rows, BLK:], dor[...])
        if masked:
            kpos = start + lax.broadcasted_iota(jnp.int32, (size, R), 0)
            qpos = qb * BLK + (lax.broadcasted_iota(jnp.int32, (size, R), 1) & (BLK - 1))
            s = jnp.where(kpos <= qpos, s, MASKED)
        s_scr[rows, :] = s
        dp_scr[rows, :] = dp
        s3 = s.reshape(size // 8, 8, R)
        new = jnp.maximum(m, jnp.max(s3, axis=0))
        p = jnp.exp2((s3 - new[None]) * c)
        f = jnp.exp2((m - new) * c)
        l = l * f + jnp.sum(p, axis=0)
        d = d * f + jnp.sum(p * dp.reshape(size // 8, 8, R), axis=0)
        return new, l, d

    state = (
        jnp.full((8, R), MASKED, jnp.float32),
        jnp.zeros((8, R), jnp.float32),
        jnp.zeros((8, R), jnp.float32),
    )
    runs = (nk - 1) // LONG
    state = lax.fori_loop(
        0, runs, lambda i, state: scores(i * LONG * KC, LONG * KC, state, False), state
    )
    state = lax.fori_loop(
        runs * LONG, nk - 1, lambda i, state: scores(i * KC, KC, state, False), state
    )
    m, l, d = scores((nk - 1) * KC, KC, state, True)
    top = jnp.max(m, axis=0, keepdims=True)
    f = jnp.exp2((m - top) * c)
    total = jnp.sum(l * f, axis=0, keepdims=True)
    dvec = jnp.sum(d * f, axis=0, keepdims=True) / total
    lse = top * c + jnp.log2(total)

    def weigh(start, size, p_buf, d_buf):
        rows = pl.ds(pl.multiple_of(start, KC), size)
        p = jnp.exp2(s_scr[rows, :] * c - lse)
        d_buf[:size, :] = (p * (dp_scr[rows, :] - dvec)).astype(jnp.bfloat16)
        p_buf[:size, :] = p.astype(jnp.bfloat16)

    def spend(start, size, p_buf, d_buf):
        rows = pl.ds(pl.multiple_of(start, KC), size)
        dq_acc[...] += mm_tn(d_buf[:size, :], kvs[rows, :BLK])
        acc[rows, :BLK] += mm(d_buf[:size, :], qr[...])
        acc[rows, BLK:] += mm(p_buf[:size, :], dor[...])

    run = p_even.shape[0]
    pairs = nk // (2 * run // KC)

    @pl.when(pairs > 0)
    def _():
        weigh(0, run, p_even, d_even)

    def pair(i, _):
        start = i * 2 * run
        weigh(start + run, run, p_odd, d_odd)
        spend(start, run, p_even, d_even)
        weigh(jnp.minimum(start + 2 * run, blocks * BLK - run), run, p_even, d_even)
        spend(start + run, run, p_odd, d_odd)
        return 0

    def single(i, _):
        weigh(i * KC, KC, p_even, d_even)
        spend(i * KC, KC, p_even, d_even)
        return 0

    lax.fori_loop(0, pairs, pair, 0)
    lax.fori_loop(pairs * (2 * run // KC), nk, single, 0)

    for h in range(G):
        cols = slice(h * BLK, (h + 1) * BLK)
        dq_ref[:, cols] = (dq_acc[cols, :] * scale).astype(jnp.bfloat16)

    @pl.when((side == pl.num_programs(0) - 1) & (grp == pl.num_programs(1) - 1))
    def _():
        span = owners // NX
        cut = span // 2
        for owner in range(owners):
            dx, dz = owner // span, owner % span
            late = dz >= cut
            if dx == 0:
                out, row = keep_ref, dz
            elif dx == 1:
                out, row = (minus_late_ref, dz - cut) if late else (minus_ref, dz)
            elif dx == 2:
                out, row = (plus_ref, dz) if late else (plus_late_ref, dz)
            else:
                out, row = (minus_ref, dz) if late else (plus_ref, dz)
            first = first_ref[owner]
            for half, place in ((0, first), (1, blocks - 1 - first)):
                src = pl.ds(pl.multiple_of(place * BLK, BLK), BLK)
                dst = slice(row * toks + half * BLK, row * toks + (half + 1) * BLK)
                out[dst, :BLK] = (acc[src, :BLK] * scale).astype(jnp.bfloat16)
                out[dst, BLK:] = acc[src, BLK:].astype(jnp.bfloat16)


def attention(q, do, pieces, seq, G=8, KC=256):
    toks, width = q.shape
    heads = width // BLK
    R = G * BLK
    part = pl.BlockSpec((BLK, R), lambda s, g: (s, g))
    quarter = seq // NX

    def whole(rows):
        return pl.BlockSpec((rows, 2 * BLK), lambda s, g: (0, 0), pipeline_mode=pl.Buffered(1))

    out_rows = (quarter, quarter, quarter, quarter // 2, quarter // 2)
    return pl.pallas_call(
        functools.partial(attn_kernel, G, KC, seq // BLK, 1.0 / math.sqrt(BLK)),
        grid=(2, heads // G),
        in_specs=[part, part, *(whole(piece.shape[0]) for piece in pieces)],
        out_specs=[part, *(whole(rows) for rows in out_rows)],
        scratch_shapes=[
            pltpu.VMEM((seq, 2 * BLK), jnp.bfloat16),
            pltpu.VMEM((seq, R), jnp.float32),
            pltpu.VMEM((seq, R), jnp.float32),
            pltpu.VMEM((seq, 2 * BLK), jnp.float32),
            pltpu.VMEM((R, BLK), jnp.float32),
            pltpu.VMEM((R, BLK), jnp.bfloat16),
            pltpu.VMEM((R, BLK), jnp.bfloat16),
            *(pltpu.VMEM((LONG // 2 * KC, R), jnp.bfloat16) for _ in range(4)),
            pltpu.SMEM((seq // BLK // 2,), jnp.int32),
        ],
        out_shape=[
            jax.ShapeDtypeStruct((toks, width), jnp.bfloat16),
            *(jax.ShapeDtypeStruct((rows, 2 * BLK), jnp.bfloat16) for rows in out_rows),
        ],
        compiler_params=pltpu.CompilerParams(
            dimension_semantics=("arbitrary", "arbitrary"), vmem_limit_bytes=60 * 2**20
        ),
        cost_estimate=pl.CostEstimate(
            flops=40 * 10**9, bytes_accessed=8 * 2**20, transcendentals=2 * 10**7
        ),
    )(q, do, *pieces)


NZ, NX = 4, 4
NY, NH, NC = 4, 2, 2
CORE_PAIRS = [(i, i ^ 1) for i in range(NY * NH * NC)]


def along_x(array, step):
    pairs = [
        (z * NX + x, z * NX + (x + step) % NX) for z in range(NZ) for x in range(NX)
    ]
    return lax.ppermute(array, "ctx", pairs)


def along_z(array, step):
    pairs = [
        (z * NX + x, (z + step) % NZ * NX + x) for z in range(NZ) for x in range(NX)
    ]
    return lax.ppermute(array, "ctx", pairs)


def swap_x(array, bits):
    pairs = [(i, i ^ bits) for i in range(NZ * NX)]
    return lax.ppermute(array, "ctx", pairs)


def swap_z(array, bits):
    high, low_bits = bits // NZ, bits % NZ
    size = NZ * NX
    pairs = [
        (i * size + j, (i ^ high * NC) * size + (j ^ low_bits * NX))
        for i in range(NY * NH * NC)
        for j in range(size)
    ]
    return lax.ppermute(array, ("dp", "ctx"), pairs)


X_SWAPS = (1, 3)
Z_SWAPS = (1, 3, 7)


def swap_order(swaps):
    order = [0]
    for bits in reversed(swaps):
        order += [place ^ bits for place in order]
    return order


def along_y(array, step):
    rest = NH * NC
    pairs = [(i, (i + step * rest) % (NY * rest)) for i in range(NY * rest)]
    return lax.ppermute(array, "dp", pairs)


def tag_kernel(positions_ref, kv_ref, out_ref):
    toks = kv_ref.shape[0]
    out_ref[:toks, :] = kv_ref[...]
    first = (positions_ref[0] // BLK).astype(jnp.float32)
    out_ref[toks:, :] = jnp.full((TAG, kv_ref.shape[1]), first).astype(out_ref.dtype)


def tagged_tokens(positions, kv):
    toks, width = kv.shape
    return pl.pallas_call(
        tag_kernel,
        in_specs=[
            pl.BlockSpec(memory_space=pltpu.SMEM),
            pl.BlockSpec(memory_space=pltpu.VMEM),
        ],
        out_specs=pl.BlockSpec(memory_space=pltpu.VMEM),
        out_shape=jax.ShapeDtypeStruct((toks + TAG, width), kv.dtype),
    )(positions, kv)


def cut_kernel(at_ref, a_ref, out_ref):
    out_ref[...] = a_ref[...].T


def cut_features(features, at, start, count):
    toks, model = features.shape
    piece = model // (NY * NH)
    gs = pltpu.PrefetchScalarGridSpec(
        num_scalar_prefetch=1,
        grid=(count,),
        in_specs=[pl.BlockSpec((toks, piece), lambda i, at: (0, at[start + i]))],
        out_specs=pl.BlockSpec((piece, toks), lambda i, at: (i, 0)),
    )
    return pl.pallas_call(
        cut_kernel,
        grid_spec=gs,
        out_shape=jax.ShapeDtypeStruct((count * piece, toks), features.dtype),
        cost_estimate=pl.CostEstimate(
            flops=0, bytes_accessed=2**20 * count, transcendentals=0
        ),
    )(at, features)


def project_kernel(factor, at_ref, a_ref, b_ref, c_ref, d0_ref, d1_ref, g0, g1, g2, g3, out_ref):
    h = pl.program_id(0)
    far = jnp.where(h == 0, d0_ref[...], d1_ref[...])
    total = mm(a_ref[...], g0[...]) + mm(b_ref[...], g1[...])
    total = total + mm(c_ref[...], g2[...]) + mm(far, g3[...])
    total = (total * factor).astype(out_ref.dtype)
    rows = total.shape[0] // (NZ * NX)
    x_order, z_order = swap_order(X_SWAPS), swap_order(Z_SWAPS)
    x_rank = [0] * len(x_order)
    for rank, place in enumerate(x_order):
        x_rank[place] = rank
    z_rank = [0] * len(z_order)
    for rank, place in enumerate(z_order):
        z_rank[place] = rank

    def ranked(ranks, place):
        found = jnp.int32(0)
        for i, rank in enumerate(ranks):
            found = jnp.where(place == i, rank, found)
        return found

    x_to = [ranked(x_rank, x ^ at_ref[1]) for x in range(NX)]
    for z in range(NZ):
        z_to = ranked(z_rank, (h * NZ + z) ^ at_ref[0])
        for x in range(NX):
            src = (z * NX + x) * rows
            to = pl.multiple_of((x_to[x] * NH * NZ + z_to) * rows, rows)
            out_ref[pl.ds(to, rows), :] = total[src : src + rows, :]


def project(home, left, right, far_a, far_b, grads, at, which, factor):
    toks, width = grads[0].shape
    piece = home.shape[0] // (NH * NC)
    full = pl.BlockSpec((piece, toks), lambda i, at: (i * NC + at[2 + which], 0))
    half = pl.BlockSpec((piece, toks), lambda i, at: (at[2 + which], 0))
    grad = pl.BlockSpec((toks, width), lambda i, at: (0, 0))
    gs = pltpu.PrefetchScalarGridSpec(
        num_scalar_prefetch=1,
        grid=(NH,),
        in_specs=[full, full, full, half, half] + [grad] * 4,
        out_specs=pl.BlockSpec((NH * piece, width), lambda i, at: (0, 0)),
    )
    return pl.pallas_call(
        functools.partial(project_kernel, factor),
        grid_spec=gs,
        out_shape=jax.ShapeDtypeStruct((NH * piece, width), jnp.bfloat16),
        cost_estimate=pl.CostEstimate(
            flops=2**30, bytes_accessed=3 * 2**20, transcendentals=0
        ),
    )(at, home, left, right, far_a, far_b, *grads)


def total_of(*parts):
    return sum(part.astype(jnp.float32) for part in parts)


def project_back(grads, weight):
    return lax.dot_general(
        grads, weight, (((1,), (1,)), ((), ())), preferred_element_type=jnp.float32
    ).astype(jnp.bfloat16)[None]


def body(layer_input, kv_weight, kv_stored, queries, grad_out, positions):
    low = jnp.bfloat16
    tok_rows = queries.shape[1]
    width = kv_weight.shape[1]
    ctx_size = lax.axis_size("ctx")
    data_size = lax.axis_size("dp")
    seq_rows = tok_rows * ctx_size
    data_at, ctx_at = lax.axis_index("dp"), lax.axis_index("ctx")
    y_at, far_at, core_at = data_at // (NH * NC), data_at // NC % NH, data_at % NC
    z_at, x_at = ctx_at // NX, ctx_at % NX

    tagged = tagged_tokens(positions, kv_stored[0])
    steps = ((1, 0), (1, 1), (2, 0), (3, 0), (3, 1), (2, 1), (0, 0), (0, 1))
    table = [(y_at + dy) % NY * NH + h for dy, h in steps]
    at = jnp.stack([far_at * NZ + z_at, x_at, 1 - core_at, core_at, *table]).astype(jnp.int32)
    plus = cut_features(layer_input[0], at, 4, 3)
    minus = cut_features(layer_input[0], at, 7, 3)
    home = cut_features(layer_input[0], at, 10, 2)

    column = [along_z(tagged, step) for step in range(1, NZ)]
    *column, plus = lax.optimization_barrier((*column, plus))
    near = jnp.concatenate([tagged, *column], axis=0)
    half = near.shape[0] // 2
    left, right = along_x(near, 1), along_x(near, -1)
    left, right, minus, home = lax.optimization_barrier((left, right, minus, home))
    far_a, far_b = along_x(left[:half], 1), along_x(right[half:], -1)

    query, plus, minus = lax.optimization_barrier((queries[0], plus, minus))
    from_left, from_right = along_y(plus, 1), along_y(minus, -1)

    query_grad, *sums = attention(
        query, grad_out[0], (near, left, right, far_a, far_b), seq_rows
    )
    from_left, from_right, *sums = lax.optimization_barrier((from_left, from_right, *sums))
    keep, plus, minus, plus_late, minus_late = sums
    full = home.shape[0]
    weight = lax.all_gather(kv_weight, "dp", axis=0, tiled=True)

    cut = plus_late.shape[0]
    feats_left, feats_right = from_left, from_right
    from_left, from_right = along_x(plus, 1), along_x(minus, -1)
    from_left, from_right, feats_a, feats_b = lax.optimization_barrier(
        (from_left, from_right, feats_left[full:], feats_right[full:])
    )
    feats_a, feats_b = along_y(feats_a, 1), along_y(feats_b, -1)
    plus_late = total_of(plus_late, from_left[:cut]).astype(low)
    minus_late = total_of(minus_late, from_right[cut:]).astype(low)
    late_left, late_right = along_x(plus_late, 1), along_x(minus_late, -1)
    late_left, late_right, feats_a, feats_b = lax.optimization_barrier(
        (late_left, late_right, feats_a, feats_b)
    )
    early = total_of(keep[:cut], late_left, from_right[:cut]).astype(low)
    late = total_of(keep[cut:], from_left[cut:], late_right).astype(low)
    spans = [early[:tok_rows], early[tok_rows:], late[:tok_rows], late[tok_rows:]]
    spans = [spans[0], *(along_z(spans[step], -step) for step in range(1, NZ))]
    owned = total_of(*spans).astype(low)

    grads = [along_y(owned, 1), along_y(owned, -1), along_y(owned, 2)]

    def terms_for(which):
        factor = 1.0 / math.sqrt(data_size * seq_rows)
        feats = (home, feats_left, feats_right, feats_a, feats_b)
        return project(*feats, (owned, *grads), at, which, factor)

    other = lax.ppermute(terms_for(0), "dp", CORE_PAIRS)
    terms, input_grad = total_of(terms_for(1), other), None
    for swap, swaps in ((swap_x, X_SWAPS), (swap_z, Z_SWAPS)):
        for bits in swaps:
            terms = terms.astype(low)
            cut = terms.shape[0] // 2
            came = swap(terms[cut:], bits)
            if input_grad is None:
                input_grad = project_back(owned, weight)
                came, input_grad = lax.optimization_barrier((came, input_grad))
            terms = total_of(terms[:cut], came)
    weight_grad = terms

    return (query_grad[None], input_grad, weight_grad)


def solution(mesh):
    placed = (
        P("dp", "ctx", None),
        P("dp", None),
        P("dp", "ctx", None),
        P("dp", "ctx", None),
        P("dp", "ctx", None),
        P("ctx"),
    )
    return jax.shard_map(
        body,
        mesh=mesh,
        in_specs=placed,
        out_specs=(P("dp", "ctx", None), P("dp", "ctx", None), P(("dp", "ctx"), None)),
        check_vma=False,
    )
```

time: 210 us -> 184 us (0.88)
  waiting for transfers between devices: 67.4 us -> 50.4 us
  local copies, waits for them, and re-layouts: 6.64 us -> 2.33 us
  other arithmetic: 5.44 us -> 2.38 us
  between operations: 17 us -> 14.4 us
    ppermute x11 -> x8, waiting for transfers between devices: 35.5 us -> 21.8 us  [along_x(): return lax.ppermute(array, 'ctx', pairs)]
    ppermute x3 -> x6, waiting for transfers between devices: 2.56 us -> 13.4 us  [the longest x3 6.92 us: swap_z(): return lax.ppermute(array, ('dp', 'ctx'), pairs)]
    ppermute x9 -> x6, waiting for transfers between devices: 19.1 us -> 8.52 us  [along_z(): return lax.ppermute(array, 'ctx', pairs)]
    pallas_call x1 -> x4, Pallas kernels: 6.89 us -> 13.3 us  [the longest x3 11.7 us: cut_features(): pl.pallas_call(cut_kernel, grid_spec=gs, out_shape=jax.ShapeDtypeStruct((...]
    ppermute x3 -> x6, starting transfers between devices: 6.07 us -> 12.2 us  [the longest x3 8.93 us: swap_z(): return lax.ppermute(array, ('dp', 'ctx'), pairs)]
    ppermute x11 -> x8, starting transfers between devices: 18.4 us -> 13.4 us  [along_x(): return lax.ppermute(array, 'ctx', pairs)]
    ppermute x4 -> x7, starting transfers between devices: 6.31 us -> 11.3 us  [along_y(): return lax.ppermute(array, 'dp', pairs)]
    ppermute x9 -> x6, starting transfers between devices: 15.7 us -> 10.9 us  [along_z(): return lax.ppermute(array, 'ctx', pairs)]
  transfers between devices with their start and end apart: 28 -> 28, of which waited for: 19 -> 18; matrix products, arithmetic and copies ran while one was open for 6% -> 4% of each run, Pallas kernels for 29% -> 32%
where the time goes in v2:
time: 184 us; the launch traced here: 182 us
  Pallas kernels  59.3 us (32%)
  waiting for transfers between devices  50.4 us (27%)
  starting transfers between devices  47.8 us (26%)
  between operations  14.4 us (8%)
  matrix products  5.49 us (3%)
  other arithmetic  2.38 us (1%)
  local copies, waits for them, and re-layouts  2.33 us (1%)
    pallas_call x1, Pallas kernels, attention(): pl.pallas_call(functools.partial(attn_kernel, G, KC, seq // BLK, 1.0 / ma...  38.1 us
    ppermute x8, waiting for transfers between devices, along_x(): return lax.ppermute(array, 'ctx', pairs)  21.8 us
    ppermute x8, starting transfers between devices, along_x(): return lax.ppermute(array, 'ctx', pairs)  13.4 us
    pallas_call x3, Pallas kernels, cut_features(): pl.pallas_call(cut_kernel, grid_spec=gs, out_shape=jax.ShapeDtypeStruct((...  11.7 us
    ppermute x7, starting transfers between devices, along_y(): return lax.ppermute(array, 'dp', pairs)  11.3 us
    ppermute x6, starting transfers between devices, along_z(): return lax.ppermute(array, 'ctx', pairs)  10.9 us
    ppermute x3, starting transfers between devices, swap_z(): return lax.ppermute(array, ('dp', 'ctx'), pairs)  8.93 us
    ppermute x6, waiting for transfers between devices, along_z(): return lax.ppermute(array, 'ctx', pairs)  8.52 us
  transfers between devices with their start and end apart: 28, of which 18 were waited for; matrix products, arithmetic and copies ran while one was open for 4% of the time, Pallas kernels for 32%

profile of v2, /device:TPU:0, one launch (start us, length us, event | category | flops | bytes accessed | tf_op | source)
XLA Modules:
  0.0 182.1 jit_solution(9555734424471651010)
XLA Ops:
  9.0 3.3 %collective-permute-start.1 = (bf16[272,256]{1,0:T(8,128)(2,1)}, bf16[272,256]{1,0:T(8,128)(2,1)S(1)}, u32[]{:S(2)}, u32[]{:S(2)}) collective-permute-start(bf16[272,256]{1,0:T(8,128)(2,1)} %shard_map.85), channel_id=1, source_target_pairs={{0,8},{1,9},{2,10},{3,11},{4,12},{5,13},{6,14},{7,15},{8,0},{9,1},... | collective-permute-start | bytes 417800 | tf_op jit(solution)/shard_map/ppermute | solution.py:246
  14.0 4.5 %shard_map.86 = bf16[3072,256]{1,0:T(8,128)(2,1)} custom-call(s32[12]{0:T(128)} %stack.51.at_ref, bf16[256,8192]{1,0:T(8,128)(2,1)} %bitcast.21), custom_call_target="tpu_custom_call" | custom-call | bytes 3145728 | tf_op jit(solution)/shard_map/pallas_call | solution.py:315
  18.5 3.1 %collective-permute-done.1 = bf16[272,256]{1,0:T(8,128)(2,1)S(1)} collective-permute-done((bf16[272,256]{1,0:T(8,128)(2,1)}, bf16[272,256]{1,0:T(8,128)(2,1)S(1)}, u32[]{:S(2)}, u32[]{:S(2)}) %collective-permute-start.1) | collective-permute-done | bytes 139296 | tf_op jit(solution)/shard_map/ppermute | solution.py:246
  23.3 1.8 collective-permute-start.4
  25.1 4.4 %shard_map.87 = bf16[3072,256]{1,0:T(8,128)(2,1)} custom-call(s32[12]{0:T(128)} %stack.51.at_ref, bf16[256,8192]{1,0:T(8,128)(2,1)} %bitcast.22), custom_call_target="tpu_custom_call" | custom-call | bytes 3145728 | tf_op jit(solution)/shard_map/pallas_call | solution.py:315
  29.4 2.9 %shard_map.88.a_ref = bf16[2048,256]{1,0:T(8,128)(2,1)} custom-call(s32[12]{0:T(128)} %stack.51.at_ref, bf16[256,8192]{1,0:T(8,128)(2,1)} %bitcast.23), custom_call_target="tpu_custom_call" | custom-call | bytes 2097152 | tf_op jit(solution)/shard_map/pallas_call | solution.py:315
  32.3 5.1 %collective-permute-done.3.left_ref = bf16[1088,256]{1,0:T(8,128)(2,1)S(1)} collective-permute-done((bf16[1088,256]{1,0:T(8,128)(2,1)S(1)}, bf16[1088,256]{1,0:T(8,128)(2,1)S(1)}, u32[]{:S(2)}, u32[]{:S(2)}) %collective-permute-start.3) | collective-permute-done | bytes 557088 | tf_op jit(solution)/shard_map/ppermute | solution.py:239
  39.0 1.8 %collective-permute-start.6 = (bf16[544,256]{1,0:T(8,128)(2,1)S(1)}, bf16[544,256]{1,0:T(8,128)(2,1)S(1)}, u32[]{:S(2)}, u32[]{:S(2)}) collective-permute-start(bf16[544,256]{1,0:T(8,128)(2,1)S(1)} %slice.73), channel_id=1, source_target_pairs={{0,3},{1,0},{2,1},{3,2},{4,7},{5,4},{6,5},{7,6},{8,11},{9,8},{10,9... | collective-permute-start | bytes 835592 | tf_op jit(solution)/shard_map/ppermute | solution.py:239
  42.5 1.7 collective-permute-start.8
  44.1 2.3 %collective-permute-done.5.far_a_ref = bf16[544,256]{1,0:T(8,128)(2,1)S(1)} collective-permute-done((bf16[544,256]{1,0:T(8,128)(2,1)S(1)}, bf16[544,256]{1,0:T(8,128)(2,1)S(1)}, u32[]{:S(2)}, u32[]{:S(2)}) %collective-permute-start.5) | collective-permute-done | bytes 278560 | tf_op jit(solution)/shard_map/ppermute | solution.py:239
  47.2 38.1 %shard_map.89 = (bf16[256,2048]{1,0:T(8,128)(2,1)}, bf16[1024,256]{1,0:T(8,128)(2,1)}, bf16[1024,256]{1,0:T(8,128)(2,1)}, bf16[1024,256]{1,0:T(8,128)(2,1)}, bf1...) custom-call(bf16[256,2048]{1,0:T(8,128)(2,1)} %bitcast.25, bf16[256,2048]{1,0:T(8,128)(2,1)} %bitcast.26, ...), custom_call_target="tpu_custom_call" | custom-call | flops 40000000000 | bytes 8388608 | tf_op jit(solution)/shard_map/pallas_call | solution.py:201
  85.5 3.2 %collective-permute-start.10 = (bf16[1024,256]{1,0:T(8,128)(2,1)}, bf16[1024,256]{1,0:T(8,128)(2,1)S(1)}, u32[]{:S(2)}, u32[]{:S(2)}) collective-permute-start(bf16[1024,256]{1,0:T(8,128)(2,1)} %get-tuple-element.58), channel_id=1, source_target_pairs={{0,3},{1,0},{2,1},{3,2},{4,7},{5,4},{6,5},{7,6},{8,11},{9,8},{10,9... | collective-permute-start | bytes 1572872 | tf_op jit(solution)/shard_map/ppermute | solution.py:239
  88.8 10.2 %collective-permute-done.9 = bf16[1024,256]{1,0:T(8,128)(2,1)S(1)} collective-permute-done((bf16[1024,256]{1,0:T(8,128)(2,1)}, bf16[1024,256]{1,0:T(8,128)(2,1)S(1)}, u32[]{:S(2)}, u32[]{:S(2)}) %collective-permute-start.9) | collective-permute-done | bytes 524320 | tf_op jit(solution)/shard_map/ppermute | solution.py:239
  102.5 3.3 %collective-permute-start.12 = (bf16[512,256]{1,0:T(8,128)(2,1)S(1)}, bf16[512,256]{1,0:T(8,128)(2,1)S(1)}, u32[]{:S(2)}, u32[]{:S(2)}) collective-permute-start(bf16[512,256]{1,0:T(8,128)(2,1)S(1)} %add_convert_fusion.4), channel_id=1, source_target_pairs={{0,3},{1,0},{2,1},{3,2},{4,7},{5,4},{6,5},{7,6},{8,11},{9,8},{10,9... | collective-permute-start | bytes 786440 | tf_op jit(solution)/shard_map/ppermute | solution.py:239
  105.8 4.2 %collective-permute-done.11 = bf16[512,256]{1,0:T(8,128)(2,1)S(1)} collective-permute-done((bf16[512,256]{1,0:T(8,128)(2,1)S(1)}, bf16[512,256]{1,0:T(8,128)(2,1)S(1)}, u32[]{:S(2)}, u32[]{:S(2)}) %collective-permute-start.11) | collective-permute-done | bytes 262176 | tf_op jit(solution)/shard_map/ppermute | solution.py:239
  111.8 3.9 %collective-permute-start.17 = (bf16[256,256]{1,0:T(8,128)(2,1)S(1)}, bf16[256,256]{1,0:T(8,128)(2,1)S(1)}, u32[]{:S(2)}, u32[]{:S(2)}) collective-permute-start(bf16[256,256]{1,0:T(8,128)(2,1)S(1)} %get-tuple-element.74), channel_id=1, source_target_pairs={{0,4},{1,5},{2,6},{3,7},{4,8},{5,9},{6,10},{7,11},{8,12},{9,13},{1... | collective-permute-start | bytes 393224 | tf_op jit(solution)/shard_map/ppermute | solution.py:246
  115.8 2.5 %collective-permute-start.15 = (bf16[256,256]{1,0:T(8,128)(2,1)S(1)}, bf16[256,256]{1,0:T(8,128)(2,1)S(1)}, u32[]{:S(2)}, u32[]{:S(2)}) collective-permute-start(bf16[256,256]{1,0:T(8,128)(2,1)S(1)} %slice.97), channel_id=1, source_target_pairs={{0,12},{1,13},{2,14},{3,15},{4,0},{5,1},{6,2},{7,3},{8,4},{9,5},{1... | collective-permute-start | bytes 393224 | tf_op jit(solution)/shard_map/ppermute | solution.py:246
  119.5 4.1 %collective-permute-done.16 = bf16[256,256]{1,0:T(8,128)(2,1)S(1)} collective-permute-done((bf16[256,256]{1,0:T(8,128)(2,1)S(1)}, bf16[256,256]{1,0:T(8,128)(2,1)S(1)}, u32[]{:S(2)}, u32[]{:S(2)}) %collective-permute-start.16) | collective-permute-done | bytes 131104 | tf_op jit(solution)/shard_map/ppermute | solution.py:246
  125.2 1.9 %collective-permute-start.19 = (bf16[256,256]{1,0:T(8,128)(2,1)S(1)}, bf16[256,256]{1,0:T(8,128)(2,1)S(1)}, u32[]{:S(2)}, u32[]{:S(2)}) collective-permute-start(bf16[256,256]{1,0:T(8,128)(2,1)S(1)} %add_convert_fusion.7.g0), channel_id=1, source_target_pairs={{0,192},{16,208},{32,224},{48,240},{64,0},{80,16},{96,32},{112,48}... | collective-permute-start | bytes 393224 | tf_op jit(solution)/shard_map/ppermute | solution.py:279
  130.1 3.4 %collective-permute-done.20.g3 = bf16[256,256]{1,0:T(8,128)(2,1)S(1)} collective-permute-done((bf16[256,256]{1,0:T(8,128)(2,1)S(1)}, bf16[256,256]{1,0:T(8,128)(2,1)S(1)}, u32[]{:S(2)}, u32[]{:S(2)}) %collective-permute-start.20) | collective-permute-done | bytes 131104 | tf_op jit(solution)/shard_map/ppermute | solution.py:279
  134.2 4.0 %shard_map.91 = bf16[1024,256]{1,0:T(8,128)(2,1)} custom-call(s32[12]{0:T(128)} %stack.51.at_ref, bf16[2048,256]{1,0:T(8,128)(2,1)} %shard_map.88.a_ref, bf16[3072,256]{1,0:T(8,128)(2,1)} %copy-done, bf16[3072,256]{1,0:T(8,128)(2,1)} %copy-done.1, bf16[1024,256]{1,0:T(8,128)(2,1)} %copy-done.4, bf16[1024,256]{1,0:T(8,128)(2,1)} %collective-permute-done.14.d1_ref, ...), custom_call_target="tpu_custom_call" | custom-call | flops 1073741824 | bytes 3145728 | tf_op jit(solution)/shard_map/pallas_call | solution.py:367
  138.2 3.9 %shard_map.90 = bf16[1024,256]{1,0:T(8,128)(2,1)} custom-call(s32[12]{0:T(128)} %stack.51.at_ref, bf16[2048,256]{1,0:T(8,128)(2,1)} %shard_map.88.a_ref, bf16[3072,256]{1,0:T(8,128)(2,1)} %copy-done, bf16[3072,256]{1,0:T(8,128)(2,1)} %copy-done.1, bf16[1024,256]{1,0:T(8,128)(2,1)} %copy-done.4, bf16[1024,256]{1,0:T(8,128)(2,1)} %collective-permute-done.14.d1_ref, ...), custom_call_target="tpu_custom_call" | custom-call | flops 1073741824 | bytes 3145728 | tf_op jit(solution)/shard_map/pallas_call | solution.py:367
  144.0 5.5 %fusion = bf16[1,256,8192]{2,1,0:T(8,128)(2,1)} fusion(bf16[256,256]{1,0:T(8,128)(2,1)S(1)} %copy-done.3, bf16[8192,256]{1,0:T(8,128)(2,1)} %all-gather.2.cloned.1.call-done), kind=kOutput, calls=%fused_computation.1 | convolution fusion | flops 1075838976 | bytes 8519680 | tf_op jit(solution)/shard_map/dot_general | solution.py:382
  149.5 2.6 %collective-permute-done.22 = bf16[512,256]{1,0:T(8,128)(2,1)S(1)} collective-permute-done((bf16[512,256]{1,0:T(8,128)(2,1)S(1)}, bf16[512,256]{1,0:T(8,128)(2,1)S(1)}, u32[]{:S(2)}, u32[]{:S(2)}) %collective-permute-start.22) | collective-permute-done | bytes 262176 | tf_op jit(solution)/shard_map/ppermute | solution.py:251
  152.2 2.6 %collective-permute-start.23 = (bf16[256,256]{1,0:T(8,128)(2,1)S(1)}, bf16[256,256]{1,0:T(8,128)(2,1)S(1)}, u32[]{:S(2)}, u32[]{:S(2)}) collective-permute-start(bf16[256,256]{1,0:T(8,128)(2,1)S(1)} %slice.103), channel_id=1, source_target_pairs={{0,3},{1,2},{2,1},{3,0},{4,7},{5,6},{6,5},{7,4},{8,11},{9,10},{10,... | collective-permute-start | bytes 393224 | tf_op jit(solution)/shard_map/ppermute | solution.py:251
  154.8 3.9 %collective-permute-done.23 = bf16[256,256]{1,0:T(8,128)(2,1)S(1)} collective-permute-done((bf16[256,256]{1,0:T(8,128)(2,1)S(1)}, bf16[256,256]{1,0:T(8,128)(2,1)S(1)}, u32[]{:S(2)}, u32[]{:S(2)}) %collective-permute-start.23) | collective-permute-done | bytes 131104 | tf_op jit(solution)/shard_map/ppermute | solution.py:251
  158.7 2.1 %collective-permute-start.24 = (bf16[128,256]{1,0:T(8,128)(2,1)S(1)}, bf16[128,256]{1,0:T(8,128)(2,1)S(1)}, u32[]{:S(2)}, u32[]{:S(2)}) collective-permute-start(bf16[128,256]{1,0:T(8,128)(2,1)S(1)} %slice.105), channel_id=1, source_target_pairs={{0,4},{1,5},{2,6},{3,7},{4,0},{5,1},{6,2},{7,3},{8,12},{9,13},{10,... | collective-permute-start | bytes 196616 | tf_op jit(solution)/shard_map/ppermute | solution.py:262
  160.8 2.3 %collective-permute-done.24 = bf16[128,256]{1,0:T(8,128)(2,1)S(1)} collective-permute-done((bf16[128,256]{1,0:T(8,128)(2,1)S(1)}, bf16[128,256]{1,0:T(8,128)(2,1)S(1)}, u32[]{:S(2)}, u32[]{:S(2)}) %collective-permute-start.24) | collective-permute-done | bytes 65568 | tf_op jit(solution)/shard_map/ppermute | solution.py:262
  163.1 3.1 %collective-permute-start.25 = (bf16[64,256]{1,0:T(8,128)(2,1)S(1)}, bf16[64,256]{1,0:T(8,128)(2,1)S(1)}, u32[]{:S(2)}, u32[]{:S(2)}) collective-permute-start(bf16[64,256]{1,0:T(8,128)(2,1)S(1)} %slice.107), channel_id=1, source_target_pairs={{0,12},{1,13},{2,14},{3,15},{4,8},{5,9},{6,10},{7,11},{8,4},{9,5},... | collective-permute-start | bytes 98312 | tf_op jit(solution)/shard_map/ppermute | solution.py:262
  166.2 2.7 %collective-permute-done.25 = bf16[64,256]{1,0:T(8,128)(2,1)S(1)} collective-permute-done((bf16[64,256]{1,0:T(8,128)(2,1)S(1)}, bf16[64,256]{1,0:T(8,128)(2,1)S(1)}, u32[]{:S(2)}, u32[]{:S(2)}) %collective-permute-start.25) | collective-permute-done | bytes 32800 | tf_op jit(solution)/shard_map/ppermute | solution.py:262
  168.9 3.8 %collective-permute-start.26 = (bf16[32,256]{1,0:T(8,128)(2,1)S(1)}, bf16[32,256]{1,0:T(8,128)(2,1)S(1)}, u32[]{:S(2)}, u32[]{:S(2)}) collective-permute-start(bf16[32,256]{1,0:T(8,128)(2,1)S(1)} %slice.109), channel_id=1, source_target_pairs={{0,44},{1,45},{2,46},{3,47},{4,40},{5,41},{6,42},{7,43},{8,36},{9,... | collective-permute-start | bytes 49160 | tf_op jit(solution)/shard_map/ppermute | solution.py:262
  172.7 1.9 %collective-permute-done.26 = bf16[32,256]{1,0:T(8,128)(2,1)S(1)} collective-permute-done((bf16[32,256]{1,0:T(8,128)(2,1)S(1)}, bf16[32,256]{1,0:T(8,128)(2,1)S(1)}, u32[]{:S(2)}, u32[]{:S(2)}) %collective-permute-start.26) | collective-permute-done | bytes 16416 | tf_op jit(solution)/shard_map/ppermute | solution.py:262
  (90 shorter events, 23.8 us)
Async XLA Ops:
  7.2 136.8 %all-gather.2.cloned.1.call-start = ((), (), s32[]{:S(2)}) async-start(), calls=%async_computation | async-start | bytes 4456448 | tf_op jit(solution)/shard_map/all_gather | solution.py:423
  8.8 9.7 %collective-permute-start = (bf16[272,256]{1,0:T(8,128)(2,1)}, bf16[272,256]{1,0:T(8,128)(2,1)S(1)}, u32[]{:S(2)}, u32[]{:S(2)}) collective-permute-start(bf16[272,256]{1,0:T(8,128)(2,1)} %shard_map.85), channel_id=1, source_target_pairs={{0,4},{1,5},{2,6},{3,7},{4,8},{5,9},{6,10},{7,11},{8,12},{9,13},{1... | collective-permute-start | bytes 417800 | tf_op jit(solution)/shard_map/ppermute | solution.py:246
  9.0 12.7 %collective-permute-start.1 = (bf16[272,256]{1,0:T(8,128)(2,1)}, bf16[272,256]{1,0:T(8,128)(2,1)S(1)}, u32[]{:S(2)}, u32[]{:S(2)}) collective-permute-start(bf16[272,256]{1,0:T(8,128)(2,1)} %shard_map.85), channel_id=1, source_target_pairs={{0,8},{1,9},{2,10},{3,11},{4,12},{5,13},{6,14},{7,15},{8,0},{9,1},... | collective-permute-start | bytes 417800 | tf_op jit(solution)/shard_map/ppermute | solution.py:246
  12.2 9.4 %collective-permute-start.2 = (bf16[272,256]{1,0:T(8,128)(2,1)}, bf16[272,256]{1,0:T(8,128)(2,1)S(1)}, u32[]{:S(2)}, u32[]{:S(2)}) collective-permute-start(bf16[272,256]{1,0:T(8,128)(2,1)} %shard_map.85), channel_id=1, source_target_pairs={{0,12},{1,13},{2,14},{3,15},{4,0},{5,1},{6,2},{7,3},{8,4},{9,5},{1... | collective-permute-start | bytes 417800 | tf_op jit(solution)/shard_map/ppermute | solution.py:246
  21.7 15.7 %collective-permute-start.3 = (bf16[1088,256]{1,0:T(8,128)(2,1)S(1)}, bf16[1088,256]{1,0:T(8,128)(2,1)S(1)}, u32[]{:S(2)}, u32[]{:S(2)}) collective-permute-start(bf16[1088,256]{1,0:T(8,128)(2,1)S(1)} %pad_maximum_fusion.near_ref), channel_id=1, source_target_pairs={{0,1},{1,2},{2,3},{3,0},{4,5},{5,6},{6,7},{7,4},{8,9},{9,10},{10,1... | collective-permute-start | bytes 1671176 | tf_op jit(solution)/shard_map/ppermute | solution.py:239
  23.3 14.2 %collective-permute-start.4 = (bf16[1088,256]{1,0:T(8,128)(2,1)S(1)}, bf16[1088,256]{1,0:T(8,128)(2,1)S(1)}, u32[]{:S(2)}, u32[]{:S(2)}) collective-permute-start(bf16[1088,256]{1,0:T(8,128)(2,1)S(1)} %pad_maximum_fusion.near_ref), channel_id=1, source_target_pairs={{0,3},{1,0},{2,1},{3,2},{4,7},{5,4},{6,5},{7,6},{8,11},{9,8},{10,9... | collective-permute-start | bytes 1671176 | tf_op jit(solution)/shard_map/ppermute | solution.py:239
  37.5 9.0 %collective-permute-start.5 = (bf16[544,256]{1,0:T(8,128)(2,1)S(1)}, bf16[544,256]{1,0:T(8,128)(2,1)S(1)}, u32[]{:S(2)}, u32[]{:S(2)}) collective-permute-start(bf16[544,256]{1,0:T(8,128)(2,1)S(1)} %slice.72), channel_id=1, source_target_pairs={{0,1},{1,2},{2,3},{3,0},{4,5},{5,6},{6,7},{7,4},{8,9},{9,10},{10,1... | collective-permute-start | bytes 835592 | tf_op jit(solution)/shard_map/ppermute | solution.py:239
  39.0 7.4 %collective-permute-start.6 = (bf16[544,256]{1,0:T(8,128)(2,1)S(1)}, bf16[544,256]{1,0:T(8,128)(2,1)S(1)}, u32[]{:S(2)}, u32[]{:S(2)}) collective-permute-start(bf16[544,256]{1,0:T(8,128)(2,1)S(1)} %slice.73), channel_id=1, source_target_pairs={{0,3},{1,0},{2,1},{3,2},{4,7},{5,4},{6,5},{7,6},{8,11},{9,8},{10,9... | collective-permute-start | bytes 835592 | tf_op jit(solution)/shard_map/ppermute | solution.py:239
  40.9 44.5 %collective-permute-start.7 = (bf16[3072,256]{1,0:T(8,128)(2,1)}, bf16[3072,256]{1,0:T(8,128)(2,1)S(1)}, u32[]{:S(2)}, u32[]{:S(2)}) collective-permute-start(bf16[3072,256]{1,0:T(8,128)(2,1)} %shard_map.86), channel_id=1, source_target_pairs={{0,64},{16,80},{32,96},{48,112},{64,128},{80,144},{96,160},{112,17... | collective-permute-start | bytes 4718600 | tf_op jit(solution)/shard_map/ppermute | solution.py:279
  42.5 42.9 %collective-permute-start.8 = (bf16[3072,256]{1,0:T(8,128)(2,1)}, bf16[3072,256]{1,0:T(8,128)(2,1)S(1)}, u32[]{:S(2)}, u32[]{:S(2)}) collective-permute-start(bf16[3072,256]{1,0:T(8,128)(2,1)} %shard_map.87), channel_id=1, source_target_pairs={{0,192},{16,208},{32,224},{48,240},{64,0},{80,16},{96,32},{112,48}... | collective-permute-start | bytes 4718600 | tf_op jit(solution)/shard_map/ppermute | solution.py:279
  85.3 17.1 %copy-start.11 = (bf16[512,256]{1,0:T(8,128)(2,1)S(1)}, bf16[512,256]{1,0:T(8,128)(2,1)}, u32[]{:S(2)}) copy-start(bf16[512,256]{1,0:T(8,128)(2,1)} %get-tuple-element.60) | copy-start | bytes 786436
  85.3 17.1 %copy-start = (bf16[3072,256]{1,0:T(8,128)(2,1)}, bf16[3072,256]{1,0:T(8,128)(2,1)S(1)}, u32[]{:S(2)}) copy-start(bf16[3072,256]{1,0:T(8,128)(2,1)S(1)} %collective-permute-done.7.b_ref) | copy-start | bytes 4718596
  85.4 17.1 %copy-start.1 = (bf16[3072,256]{1,0:T(8,128)(2,1)}, bf16[3072,256]{1,0:T(8,128)(2,1)S(1)}, u32[]{:S(2)}) copy-start(bf16[3072,256]{1,0:T(8,128)(2,1)S(1)} %collective-permute-done.8.c_ref) | copy-start | bytes 4718596
  85.4 13.6 %collective-permute-start.9 = (bf16[1024,256]{1,0:T(8,128)(2,1)}, bf16[1024,256]{1,0:T(8,128)(2,1)S(1)}, u32[]{:S(2)}, u32[]{:S(2)}) collective-permute-start(bf16[1024,256]{1,0:T(8,128)(2,1)} %get-tuple-element.57), channel_id=1, source_target_pairs={{0,1},{1,2},{2,3},{3,0},{4,5},{5,6},{6,7},{7,4},{8,9},{9,10},{10,1... | collective-permute-start | bytes 1572872 | tf_op jit(solution)/shard_map/ppermute | solution.py:239
  85.5 13.5 %collective-permute-start.10 = (bf16[1024,256]{1,0:T(8,128)(2,1)}, bf16[1024,256]{1,0:T(8,128)(2,1)S(1)}, u32[]{:S(2)}, u32[]{:S(2)}) collective-permute-start(bf16[1024,256]{1,0:T(8,128)(2,1)} %get-tuple-element.58), channel_id=1, source_target_pairs={{0,3},{1,0},{2,1},{3,2},{4,7},{5,4},{6,5},{7,6},{8,11},{9,8},{10,9... | collective-permute-start | bytes 1572872 | tf_op jit(solution)/shard_map/ppermute | solution.py:239
  88.7 22.8 %copy-start.10 = (bf16[1024,256]{1,0:T(8,128)(2,1)S(1)}, bf16[1024,256]{1,0:T(8,128)(2,1)}, u32[]{:S(2)}) copy-start(bf16[1024,256]{1,0:T(8,128)(2,1)} %get-tuple-element.66) | copy-start | bytes 1572868
  99.0 12.5 %collective-permute-start.13 = (bf16[1024,256]{1,0:T(8,128)(2,1)S(1)}, bf16[1024,256]{1,0:T(8,128)(2,1)S(1)}, u32[]{:S(2)}, u32[]{:S(2)}) collective-permute-start(bf16[1024,256]{1,0:T(8,128)(2,1)S(1)} %slice.74), channel_id=1, source_target_pairs={{0,64},{16,80},{32,96},{48,112},{64,128},{80,144},{96,160},{112,17... | collective-permute-start | bytes 1572872 | tf_op jit(solution)/shard_map/ppermute | solution.py:279
  100.6 11.0 %collective-permute-start.14 = (bf16[1024,256]{1,0:T(8,128)(2,1)S(1)}, bf16[1024,256]{1,0:T(8,128)(2,1)}, u32[]{:S(2)}, u32[]{:S(2)}) collective-permute-start(bf16[1024,256]{1,0:T(8,128)(2,1)S(1)} %slice.75), channel_id=1, source_target_pairs={{0,192},{16,208},{32,224},{48,240},{64,0},{80,16},{96,32},{112,48}... | collective-permute-start | bytes 1572872 | tf_op jit(solution)/shard_map/ppermute | solution.py:279
  102.3 7.7 %collective-permute-start.11 = (bf16[512,256]{1,0:T(8,128)(2,1)S(1)}, bf16[512,256]{1,0:T(8,128)(2,1)S(1)}, u32[]{:S(2)}, u32[]{:S(2)}) collective-permute-start(bf16[512,256]{1,0:T(8,128)(2,1)S(1)} %add_convert_fusion.5), channel_id=1, source_target_pairs={{0,1},{1,2},{2,3},{3,0},{4,5},{5,6},{6,7},{7,4},{8,9},{9,10},{10,1... | collective-permute-start | bytes 786440 | tf_op jit(solution)/shard_map/ppermute | solution.py:239
  102.5 7.5 %collective-permute-start.12 = (bf16[512,256]{1,0:T(8,128)(2,1)S(1)}, bf16[512,256]{1,0:T(8,128)(2,1)S(1)}, u32[]{:S(2)}, u32[]{:S(2)}) collective-permute-start(bf16[512,256]{1,0:T(8,128)(2,1)S(1)} %add_convert_fusion.4), channel_id=1, source_target_pairs={{0,3},{1,0},{2,1},{3,2},{4,7},{5,4},{6,5},{7,6},{8,11},{9,8},{10,9... | collective-permute-start | bytes 786440 | tf_op jit(solution)/shard_map/ppermute | solution.py:239
  111.8 7.7 %collective-permute-start.17 = (bf16[256,256]{1,0:T(8,128)(2,1)S(1)}, bf16[256,256]{1,0:T(8,128)(2,1)S(1)}, u32[]{:S(2)}, u32[]{:S(2)}) collective-permute-start(bf16[256,256]{1,0:T(8,128)(2,1)S(1)} %get-tuple-element.74), channel_id=1, source_target_pairs={{0,4},{1,5},{2,6},{3,7},{4,8},{5,9},{6,10},{7,11},{8,12},{9,13},{1... | collective-permute-start | bytes 393224 | tf_op jit(solution)/shard_map/ppermute | solution.py:246
  115.7 7.9 %collective-permute-start.16 = (bf16[256,256]{1,0:T(8,128)(2,1)S(1)}, bf16[256,256]{1,0:T(8,128)(2,1)S(1)}, u32[]{:S(2)}, u32[]{:S(2)}) collective-permute-start(bf16[256,256]{1,0:T(8,128)(2,1)S(1)} %get-tuple-element.73), channel_id=1, source_target_pairs={{0,8},{1,9},{2,10},{3,11},{4,12},{5,13},{6,14},{7,15},{8,0},{9,1},... | collective-permute-start | bytes 393224 | tf_op jit(solution)/shard_map/ppermute | solution.py:246
  115.8 7.9 %collective-permute-start.15 = (bf16[256,256]{1,0:T(8,128)(2,1)S(1)}, bf16[256,256]{1,0:T(8,128)(2,1)S(1)}, u32[]{:S(2)}, u32[]{:S(2)}) collective-permute-start(bf16[256,256]{1,0:T(8,128)(2,1)S(1)} %slice.97), channel_id=1, source_target_pairs={{0,12},{1,13},{2,14},{3,15},{4,0},{5,1},{6,2},{7,3},{8,4},{9,5},{1... | collective-permute-start | bytes 393224 | tf_op jit(solution)/shard_map/ppermute | solution.py:246
  123.7 6.3 %collective-permute-start.18 = (bf16[256,256]{1,0:T(8,128)(2,1)S(1)}, bf16[256,256]{1,0:T(8,128)(2,1)S(1)}, u32[]{:S(2)}, u32[]{:S(2)}) collective-permute-start(bf16[256,256]{1,0:T(8,128)(2,1)S(1)} %add_convert_fusion.7.g0), channel_id=1, source_target_pairs={{0,64},{16,80},{32,96},{48,112},{64,128},{80,144},{96,160},{112,17... | collective-permute-start | bytes 393224 | tf_op jit(solution)/shard_map/ppermute | solution.py:279
  125.2 5.0 %collective-permute-start.19 = (bf16[256,256]{1,0:T(8,128)(2,1)S(1)}, bf16[256,256]{1,0:T(8,128)(2,1)S(1)}, u32[]{:S(2)}, u32[]{:S(2)}) collective-permute-start(bf16[256,256]{1,0:T(8,128)(2,1)S(1)} %add_convert_fusion.7.g0), channel_id=1, source_target_pairs={{0,192},{16,208},{32,224},{48,240},{64,0},{80,16},{96,32},{112,48}... | collective-permute-start | bytes 393224 | tf_op jit(solution)/shard_map/ppermute | solution.py:279
  127.0 6.5 %collective-permute-start.20 = (bf16[256,256]{1,0:T(8,128)(2,1)S(1)}, bf16[256,256]{1,0:T(8,128)(2,1)S(1)}, u32[]{:S(2)}, u32[]{:S(2)}) collective-permute-start(bf16[256,256]{1,0:T(8,128)(2,1)S(1)} %add_convert_fusion.7.g0), channel_id=1, source_target_pairs={{0,128},{16,144},{32,160},{48,176},{64,192},{80,208},{96,224},{112... | collective-permute-start | bytes 393224 | tf_op jit(solution)/shard_map/ppermute | solution.py:279
  138.1 3.9 %collective-permute-start.21 = (bf16[1024,256]{1,0:T(8,128)(2,1)}, bf16[1024,256]{1,0:T(8,128)(2,1)S(1)}, u32[]{:S(2)}, u32[]{:S(2)}) collective-permute-start(bf16[1024,256]{1,0:T(8,128)(2,1)} %shard_map.91), channel_id=1, source_target_pairs={{0,16},{16,0},{32,48},{48,32},{64,80},{80,64},{96,112},{112,96},{1... | collective-permute-start | bytes 1572872 | tf_op jit(solution)/shard_map/ppermute | solution.py:451
  143.3 8.8 %collective-permute-start.22 = (bf16[512,256]{1,0:T(8,128)(2,1)S(1)}, bf16[512,256]{1,0:T(8,128)(2,1)S(1)}, u32[]{:S(2)}, u32[]{:S(2)}) collective-permute-start(bf16[512,256]{1,0:T(8,128)(2,1)S(1)} %slice.100), channel_id=1, source_target_pairs={{0,1},{1,0},{2,3},{3,2},{4,5},{5,4},{6,7},{7,6},{8,9},{9,8},{10,11... | collective-permute-start | bytes 786440 | tf_op jit(solution)/shard_map/ppermute | solution.py:251
  152.2 6.4 %collective-permute-start.23 = (bf16[256,256]{1,0:T(8,128)(2,1)S(1)}, bf16[256,256]{1,0:T(8,128)(2,1)S(1)}, u32[]{:S(2)}, u32[]{:S(2)}) collective-permute-start(bf16[256,256]{1,0:T(8,128)(2,1)S(1)} %slice.103), channel_id=1, source_target_pairs={{0,3},{1,2},{2,1},{3,0},{4,7},{5,6},{6,5},{7,4},{8,11},{9,10},{10,... | collective-permute-start | bytes 393224 | tf_op jit(solution)/shard_map/ppermute | solution.py:251
  158.7 4.4 %collective-permute-start.24 = (bf16[128,256]{1,0:T(8,128)(2,1)S(1)}, bf16[128,256]{1,0:T(8,128)(2,1)S(1)}, u32[]{:S(2)}, u32[]{:S(2)}) collective-permute-start(bf16[128,256]{1,0:T(8,128)(2,1)S(1)} %slice.105), channel_id=1, source_target_pairs={{0,4},{1,5},{2,6},{3,7},{4,0},{5,1},{6,2},{7,3},{8,12},{9,13},{10,... | collective-permute-start | bytes 196616 | tf_op jit(solution)/shard_map/ppermute | solution.py:262
  163.1 5.8 %collective-permute-start.25 = (bf16[64,256]{1,0:T(8,128)(2,1)S(1)}, bf16[64,256]{1,0:T(8,128)(2,1)S(1)}, u32[]{:S(2)}, u32[]{:S(2)}) collective-permute-start(bf16[64,256]{1,0:T(8,128)(2,1)S(1)} %slice.107), channel_id=1, source_target_pairs={{0,12},{1,13},{2,14},{3,15},{4,8},{5,9},{6,10},{7,11},{8,4},{9,5},... | collective-permute-start | bytes 98312 | tf_op jit(solution)/shard_map/ppermute | solution.py:262
  168.9 5.7 %collective-permute-start.26 = (bf16[32,256]{1,0:T(8,128)(2,1)S(1)}, bf16[32,256]{1,0:T(8,128)(2,1)S(1)}, u32[]{:S(2)}, u32[]{:S(2)}) collective-permute-start(bf16[32,256]{1,0:T(8,128)(2,1)S(1)} %slice.109), channel_id=1, source_target_pairs={{0,44},{1,45},{2,46},{3,47},{4,40},{5,41},{6,42},{7,43},{8,36},{9,... | collective-permute-start | bytes 49160 | tf_op jit(solution)/shard_map/ppermute | solution.py:262
  (13 other events, 78.6 us)
Sparse Core Ops, SparseCore 0:
  13.4 78.8 all-gather.1

commit v3 on v2

--- a/solution.py
+++ b/solution.py
@@ -357,7 +357,7 @@
     piece = home.shape[0] // (NH * NC)
     full = pl.BlockSpec((piece, toks), lambda i, at: (i * NC + at[2 + which], 0))
     half = pl.BlockSpec((piece, toks), lambda i, at: (at[2 + which], 0))
-    grad = pl.BlockSpec((toks, width), lambda i, at: (0, 0))
+    grad = pl.BlockSpec(memory_space=pltpu.VMEM)
     gs = pltpu.PrefetchScalarGridSpec(
         num_scalar_prefetch=1,
         grid=(NH,),
@@ -420,7 +420,8 @@
     from_left, from_right, *sums = lax.optimization_barrier((from_left, from_right, *sums))
     keep, plus, minus, plus_late, minus_late = sums
     full = home.shape[0]
-    weight = lax.all_gather(kv_weight, "dp", axis=0, tiled=True)
+    held, _ = lax.optimization_barrier((kv_weight, near))
+    weight = lax.all_gather(held, "dp", axis=0, tiled=True)
 
     cut = plus_late.shape[0]
     feats_left, feats_right = from_left, from_right
@@ -432,13 +433,11 @@
     plus_late = total_of(plus_late, from_left[:cut]).astype(low)
     minus_late = total_of(minus_late, from_right[cut:]).astype(low)
     late_left, late_right = along_x(plus_late, 1), along_x(minus_late, -1)
-    late_left, late_right, feats_a, feats_b = lax.optimization_barrier(
-        (late_left, late_right, feats_a, feats_b)
-    )
     early = total_of(keep[:cut], late_left, from_right[:cut]).astype(low)
     late = total_of(keep[cut:], from_left[cut:], late_right).astype(low)
     spans = [early[:tok_rows], early[tok_rows:], late[:tok_rows], late[tok_rows:]]
     spans = [spans[0], *(along_z(spans[step], -step) for step in range(1, NZ))]
+    *spans, feats_a, feats_b = lax.optimization_barrier((*spans, feats_a, feats_b))
     owned = total_of(*spans).astype(low)
 
     grads = [along_y(owned, 1), along_y(owned, -1), along_y(owned, 2)]

time: 184 us -> 182 us (0.989)
  starting transfers between devices: 47.8 us -> 38.3 us
  waiting for transfers between devices: 50.4 us -> 59.1 us
    ppermute x3, starting transfers between devices: 8.93 us -> 3.42 us  [swap_z(): return lax.ppermute(array, ('dp', 'ctx'), pairs)]
    ppermute x3, waiting for transfers between devices: 6.92 us -> 11.8 us  [swap_z(): return lax.ppermute(array, ('dp', 'ctx'), pairs)]
    ppermute x2, starting transfers between devices: 3.22 us -> 0.29 us  [swap_x(): return lax.ppermute(array, 'ctx', pairs)]
    ppermute x2, waiting for transfers between devices: 6.51 us -> 9.4 us  [swap_x(): return lax.ppermute(array, 'ctx', pairs)]
where the time goes in v3:
time: 182 us; the launch traced here: 180 us
  waiting for transfers between devices  59.1 us (32%)
  Pallas kernels  58.4 us (32%)
  starting transfers between devices  38.3 us (21%)
  between operations  14.3 us (8%)
  matrix products  5.49 us (3%)
  other arithmetic  2.4 us (1%)
  local copies, waits for them, and re-layouts  2.29 us (1%)
    pallas_call x1, Pallas kernels, attention(): pl.pallas_call(functools.partial(attn_kernel, G, KC, seq // BLK, 1.0 / ma...  37.2 us
    ppermute x8, waiting for transfers between devices, along_x(): return lax.ppermute(array, 'ctx', pairs)  22.6 us
    ppermute x8, starting transfers between devices, along_x(): return lax.ppermute(array, 'ctx', pairs)  13.1 us
    ppermute x3, waiting for transfers between devices, swap_z(): return lax.ppermute(array, ('dp', 'ctx'), pairs)  11.8 us
    pallas_call x3, Pallas kernels, cut_features(): pl.pallas_call(cut_kernel, grid_spec=gs, out_shape=jax.ShapeDtypeStruct((...  11.7 us
    ppermute x7, starting transfers between devices, along_y(): return lax.ppermute(array, 'dp', pairs)  11.6 us
    ppermute x6, waiting for transfers between devices, along_z(): return lax.ppermute(array, 'ctx', pairs)  10 us
    ppermute x6, starting transfers between devices, along_z(): return lax.ppermute(array, 'ctx', pairs)  9.77 us
  transfers between devices with their start and end apart: 28, of which 18 were waited for; matrix products, arithmetic and copies ran while one was open for 4% of the time, Pallas kernels for 32%

profile of v3, /device:TPU:0, one launch (start us, length us, event | category | flops | bytes accessed | tf_op | source)
XLA Modules:
  0.0 180.2 jit_solution(5350653305613255697)
XLA Ops:
  7.2 1.6 shard_map.85
  9.0 3.3 %collective-permute-start.1 = (bf16[272,256]{1,0:T(8,128)(2,1)}, bf16[272,256]{1,0:T(8,128)(2,1)S(1)}, u32[]{:S(2)}, u32[]{:S(2)}) collective-permute-start(bf16[272,256]{1,0:T(8,128)(2,1)} %shard_map.85), channel_id=1, source_target_pairs={{0,8},{1,9},{2,10},{3,11},{4,12},{5,13},{6,14},{7,15},{8,0},{9,1},... | collective-permute-start | bytes 417800 | tf_op jit(solution)/shard_map/ppermute | solution.py:246
  13.8 4.5 %shard_map.86 = bf16[3072,256]{1,0:T(8,128)(2,1)} custom-call(s32[12]{0:T(128)} %stack.51.at_ref, bf16[256,8192]{1,0:T(8,128)(2,1)} %bitcast.21), custom_call_target="tpu_custom_call" | custom-call | bytes 3145728 | tf_op jit(solution)/shard_map/pallas_call | solution.py:315
  18.3 3.3 %collective-permute-done.1 = bf16[272,256]{1,0:T(8,128)(2,1)S(1)} collective-permute-done((bf16[272,256]{1,0:T(8,128)(2,1)}, bf16[272,256]{1,0:T(8,128)(2,1)S(1)}, u32[]{:S(2)}, u32[]{:S(2)}) %collective-permute-start.1) | collective-permute-done | bytes 139296 | tf_op jit(solution)/shard_map/ppermute | solution.py:246
  23.3 1.8 %collective-permute-start.4 = (bf16[1088,256]{1,0:T(8,128)(2,1)S(1)}, bf16[1088,256]{1,0:T(8,128)(2,1)S(1)}, u32[]{:S(2)}, u32[]{:S(2)}) collective-permute-start(bf16[1088,256]{1,0:T(8,128)(2,1)S(1)} %pad_maximum_fusion.near_ref), channel_id=1, source_target_pairs={{0,3},{1,0},{2,1},{3,2},{4,7},{5,4},{6,5},{7,6},{8,11},{9,8},{10,9... | collective-permute-start | bytes 1671176 | tf_op jit(solution)/shard_map/ppermute | solution.py:239
  25.1 4.3 %shard_map.87 = bf16[3072,256]{1,0:T(8,128)(2,1)} custom-call(s32[12]{0:T(128)} %stack.51.at_ref, bf16[256,8192]{1,0:T(8,128)(2,1)} %bitcast.22), custom_call_target="tpu_custom_call" | custom-call | bytes 3145728 | tf_op jit(solution)/shard_map/pallas_call | solution.py:315
  29.4 2.9 %shard_map.88.a_ref = bf16[2048,256]{1,0:T(8,128)(2,1)} custom-call(s32[12]{0:T(128)} %stack.51.at_ref, bf16[256,8192]{1,0:T(8,128)(2,1)} %bitcast.23), custom_call_target="tpu_custom_call" | custom-call | bytes 2097152 | tf_op jit(solution)/shard_map/pallas_call | solution.py:315
  32.3 5.1 %collective-permute-done.3.left_ref = bf16[1088,256]{1,0:T(8,128)(2,1)S(1)} collective-permute-done((bf16[1088,256]{1,0:T(8,128)(2,1)S(1)}, bf16[1088,256]{1,0:T(8,128)(2,1)S(1)}, u32[]{:S(2)}, u32[]{:S(2)}) %collective-permute-start.3) | collective-permute-done | bytes 557088 | tf_op jit(solution)/shard_map/ppermute | solution.py:239
  39.0 1.8 %collective-permute-start.6 = (bf16[544,256]{1,0:T(8,128)(2,1)S(1)}, bf16[544,256]{1,0:T(8,128)(2,1)S(1)}, u32[]{:S(2)}, u32[]{:S(2)}) collective-permute-start(bf16[544,256]{1,0:T(8,128)(2,1)S(1)} %slice.73), channel_id=1, source_target_pairs={{0,3},{1,0},{2,1},{3,2},{4,7},{5,4},{6,5},{7,6},{8,11},{9,8},{10,9... | collective-permute-start | bytes 835592 | tf_op jit(solution)/shard_map/ppermute | solution.py:239
  42.5 1.7 collective-permute-start.8
  44.1 2.2 %collective-permute-done.5.far_a_ref = bf16[544,256]{1,0:T(8,128)(2,1)S(1)} collective-permute-done((bf16[544,256]{1,0:T(8,128)(2,1)S(1)}, bf16[544,256]{1,0:T(8,128)(2,1)S(1)}, u32[]{:S(2)}, u32[]{:S(2)}) %collective-permute-start.5) | collective-permute-done | bytes 278560 | tf_op jit(solution)/shard_map/ppermute | solution.py:239
  47.1 37.2 %shard_map.89 = (bf16[256,2048]{1,0:T(8,128)(2,1)}, bf16[1024,256]{1,0:T(8,128)(2,1)}, bf16[1024,256]{1,0:T(8,128)(2,1)}, bf16[1024,256]{1,0:T(8,128)(2,1)}, bf1...) custom-call(bf16[256,2048]{1,0:T(8,128)(2,1)} %bitcast.25, bf16[256,2048]{1,0:T(8,128)(2,1)} %bitcast.26, ...), custom_call_target="tpu_custom_call" | custom-call | flops 40000000000 | bytes 8388608 | tf_op jit(solution)/shard_map/pallas_call | solution.py:201
  85.2 3.0 %collective-permute-start.10 = (bf16[1024,256]{1,0:T(8,128)(2,1)}, bf16[1024,256]{1,0:T(8,128)(2,1)S(1)}, u32[]{:S(2)}, u32[]{:S(2)}) collective-permute-start(bf16[1024,256]{1,0:T(8,128)(2,1)} %get-tuple-element.62), channel_id=1, source_target_pairs={{0,3},{1,0},{2,1},{3,2},{4,7},{5,4},{6,5},{7,6},{8,11},{9,8},{10,9... | collective-permute-start | bytes 1572872 | tf_op jit(solution)/shard_map/ppermute | solution.py:239
  88.3 11.0 %collective-permute-done.9 = bf16[1024,256]{1,0:T(8,128)(2,1)S(1)} collective-permute-done((bf16[1024,256]{1,0:T(8,128)(2,1)}, bf16[1024,256]{1,0:T(8,128)(2,1)S(1)}, u32[]{:S(2)}, u32[]{:S(2)}) %collective-permute-start.9) | collective-permute-done | bytes 524320 | tf_op jit(solution)/shard_map/ppermute | solution.py:239
  99.4 3.0 %collective-permute-start.13 = (bf16[512,256]{1,0:T(8,128)(2,1)S(1)}, bf16[512,256]{1,0:T(8,128)(2,1)S(1)}, u32[]{:S(2)}, u32[]{:S(2)}) collective-permute-start(bf16[512,256]{1,0:T(8,128)(2,1)S(1)} %add_convert_fusion.3), channel_id=1, source_target_pairs={{0,3},{1,0},{2,1},{3,2},{4,7},{5,4},{6,5},{7,6},{8,11},{9,8},{10,9... | collective-permute-start | bytes 786440 | tf_op jit(solution)/shard_map/ppermute | solution.py:239
  102.9 3.1 %collective-permute-start.17 = (bf16[1024,256]{1,0:T(8,128)(2,1)S(1)}, bf16[1024,256]{1,0:T(8,128)(2,1)S(1)}, u32[]{:S(2)}, u32[]{:S(2)}) collective-permute-start(bf16[1024,256]{1,0:T(8,128)(2,1)S(1)} %slice.76), channel_id=1, source_target_pairs={{0,192},{16,208},{32,224},{48,240},{64,0},{80,16},{96,32},{112,48}... | collective-permute-start | bytes 1572872 | tf_op jit(solution)/shard_map/ppermute | solution.py:279
  106.3 3.9 %collective-permute-done.11 = bf16[512,256]{1,0:T(8,128)(2,1)S(1)} collective-permute-done((bf16[512,256]{1,0:T(8,128)(2,1)S(1)}, bf16[512,256]{1,0:T(8,128)(2,1)S(1)}, u32[]{:S(2)}, u32[]{:S(2)}) %collective-permute-start.11) | collective-permute-done | bytes 262176 | tf_op jit(solution)/shard_map/ppermute | solution.py:239
  111.6 3.1 %collective-permute-start.14 = (bf16[256,256]{1,0:T(8,128)(2,1)S(1)}, bf16[256,256]{1,0:T(8,128)(2,1)S(1)}, u32[]{:S(2)}, u32[]{:S(2)}) collective-permute-start(bf16[256,256]{1,0:T(8,128)(2,1)S(1)} %get-tuple-element.80), channel_id=1, source_target_pairs={{0,8},{1,9},{2,10},{3,11},{4,12},{5,13},{6,14},{7,15},{8,0},{9,1},... | collective-permute-start | bytes 393224 | tf_op jit(solution)/shard_map/ppermute | solution.py:246
  115.8 1.9 %collective-permute-done.12 = bf16[256,256]{1,0:T(8,128)(2,1)S(1)} collective-permute-done((bf16[256,256]{1,0:T(8,128)(2,1)S(1)}, bf16[256,256]{1,0:T(8,128)(2,1)S(1)}, u32[]{:S(2)}, u32[]{:S(2)}) %collective-permute-start.12) | collective-permute-done | bytes 131104 | tf_op jit(solution)/shard_map/ppermute | solution.py:246
  117.7 4.7 %collective-permute-done.14 = bf16[256,256]{1,0:T(8,128)(2,1)S(1)} collective-permute-done((bf16[256,256]{1,0:T(8,128)(2,1)S(1)}, bf16[256,256]{1,0:T(8,128)(2,1)S(1)}, u32[]{:S(2)}, u32[]{:S(2)}) %collective-permute-start.14) | collective-permute-done | bytes 131104 | tf_op jit(solution)/shard_map/ppermute | solution.py:246
  123.9 1.9 %collective-permute-start.19 = (bf16[256,256]{1,0:T(8,128)(2,1)S(1)}, bf16[256,256]{1,0:T(8,128)(2,1)S(1)}, u32[]{:S(2)}, u32[]{:S(2)}) collective-permute-start(bf16[256,256]{1,0:T(8,128)(2,1)S(1)} %add_convert_fusion.7.g0), channel_id=1, source_target_pairs={{0,192},{16,208},{32,224},{48,240},{64,0},{80,16},{96,32},{112,48}... | collective-permute-start | bytes 393224 | tf_op jit(solution)/shard_map/ppermute | solution.py:279
  125.8 1.8 collective-permute-start.20
  128.9 3.4 %collective-permute-done.20.g3 = bf16[256,256]{1,0:T(8,128)(2,1)S(1)} collective-permute-done((bf16[256,256]{1,0:T(8,128)(2,1)S(1)}, bf16[256,256]{1,0:T(8,128)(2,1)S(1)}, u32[]{:S(2)}, u32[]{:S(2)}) %collective-permute-start.20) | collective-permute-done | bytes 131104 | tf_op jit(solution)/shard_map/ppermute | solution.py:279
  133.0 4.0 %shard_map.91 = bf16[1024,256]{1,0:T(8,128)(2,1)} custom-call(s32[12]{0:T(128)} %stack.51.at_ref, bf16[2048,256]{1,0:T(8,128)(2,1)} %shard_map.88.a_ref, bf16[3072,256]{1,0:T(8,128)(2,1)} %copy-done, bf16[3072,256]{1,0:T(8,128)(2,1)} %copy-done.1, bf16[1024,256]{1,0:T(8,128)(2,1)} %copy-done.4, bf16[1024,256]{1,0:T(8,128)(2,1)} %copy-done.5, ...), custom_call_target="tpu_custom_call" | custom-call | flops 1073741824 | bytes 3145728 | tf_op jit(solution)/shard_map/pallas_call | solution.py:367
  137.0 3.9 %shard_map.90 = bf16[1024,256]{1,0:T(8,128)(2,1)} custom-call(s32[12]{0:T(128)} %stack.51.at_ref, bf16[2048,256]{1,0:T(8,128)(2,1)} %shard_map.88.a_ref, bf16[3072,256]{1,0:T(8,128)(2,1)} %copy-done, bf16[3072,256]{1,0:T(8,128)(2,1)} %copy-done.1, bf16[1024,256]{1,0:T(8,128)(2,1)} %copy-done.4, bf16[1024,256]{1,0:T(8,128)(2,1)} %copy-done.5, ...), custom_call_target="tpu_custom_call" | custom-call | flops 1073741824 | bytes 3145728 | tf_op jit(solution)/shard_map/pallas_call | solution.py:367
  142.3 5.5 %fusion = bf16[1,256,8192]{2,1,0:T(8,128)(2,1)} fusion(bf16[256,256]{1,0:T(8,128)(2,1)S(1)} %copy-done.3, bf16[8192,256]{1,0:T(8,128)(2,1)} %all-gather.2.cloned.1.call-done), kind=kOutput, calls=%fused_computation.1 | convolution fusion | flops 1075838976 | bytes 8519680 | tf_op jit(solution)/shard_map/dot_general | solution.py:382
  147.8 3.2 %collective-permute-done.22 = bf16[512,256]{1,0:T(8,128)(2,1)S(1)} collective-permute-done((bf16[512,256]{1,0:T(8,128)(2,1)S(1)}, bf16[512,256]{1,0:T(8,128)(2,1)S(1)}, u32[]{:S(2)}, u32[]{:S(2)}) %collective-permute-start.22) | collective-permute-done | bytes 262176 | tf_op jit(solution)/shard_map/ppermute | solution.py:251
  151.2 6.2 %collective-permute-done.23 = bf16[256,256]{1,0:T(8,128)(2,1)S(1)} collective-permute-done((bf16[256,256]{1,0:T(8,128)(2,1)S(1)}, bf16[256,256]{1,0:T(8,128)(2,1)S(1)}, u32[]{:S(2)}, u32[]{:S(2)}) %collective-permute-start.23) | collective-permute-done | bytes 131104 | tf_op jit(solution)/shard_map/ppermute | solution.py:251
  157.6 4.3 %collective-permute-done.24 = bf16[128,256]{1,0:T(8,128)(2,1)S(1)} collective-permute-done((bf16[128,256]{1,0:T(8,128)(2,1)S(1)}, bf16[128,256]{1,0:T(8,128)(2,1)S(1)}, u32[]{:S(2)}, u32[]{:S(2)}) %collective-permute-start.24) | collective-permute-done | bytes 65568 | tf_op jit(solution)/shard_map/ppermute | solution.py:262
  162.8 4.9 %collective-permute-done.25 = bf16[64,256]{1,0:T(8,128)(2,1)S(1)} collective-permute-done((bf16[64,256]{1,0:T(8,128)(2,1)S(1)}, bf16[64,256]{1,0:T(8,128)(2,1)S(1)}, u32[]{:S(2)}, u32[]{:S(2)}) %collective-permute-start.25) | collective-permute-done | bytes 32800 | tf_op jit(solution)/shard_map/ppermute | solution.py:262
  167.7 2.4 %collective-permute-start.26 = (bf16[32,256]{1,0:T(8,128)(2,1)S(1)}, bf16[32,256]{1,0:T(8,128)(2,1)S(1)}, u32[]{:S(2)}, u32[]{:S(2)}) collective-permute-start(bf16[32,256]{1,0:T(8,128)(2,1)S(1)} %slice.109), channel_id=1, source_target_pairs={{0,44},{1,45},{2,46},{3,47},{4,40},{5,41},{6,42},{7,43},{8,36},{9,... | collective-permute-start | bytes 49160 | tf_op jit(solution)/shard_map/ppermute | solution.py:262
  170.2 2.6 %collective-permute-done.26 = bf16[32,256]{1,0:T(8,128)(2,1)S(1)} collective-permute-done((bf16[32,256]{1,0:T(8,128)(2,1)S(1)}, bf16[32,256]{1,0:T(8,128)(2,1)S(1)}, u32[]{:S(2)}, u32[]{:S(2)}) %collective-permute-start.26) | collective-permute-done | bytes 16416 | tf_op jit(solution)/shard_map/ppermute | solution.py:262
  (92 shorter events, 18.5 us)
Async XLA Ops:
  7.2 135.1 %all-gather.2.cloned.1.call-start = ((), (), s32[]{:S(2)}) async-start(), calls=%async_computation | async-start | bytes 4456448 | tf_op jit(solution)/shard_map/all_gather | solution.py:424
  8.8 9.5 %collective-permute-start = (bf16[272,256]{1,0:T(8,128)(2,1)}, bf16[272,256]{1,0:T(8,128)(2,1)S(1)}, u32[]{:S(2)}, u32[]{:S(2)}) collective-permute-start(bf16[272,256]{1,0:T(8,128)(2,1)} %shard_map.85), channel_id=1, source_target_pairs={{0,4},{1,5},{2,6},{3,7},{4,8},{5,9},{6,10},{7,11},{8,12},{9,13},{1... | collective-permute-start | bytes 417800 | tf_op jit(solution)/shard_map/ppermute | solution.py:246
  9.0 12.7 %collective-permute-start.1 = (bf16[272,256]{1,0:T(8,128)(2,1)}, bf16[272,256]{1,0:T(8,128)(2,1)S(1)}, u32[]{:S(2)}, u32[]{:S(2)}) collective-permute-start(bf16[272,256]{1,0:T(8,128)(2,1)} %shard_map.85), channel_id=1, source_target_pairs={{0,8},{1,9},{2,10},{3,11},{4,12},{5,13},{6,14},{7,15},{8,0},{9,1},... | collective-permute-start | bytes 417800 | tf_op jit(solution)/shard_map/ppermute | solution.py:246
  12.2 9.4 %collective-permute-start.2 = (bf16[272,256]{1,0:T(8,128)(2,1)}, bf16[272,256]{1,0:T(8,128)(2,1)S(1)}, u32[]{:S(2)}, u32[]{:S(2)}) collective-permute-start(bf16[272,256]{1,0:T(8,128)(2,1)} %shard_map.85), channel_id=1, source_target_pairs={{0,12},{1,13},{2,14},{3,15},{4,0},{5,1},{6,2},{7,3},{8,4},{9,5},{1... | collective-permute-start | bytes 417800 | tf_op jit(solution)/shard_map/ppermute | solution.py:246
  21.7 15.7 %collective-permute-start.3 = (bf16[1088,256]{1,0:T(8,128)(2,1)S(1)}, bf16[1088,256]{1,0:T(8,128)(2,1)S(1)}, u32[]{:S(2)}, u32[]{:S(2)}) collective-permute-start(bf16[1088,256]{1,0:T(8,128)(2,1)S(1)} %pad_maximum_fusion.near_ref), channel_id=1, source_target_pairs={{0,1},{1,2},{2,3},{3,0},{4,5},{5,6},{6,7},{7,4},{8,9},{9,10},{10,1... | collective-permute-start | bytes 1671176 | tf_op jit(solution)/shard_map/ppermute | solution.py:239
  23.3 14.2 %collective-permute-start.4 = (bf16[1088,256]{1,0:T(8,128)(2,1)S(1)}, bf16[1088,256]{1,0:T(8,128)(2,1)S(1)}, u32[]{:S(2)}, u32[]{:S(2)}) collective-permute-start(bf16[1088,256]{1,0:T(8,128)(2,1)S(1)} %pad_maximum_fusion.near_ref), channel_id=1, source_target_pairs={{0,3},{1,0},{2,1},{3,2},{4,7},{5,4},{6,5},{7,6},{8,11},{9,8},{10,9... | collective-permute-start | bytes 1671176 | tf_op jit(solution)/shard_map/ppermute | solution.py:239
  37.5 8.8 %collective-permute-start.5 = (bf16[544,256]{1,0:T(8,128)(2,1)S(1)}, bf16[544,256]{1,0:T(8,128)(2,1)S(1)}, u32[]{:S(2)}, u32[]{:S(2)}) collective-permute-start(bf16[544,256]{1,0:T(8,128)(2,1)S(1)} %slice.72), channel_id=1, source_target_pairs={{0,1},{1,2},{2,3},{3,0},{4,5},{5,6},{6,7},{7,4},{8,9},{9,10},{10,1... | collective-permute-start | bytes 835592 | tf_op jit(solution)/shard_map/ppermute | solution.py:239
  39.0 7.3 %collective-permute-start.6 = (bf16[544,256]{1,0:T(8,128)(2,1)S(1)}, bf16[544,256]{1,0:T(8,128)(2,1)S(1)}, u32[]{:S(2)}, u32[]{:S(2)}) collective-permute-start(bf16[544,256]{1,0:T(8,128)(2,1)S(1)} %slice.73), channel_id=1, source_target_pairs={{0,3},{1,0},{2,1},{3,2},{4,7},{5,4},{6,5},{7,6},{8,11},{9,8},{10,9... | collective-permute-start | bytes 835592 | tf_op jit(solution)/shard_map/ppermute | solution.py:239
  40.9 44.0 %collective-permute-start.7 = (bf16[3072,256]{1,0:T(8,128)(2,1)}, bf16[3072,256]{1,0:T(8,128)(2,1)S(1)}, u32[]{:S(2)}, u32[]{:S(2)}) collective-permute-start(bf16[3072,256]{1,0:T(8,128)(2,1)} %shard_map.86), channel_id=1, source_target_pairs={{0,64},{16,80},{32,96},{48,112},{64,128},{80,144},{96,160},{112,17... | collective-permute-start | bytes 4718600 | tf_op jit(solution)/shard_map/ppermute | solution.py:279
  42.5 42.4 %collective-permute-start.8 = (bf16[3072,256]{1,0:T(8,128)(2,1)}, bf16[3072,256]{1,0:T(8,128)(2,1)S(1)}, u32[]{:S(2)}, u32[]{:S(2)}) collective-permute-start(bf16[3072,256]{1,0:T(8,128)(2,1)} %shard_map.87), channel_id=1, source_target_pairs={{0,192},{16,208},{32,224},{48,240},{64,0},{80,16},{96,32},{112,48}... | collective-permute-start | bytes 4718600 | tf_op jit(solution)/shard_map/ppermute | solution.py:279
  84.3 18.1 %copy-start.12 = (bf16[512,256]{1,0:T(8,128)(2,1)S(1)}, bf16[512,256]{1,0:T(8,128)(2,1)}, u32[]{:S(2)}) copy-start(bf16[512,256]{1,0:T(8,128)(2,1)} %get-tuple-element.60) | copy-start | bytes 786436
  84.9 17.6 %copy-start = (bf16[3072,256]{1,0:T(8,128)(2,1)}, bf16[3072,256]{1,0:T(8,128)(2,1)S(1)}, u32[]{:S(2)}) copy-start(bf16[3072,256]{1,0:T(8,128)(2,1)S(1)} %collective-permute-done.7.b_ref) | copy-start | bytes 4718596
  84.9 17.6 %copy-start.1 = (bf16[3072,256]{1,0:T(8,128)(2,1)}, bf16[3072,256]{1,0:T(8,128)(2,1)S(1)}, u32[]{:S(2)}) copy-start(bf16[3072,256]{1,0:T(8,128)(2,1)S(1)} %collective-permute-done.8.c_ref) | copy-start | bytes 4718596
  84.9 14.4 %collective-permute-start.9 = (bf16[1024,256]{1,0:T(8,128)(2,1)}, bf16[1024,256]{1,0:T(8,128)(2,1)S(1)}, u32[]{:S(2)}, u32[]{:S(2)}) collective-permute-start(bf16[1024,256]{1,0:T(8,128)(2,1)} %get-tuple-element.61), channel_id=1, source_target_pairs={{0,1},{1,2},{2,3},{3,0},{4,5},{5,6},{6,7},{7,4},{8,9},{9,10},{10,1... | collective-permute-start | bytes 1572872 | tf_op jit(solution)/shard_map/ppermute | solution.py:239
  85.2 14.1 %collective-permute-start.10 = (bf16[1024,256]{1,0:T(8,128)(2,1)}, bf16[1024,256]{1,0:T(8,128)(2,1)S(1)}, u32[]{:S(2)}, u32[]{:S(2)}) collective-permute-start(bf16[1024,256]{1,0:T(8,128)(2,1)} %get-tuple-element.62), channel_id=1, source_target_pairs={{0,3},{1,0},{2,1},{3,2},{4,7},{5,4},{6,5},{7,6},{8,11},{9,8},{10,9... | collective-permute-start | bytes 1572872 | tf_op jit(solution)/shard_map/ppermute | solution.py:239
  88.2 22.0 %copy-start.11 = (bf16[1024,256]{1,0:T(8,128)(2,1)S(1)}, bf16[1024,256]{1,0:T(8,128)(2,1)}, u32[]{:S(2)}) copy-start(bf16[1024,256]{1,0:T(8,128)(2,1)} %get-tuple-element.59) | copy-start | bytes 1572868
  99.4 6.9 %collective-permute-start.13 = (bf16[512,256]{1,0:T(8,128)(2,1)S(1)}, bf16[512,256]{1,0:T(8,128)(2,1)S(1)}, u32[]{:S(2)}, u32[]{:S(2)}) collective-permute-start(bf16[512,256]{1,0:T(8,128)(2,1)S(1)} %add_convert_fusion.3), channel_id=1, source_target_pairs={{0,3},{1,0},{2,1},{3,2},{4,7},{5,4},{6,5},{7,6},{8,11},{9,8},{10,9... | collective-permute-start | bytes 786440 | tf_op jit(solution)/shard_map/ppermute | solution.py:239
  102.5 7.7 %collective-permute-start.11 = (bf16[512,256]{1,0:T(8,128)(2,1)S(1)}, bf16[512,256]{1,0:T(8,128)(2,1)S(1)}, u32[]{:S(2)}, u32[]{:S(2)}) collective-permute-start(bf16[512,256]{1,0:T(8,128)(2,1)S(1)} %add_convert_fusion.5), channel_id=1, source_target_pairs={{0,1},{1,2},{2,3},{3,0},{4,5},{5,6},{6,7},{7,4},{8,9},{9,10},{10,1... | collective-permute-start | bytes 786440 | tf_op jit(solution)/shard_map/ppermute | solution.py:239
  102.6 19.8 %collective-permute-start.16 = (bf16[1024,256]{1,0:T(8,128)(2,1)S(1)}, bf16[1024,256]{1,0:T(8,128)(2,1)S(1)}, u32[]{:S(2)}, u32[]{:S(2)}) collective-permute-start(bf16[1024,256]{1,0:T(8,128)(2,1)S(1)} %slice.75), channel_id=1, source_target_pairs={{0,64},{16,80},{32,96},{48,112},{64,128},{80,144},{96,160},{112,17... | collective-permute-start | bytes 1572872 | tf_op jit(solution)/shard_map/ppermute | solution.py:279
  102.9 19.5 %collective-permute-start.17 = (bf16[1024,256]{1,0:T(8,128)(2,1)S(1)}, bf16[1024,256]{1,0:T(8,128)(2,1)S(1)}, u32[]{:S(2)}, u32[]{:S(2)}) collective-permute-start(bf16[1024,256]{1,0:T(8,128)(2,1)S(1)} %slice.76), channel_id=1, source_target_pairs={{0,192},{16,208},{32,224},{48,240},{64,0},{80,16},{96,32},{112,48}... | collective-permute-start | bytes 1572872 | tf_op jit(solution)/shard_map/ppermute | solution.py:279
  110.4 7.2 %collective-permute-start.12 = (bf16[256,256]{1,0:T(8,128)(2,1)S(1)}, bf16[256,256]{1,0:T(8,128)(2,1)S(1)}, u32[]{:S(2)}, u32[]{:S(2)}) collective-permute-start(bf16[256,256]{1,0:T(8,128)(2,1)S(1)} %get-tuple-element.81), channel_id=1, source_target_pairs={{0,12},{1,13},{2,14},{3,15},{4,0},{5,1},{6,2},{7,3},{8,4},{9,5},{1... | collective-permute-start | bytes 393224 | tf_op jit(solution)/shard_map/ppermute | solution.py:246
  111.6 10.8 %collective-permute-start.14 = (bf16[256,256]{1,0:T(8,128)(2,1)S(1)}, bf16[256,256]{1,0:T(8,128)(2,1)S(1)}, u32[]{:S(2)}, u32[]{:S(2)}) collective-permute-start(bf16[256,256]{1,0:T(8,128)(2,1)S(1)} %get-tuple-element.80), channel_id=1, source_target_pairs={{0,8},{1,9},{2,10},{3,11},{4,12},{5,13},{6,14},{7,15},{8,0},{9,1},... | collective-permute-start | bytes 393224 | tf_op jit(solution)/shard_map/ppermute | solution.py:246
  114.7 7.7 %collective-permute-start.15 = (bf16[256,256]{1,0:T(8,128)(2,1)S(1)}, bf16[256,256]{1,0:T(8,128)(2,1)S(1)}, u32[]{:S(2)}, u32[]{:S(2)}) collective-permute-start(bf16[256,256]{1,0:T(8,128)(2,1)S(1)} %get-tuple-element.79), channel_id=1, source_target_pairs={{0,4},{1,5},{2,6},{3,7},{4,8},{5,9},{6,10},{7,11},{8,12},{9,13},{1... | collective-permute-start | bytes 393224 | tf_op jit(solution)/shard_map/ppermute | solution.py:246
  122.5 6.3 %collective-permute-start.18 = (bf16[256,256]{1,0:T(8,128)(2,1)S(1)}, bf16[256,256]{1,0:T(8,128)(2,1)S(1)}, u32[]{:S(2)}, u32[]{:S(2)}) collective-permute-start(bf16[256,256]{1,0:T(8,128)(2,1)S(1)} %add_convert_fusion.7.g0), channel_id=1, source_target_pairs={{0,64},{16,80},{32,96},{48,112},{64,128},{80,144},{96,160},{112,17... | collective-permute-start | bytes 393224 | tf_op jit(solution)/shard_map/ppermute | solution.py:279
  123.9 5.0 %collective-permute-start.19 = (bf16[256,256]{1,0:T(8,128)(2,1)S(1)}, bf16[256,256]{1,0:T(8,128)(2,1)S(1)}, u32[]{:S(2)}, u32[]{:S(2)}) collective-permute-start(bf16[256,256]{1,0:T(8,128)(2,1)S(1)} %add_convert_fusion.7.g0), channel_id=1, source_target_pairs={{0,192},{16,208},{32,224},{48,240},{64,0},{80,16},{96,32},{112,48}... | collective-permute-start | bytes 393224 | tf_op jit(solution)/shard_map/ppermute | solution.py:279
  125.8 6.5 %collective-permute-start.20 = (bf16[256,256]{1,0:T(8,128)(2,1)S(1)}, bf16[256,256]{1,0:T(8,128)(2,1)S(1)}, u32[]{:S(2)}, u32[]{:S(2)}) collective-permute-start(bf16[256,256]{1,0:T(8,128)(2,1)S(1)} %add_convert_fusion.7.g0), channel_id=1, source_target_pairs={{0,128},{16,144},{32,160},{48,176},{64,192},{80,208},{96,224},{112... | collective-permute-start | bytes 393224 | tf_op jit(solution)/shard_map/ppermute | solution.py:279
  137.0 4.0 %collective-permute-start.21 = (bf16[1024,256]{1,0:T(8,128)(2,1)}, bf16[1024,256]{1,0:T(8,128)(2,1)S(1)}, u32[]{:S(2)}, u32[]{:S(2)}) collective-permute-start(bf16[1024,256]{1,0:T(8,128)(2,1)} %shard_map.91), channel_id=1, source_target_pairs={{0,16},{16,0},{32,48},{48,32},{64,80},{80,64},{96,112},{112,96},{1... | collective-permute-start | bytes 1572872 | tf_op jit(solution)/shard_map/ppermute | solution.py:450
  142.1 8.8 %collective-permute-start.22 = (bf16[512,256]{1,0:T(8,128)(2,1)S(1)}, bf16[512,256]{1,0:T(8,128)(2,1)S(1)}, u32[]{:S(2)}, u32[]{:S(2)}) collective-permute-start(bf16[512,256]{1,0:T(8,128)(2,1)S(1)} %slice.100), channel_id=1, source_target_pairs={{0,1},{1,0},{2,3},{3,2},{4,5},{5,4},{6,7},{7,6},{8,9},{9,8},{10,11... | collective-permute-start | bytes 786440 | tf_op jit(solution)/shard_map/ppermute | solution.py:251
  151.0 6.4 %collective-permute-start.23 = (bf16[256,256]{1,0:T(8,128)(2,1)S(1)}, bf16[256,256]{1,0:T(8,128)(2,1)S(1)}, u32[]{:S(2)}, u32[]{:S(2)}) collective-permute-start(bf16[256,256]{1,0:T(8,128)(2,1)S(1)} %slice.103), channel_id=1, source_target_pairs={{0,3},{1,2},{2,1},{3,0},{4,7},{5,6},{6,5},{7,4},{8,11},{9,10},{10,... | collective-permute-start | bytes 393224 | tf_op jit(solution)/shard_map/ppermute | solution.py:251
  157.5 4.4 %collective-permute-start.24 = (bf16[128,256]{1,0:T(8,128)(2,1)S(1)}, bf16[128,256]{1,0:T(8,128)(2,1)S(1)}, u32[]{:S(2)}, u32[]{:S(2)}) collective-permute-start(bf16[128,256]{1,0:T(8,128)(2,1)S(1)} %slice.105), channel_id=1, source_target_pairs={{0,4},{1,5},{2,6},{3,7},{4,0},{5,1},{6,2},{7,3},{8,12},{9,13},{10,... | collective-permute-start | bytes 196616 | tf_op jit(solution)/shard_map/ppermute | solution.py:262
  161.9 5.8 %collective-permute-start.25 = (bf16[64,256]{1,0:T(8,128)(2,1)S(1)}, bf16[64,256]{1,0:T(8,128)(2,1)S(1)}, u32[]{:S(2)}, u32[]{:S(2)}) collective-permute-start(bf16[64,256]{1,0:T(8,128)(2,1)S(1)} %slice.107), channel_id=1, source_target_pairs={{0,12},{1,13},{2,14},{3,15},{4,8},{5,9},{6,10},{7,11},{8,4},{9,5},... | collective-permute-start | bytes 98312 | tf_op jit(solution)/shard_map/ppermute | solution.py:262
  167.7 5.0 %collective-permute-start.26 = (bf16[32,256]{1,0:T(8,128)(2,1)S(1)}, bf16[32,256]{1,0:T(8,128)(2,1)S(1)}, u32[]{:S(2)}, u32[]{:S(2)}) collective-permute-start(bf16[32,256]{1,0:T(8,128)(2,1)S(1)} %slice.109), channel_id=1, source_target_pairs={{0,44},{1,45},{2,46},{3,47},{4,40},{5,41},{6,42},{7,43},{8,36},{9,... | collective-permute-start | bytes 49160 | tf_op jit(solution)/shard_map/ppermute | solution.py:262
  (14 other events, 83.8 us)
Sparse Core Ops, SparseCore 0:
  25.2 80.9 all-gather.1

commit v4 on v3

--- a/solution.py
+++ b/solution.py
@@ -115,8 +115,13 @@
     state = lax.fori_loop(
         0, runs, lambda i, state: scores(i * LONG * KC, LONG * KC, state, False), state
     )
+    done = runs * LONG
+    middle = (nk - 1 - done) // 2
     state = lax.fori_loop(
-        runs * LONG, nk - 1, lambda i, state: scores(i * KC, KC, state, False), state
+        0, middle, lambda i, state: scores(done * KC, 2 * KC, state, False), state
+    )
+    state = lax.fori_loop(
+        done + 2 * middle, nk - 1, lambda i, state: scores(i * KC, KC, state, False), state
     )
     m, l, d = scores((nk - 1) * KC, KC, state, True)
     top = jnp.max(m, axis=0, keepdims=True)
@@ -158,7 +163,15 @@
         return 0
 
     lax.fori_loop(0, pairs, pair, 0)
-    lax.fori_loop(pairs * (2 * run // KC), nk, single, 0)
+    spent = pairs * (2 * run // KC)
+    left = (nk - spent) // (run // KC)
+
+    @pl.when(left > 0)
+    def _():
+        weigh(spent * KC, run, p_even, d_even)
+        spend(spent * KC, run, p_even, d_even)
+
+    lax.fori_loop(spent + left * (run // KC), nk, single, 0)
 
     for h in range(G):
         cols = slice(h * BLK, (h + 1) * BLK)

time: 182 us -> 182 us (level)
  transfers between devices with their start and end apart: 28 -> 28, of which waited for: 18 -> 17; matrix products, arithmetic and copies ran while one was open for 4% -> 4% of each run, Pallas kernels for 32% -> 32%
where the time goes in v4:
time: 182 us; the launch traced here: 180 us
  Pallas kernels  59.1 us (32%)
  waiting for transfers between devices  58.7 us (32%)
  starting transfers between devices  38.2 us (21%)
  between operations  14.3 us (8%)
  matrix products  5.49 us (3%)
  other arithmetic  2.4 us (1%)
  local copies, waits for them, and re-layouts  2.29 us (1%)
    pallas_call x1, Pallas kernels, attention(): pl.pallas_call(functools.partial(attn_kernel, G, KC, seq // BLK, 1.0 / ma...  37.9 us
    ppermute x8, waiting for transfers between devices, along_x(): return lax.ppermute(array, 'ctx', pairs)  22.2 us
    ppermute x8, starting transfers between devices, along_x(): return lax.ppermute(array, 'ctx', pairs)  13.1 us
    ppermute x7, starting transfers between devices, along_y(): return lax.ppermute(array, 'dp', pairs)  12.2 us
    ppermute x3, waiting for transfers between devices, swap_z(): return lax.ppermute(array, ('dp', 'ctx'), pairs)  12.2 us
    pallas_call x3, Pallas kernels, cut_features(): pl.pallas_call(cut_kernel, grid_spec=gs, out_shape=jax.ShapeDtypeStruct((...  11.7 us
    ppermute x6, waiting for transfers between devices, along_z(): return lax.ppermute(array, 'ctx', pairs)  10.5 us
    ppermute x6, starting transfers between devices, along_z(): return lax.ppermute(array, 'ctx', pairs)  9.55 us
  transfers between devices with their start and end apart: 28, of which 17 were waited for; matrix products, arithmetic and copies ran while one was open for 4% of the time, Pallas kernels for 32%

profile of v4, /device:TPU:0, one launch (start us, length us, event | category | flops | bytes accessed | tf_op | source)
XLA Modules:
  0.0 180.5 jit_solution(4469950200745862484)
XLA Ops:
  7.2 1.6 shard_map.85
  9.0 3.3 %collective-permute-start.1 = (bf16[272,256]{1,0:T(8,128)(2,1)}, bf16[272,256]{1,0:T(8,128)(2,1)S(1)}, u32[]{:S(2)}, u32[]{:S(2)}) collective-permute-start(bf16[272,256]{1,0:T(8,128)(2,1)} %shard_map.85), channel_id=1, source_target_pairs={{0,8},{1,9},{2,10},{3,11},{4,12},{5,13},{6,14},{7,15},{8,0},{9,1},... | collective-permute-start | bytes 417800 | tf_op jit(solution)/shard_map/ppermute | solution.py:259
  13.8 4.5 %shard_map.86 = bf16[3072,256]{1,0:T(8,128)(2,1)} custom-call(s32[12]{0:T(128)} %stack.51.at_ref, bf16[256,8192]{1,0:T(8,128)(2,1)} %bitcast.21), custom_call_target="tpu_custom_call" | custom-call | bytes 3145728 | tf_op jit(solution)/shard_map/pallas_call | solution.py:328
  18.3 3.3 %collective-permute-done.1 = bf16[272,256]{1,0:T(8,128)(2,1)S(1)} collective-permute-done((bf16[272,256]{1,0:T(8,128)(2,1)}, bf16[272,256]{1,0:T(8,128)(2,1)S(1)}, u32[]{:S(2)}, u32[]{:S(2)}) %collective-permute-start.1) | collective-permute-done | bytes 139296 | tf_op jit(solution)/shard_map/ppermute | solution.py:259
  23.3 1.8 collective-permute-start.4
  25.1 4.3 %shard_map.87 = bf16[3072,256]{1,0:T(8,128)(2,1)} custom-call(s32[12]{0:T(128)} %stack.51.at_ref, bf16[256,8192]{1,0:T(8,128)(2,1)} %bitcast.22), custom_call_target="tpu_custom_call" | custom-call | bytes 3145728 | tf_op jit(solution)/shard_map/pallas_call | solution.py:328
  29.4 2.9 %shard_map.88.a_ref = bf16[2048,256]{1,0:T(8,128)(2,1)} custom-call(s32[12]{0:T(128)} %stack.51.at_ref, bf16[256,8192]{1,0:T(8,128)(2,1)} %bitcast.23), custom_call_target="tpu_custom_call" | custom-call | bytes 2097152 | tf_op jit(solution)/shard_map/pallas_call | solution.py:328
  32.3 5.1 %collective-permute-done.3.left_ref = bf16[1088,256]{1,0:T(8,128)(2,1)S(1)} collective-permute-done((bf16[1088,256]{1,0:T(8,128)(2,1)S(1)}, bf16[1088,256]{1,0:T(8,128)(2,1)S(1)}, u32[]{:S(2)}, u32[]{:S(2)}) %collective-permute-start.3) | collective-permute-done | bytes 557088 | tf_op jit(solution)/shard_map/ppermute | solution.py:252
  39.0 1.8 %collective-permute-start.6 = (bf16[544,256]{1,0:T(8,128)(2,1)S(1)}, bf16[544,256]{1,0:T(8,128)(2,1)S(1)}, u32[]{:S(2)}, u32[]{:S(2)}) collective-permute-start(bf16[544,256]{1,0:T(8,128)(2,1)S(1)} %slice.73), channel_id=1, source_target_pairs={{0,3},{1,0},{2,1},{3,2},{4,7},{5,4},{6,5},{7,6},{8,11},{9,8},{10,9... | collective-permute-start | bytes 835592 | tf_op jit(solution)/shard_map/ppermute | solution.py:252
  42.5 1.7 collective-permute-start.8
  44.1 2.2 %collective-permute-done.5.far_a_ref = bf16[544,256]{1,0:T(8,128)(2,1)S(1)} collective-permute-done((bf16[544,256]{1,0:T(8,128)(2,1)S(1)}, bf16[544,256]{1,0:T(8,128)(2,1)S(1)}, u32[]{:S(2)}, u32[]{:S(2)}) %collective-permute-start.5) | collective-permute-done | bytes 278560 | tf_op jit(solution)/shard_map/ppermute | solution.py:252
  47.1 37.9 %shard_map.89 = (bf16[256,2048]{1,0:T(8,128)(2,1)}, bf16[1024,256]{1,0:T(8,128)(2,1)}, bf16[1024,256]{1,0:T(8,128)(2,1)}, bf16[1024,256]{1,0:T(8,128)(2,1)}, bf1...) custom-call(bf16[256,2048]{1,0:T(8,128)(2,1)} %bitcast.25, bf16[256,2048]{1,0:T(8,128)(2,1)} %bitcast.26, ...), custom_call_target="tpu_custom_call" | custom-call | flops 40000000000 | bytes 8388608 | tf_op jit(solution)/shard_map/pallas_call | solution.py:214
  85.2 3.2 %collective-permute-start.10 = (bf16[1024,256]{1,0:T(8,128)(2,1)}, bf16[1024,256]{1,0:T(8,128)(2,1)S(1)}, u32[]{:S(2)}, u32[]{:S(2)}) collective-permute-start(bf16[1024,256]{1,0:T(8,128)(2,1)} %get-tuple-element.62), channel_id=1, source_target_pairs={{0,3},{1,0},{2,1},{3,2},{4,7},{5,4},{6,5},{7,6},{8,11},{9,8},{10,9... | collective-permute-start | bytes 1572872 | tf_op jit(solution)/shard_map/ppermute | solution.py:252
  88.5 10.9 %collective-permute-done.9 = bf16[1024,256]{1,0:T(8,128)(2,1)S(1)} collective-permute-done((bf16[1024,256]{1,0:T(8,128)(2,1)}, bf16[1024,256]{1,0:T(8,128)(2,1)S(1)}, u32[]{:S(2)}, u32[]{:S(2)}) %collective-permute-start.9) | collective-permute-done | bytes 524320 | tf_op jit(solution)/shard_map/ppermute | solution.py:252
  99.4 3.0 %collective-permute-start.13 = (bf16[512,256]{1,0:T(8,128)(2,1)S(1)}, bf16[512,256]{1,0:T(8,128)(2,1)S(1)}, u32[]{:S(2)}, u32[]{:S(2)}) collective-permute-start(bf16[512,256]{1,0:T(8,128)(2,1)S(1)} %add_convert_fusion.3), channel_id=1, source_target_pairs={{0,3},{1,0},{2,1},{3,2},{4,7},{5,4},{6,5},{7,6},{8,11},{9,8},{10,9... | collective-permute-start | bytes 786440 | tf_op jit(solution)/shard_map/ppermute | solution.py:252
  103.8 2.4 %collective-permute-start.17 = (bf16[1024,256]{1,0:T(8,128)(2,1)S(1)}, bf16[1024,256]{1,0:T(8,128)(2,1)S(1)}, u32[]{:S(2)}, u32[]{:S(2)}) collective-permute-start(bf16[1024,256]{1,0:T(8,128)(2,1)S(1)} %slice.76), channel_id=1, source_target_pairs={{0,192},{16,208},{32,224},{48,240},{64,0},{80,16},{96,32},{112,48}... | collective-permute-start | bytes 1572872 | tf_op jit(solution)/shard_map/ppermute | solution.py:292
  106.3 3.9 %collective-permute-done.11 = bf16[512,256]{1,0:T(8,128)(2,1)S(1)} collective-permute-done((bf16[512,256]{1,0:T(8,128)(2,1)S(1)}, bf16[512,256]{1,0:T(8,128)(2,1)S(1)}, u32[]{:S(2)}, u32[]{:S(2)}) %collective-permute-start.11) | collective-permute-done | bytes 262176 | tf_op jit(solution)/shard_map/ppermute | solution.py:252
  111.3 3.9 %collective-permute-start.14 = (bf16[256,256]{1,0:T(8,128)(2,1)S(1)}, bf16[256,256]{1,0:T(8,128)(2,1)S(1)}, u32[]{:S(2)}, u32[]{:S(2)}) collective-permute-start(bf16[256,256]{1,0:T(8,128)(2,1)S(1)} %get-tuple-element.80), channel_id=1, source_target_pairs={{0,8},{1,9},{2,10},{3,11},{4,12},{5,13},{6,14},{7,15},{8,0},{9,1},... | collective-permute-start | bytes 393224 | tf_op jit(solution)/shard_map/ppermute | solution.py:259
  115.5 2.9 %collective-permute-done.12 = bf16[256,256]{1,0:T(8,128)(2,1)S(1)} collective-permute-done((bf16[256,256]{1,0:T(8,128)(2,1)S(1)}, bf16[256,256]{1,0:T(8,128)(2,1)S(1)}, u32[]{:S(2)}, u32[]{:S(2)}) %collective-permute-start.12) | collective-permute-done | bytes 131104 | tf_op jit(solution)/shard_map/ppermute | solution.py:259
  118.4 4.2 %collective-permute-done.14 = bf16[256,256]{1,0:T(8,128)(2,1)S(1)} collective-permute-done((bf16[256,256]{1,0:T(8,128)(2,1)S(1)}, bf16[256,256]{1,0:T(8,128)(2,1)S(1)}, u32[]{:S(2)}, u32[]{:S(2)}) %collective-permute-start.14) | collective-permute-done | bytes 131104 | tf_op jit(solution)/shard_map/ppermute | solution.py:259
  122.8 1.7 collective-permute-start.18
  126.1 2.1 %collective-permute-start.20 = (bf16[256,256]{1,0:T(8,128)(2,1)S(1)}, bf16[256,256]{1,0:T(8,128)(2,1)S(1)}, u32[]{:S(2)}, u32[]{:S(2)}) collective-permute-start(bf16[256,256]{1,0:T(8,128)(2,1)S(1)} %add_convert_fusion.7.g0), channel_id=1, source_target_pairs={{0,128},{16,144},{32,160},{48,176},{64,192},{80,208},{96,224},{112... | collective-permute-start | bytes 393224 | tf_op jit(solution)/shard_map/ppermute | solution.py:292
  129.5 3.1 %collective-permute-done.20.g3 = bf16[256,256]{1,0:T(8,128)(2,1)S(1)} collective-permute-done((bf16[256,256]{1,0:T(8,128)(2,1)S(1)}, bf16[256,256]{1,0:T(8,128)(2,1)S(1)}, u32[]{:S(2)}, u32[]{:S(2)}) %collective-permute-start.20) | collective-permute-done | bytes 131104 | tf_op jit(solution)/shard_map/ppermute | solution.py:292
  133.2 4.0 %shard_map.91 = bf16[1024,256]{1,0:T(8,128)(2,1)} custom-call(s32[12]{0:T(128)} %stack.51.at_ref, bf16[2048,256]{1,0:T(8,128)(2,1)} %shard_map.88.a_ref, bf16[3072,256]{1,0:T(8,128)(2,1)} %copy-done, bf16[3072,256]{1,0:T(8,128)(2,1)} %copy-done.1, bf16[1024,256]{1,0:T(8,128)(2,1)} %copy-done.4, bf16[1024,256]{1,0:T(8,128)(2,1)} %copy-done.5, ...), custom_call_target="tpu_custom_call" | custom-call | flops 1073741824 | bytes 3145728 | tf_op jit(solution)/shard_map/pallas_call | solution.py:380
  137.2 3.9 %shard_map.90 = bf16[1024,256]{1,0:T(8,128)(2,1)} custom-call(s32[12]{0:T(128)} %stack.51.at_ref, bf16[2048,256]{1,0:T(8,128)(2,1)} %shard_map.88.a_ref, bf16[3072,256]{1,0:T(8,128)(2,1)} %copy-done, bf16[3072,256]{1,0:T(8,128)(2,1)} %copy-done.1, bf16[1024,256]{1,0:T(8,128)(2,1)} %copy-done.4, bf16[1024,256]{1,0:T(8,128)(2,1)} %copy-done.5, ...), custom_call_target="tpu_custom_call" | custom-call | flops 1073741824 | bytes 3145728 | tf_op jit(solution)/shard_map/pallas_call | solution.py:380
  142.6 5.5 %fusion = bf16[1,256,8192]{2,1,0:T(8,128)(2,1)} fusion(bf16[256,256]{1,0:T(8,128)(2,1)S(1)} %copy-done.3, bf16[8192,256]{1,0:T(8,128)(2,1)} %all-gather.2.cloned.1.call-done), kind=kOutput, calls=%fused_computation.1 | convolution fusion | flops 1075838976 | bytes 8519680 | tf_op jit(solution)/shard_map/dot_general | solution.py:395
  148.0 3.2 %collective-permute-done.22 = bf16[512,256]{1,0:T(8,128)(2,1)S(1)} collective-permute-done((bf16[512,256]{1,0:T(8,128)(2,1)S(1)}, bf16[512,256]{1,0:T(8,128)(2,1)S(1)}, u32[]{:S(2)}, u32[]{:S(2)}) %collective-permute-start.22) | collective-permute-done | bytes 262176 | tf_op jit(solution)/shard_map/ppermute | solution.py:264
  151.5 6.2 %collective-permute-done.23 = bf16[256,256]{1,0:T(8,128)(2,1)S(1)} collective-permute-done((bf16[256,256]{1,0:T(8,128)(2,1)S(1)}, bf16[256,256]{1,0:T(8,128)(2,1)S(1)}, u32[]{:S(2)}, u32[]{:S(2)}) %collective-permute-start.23) | collective-permute-done | bytes 131104 | tf_op jit(solution)/shard_map/ppermute | solution.py:264
  157.9 4.3 %collective-permute-done.24 = bf16[128,256]{1,0:T(8,128)(2,1)S(1)} collective-permute-done((bf16[128,256]{1,0:T(8,128)(2,1)S(1)}, bf16[128,256]{1,0:T(8,128)(2,1)S(1)}, u32[]{:S(2)}, u32[]{:S(2)}) %collective-permute-start.24) | collective-permute-done | bytes 65568 | tf_op jit(solution)/shard_map/ppermute | solution.py:275
  162.8 5.1 %collective-permute-done.25 = bf16[64,256]{1,0:T(8,128)(2,1)S(1)} collective-permute-done((bf16[64,256]{1,0:T(8,128)(2,1)S(1)}, bf16[64,256]{1,0:T(8,128)(2,1)S(1)}, u32[]{:S(2)}, u32[]{:S(2)}) %collective-permute-start.25) | collective-permute-done | bytes 32800 | tf_op jit(solution)/shard_map/ppermute | solution.py:275
  168.0 2.3 %collective-permute-start.26 = (bf16[32,256]{1,0:T(8,128)(2,1)S(1)}, bf16[32,256]{1,0:T(8,128)(2,1)S(1)}, u32[]{:S(2)}, u32[]{:S(2)}) collective-permute-start(bf16[32,256]{1,0:T(8,128)(2,1)S(1)} %slice.109), channel_id=1, source_target_pairs={{0,44},{1,45},{2,46},{3,47},{4,40},{5,41},{6,42},{7,43},{8,36},{9,... | collective-permute-start | bytes 49160 | tf_op jit(solution)/shard_map/ppermute | solution.py:275
  170.3 2.8 %collective-permute-done.26 = bf16[32,256]{1,0:T(8,128)(2,1)S(1)} collective-permute-done((bf16[32,256]{1,0:T(8,128)(2,1)S(1)}, bf16[32,256]{1,0:T(8,128)(2,1)S(1)}, u32[]{:S(2)}, u32[]{:S(2)}) %collective-permute-start.26) | collective-permute-done | bytes 16416 | tf_op jit(solution)/shard_map/ppermute | solution.py:275
  (92 shorter events, 17.4 us)
Async XLA Ops:
  7.2 135.4 %all-gather.2.cloned.1.call-start = ((), (), s32[]{:S(2)}) async-start(), calls=%async_computation | async-start | bytes 4456448 | tf_op jit(solution)/shard_map/all_gather | solution.py:437
  8.8 9.5 %collective-permute-start = (bf16[272,256]{1,0:T(8,128)(2,1)}, bf16[272,256]{1,0:T(8,128)(2,1)S(1)}, u32[]{:S(2)}, u32[]{:S(2)}) collective-permute-start(bf16[272,256]{1,0:T(8,128)(2,1)} %shard_map.85), channel_id=1, source_target_pairs={{0,4},{1,5},{2,6},{3,7},{4,8},{5,9},{6,10},{7,11},{8,12},{9,13},{1... | collective-permute-start | bytes 417800 | tf_op jit(solution)/shard_map/ppermute | solution.py:259
  9.0 12.7 %collective-permute-start.1 = (bf16[272,256]{1,0:T(8,128)(2,1)}, bf16[272,256]{1,0:T(8,128)(2,1)S(1)}, u32[]{:S(2)}, u32[]{:S(2)}) collective-permute-start(bf16[272,256]{1,0:T(8,128)(2,1)} %shard_map.85), channel_id=1, source_target_pairs={{0,8},{1,9},{2,10},{3,11},{4,12},{5,13},{6,14},{7,15},{8,0},{9,1},... | collective-permute-start | bytes 417800 | tf_op jit(solution)/shard_map/ppermute | solution.py:259
  12.2 9.4 %collective-permute-start.2 = (bf16[272,256]{1,0:T(8,128)(2,1)}, bf16[272,256]{1,0:T(8,128)(2,1)S(1)}, u32[]{:S(2)}, u32[]{:S(2)}) collective-permute-start(bf16[272,256]{1,0:T(8,128)(2,1)} %shard_map.85), channel_id=1, source_target_pairs={{0,12},{1,13},{2,14},{3,15},{4,0},{5,1},{6,2},{7,3},{8,4},{9,5},{1... | collective-permute-start | bytes 417800 | tf_op jit(solution)/shard_map/ppermute | solution.py:259
  21.7 15.7 %collective-permute-start.3 = (bf16[1088,256]{1,0:T(8,128)(2,1)S(1)}, bf16[1088,256]{1,0:T(8,128)(2,1)S(1)}, u32[]{:S(2)}, u32[]{:S(2)}) collective-permute-start(bf16[1088,256]{1,0:T(8,128)(2,1)S(1)} %pad_maximum_fusion.near_ref), channel_id=1, source_target_pairs={{0,1},{1,2},{2,3},{3,0},{4,5},{5,6},{6,7},{7,4},{8,9},{9,10},{10,1... | collective-permute-start | bytes 1671176 | tf_op jit(solution)/shard_map/ppermute | solution.py:252
  23.3 14.2 %collective-permute-start.4 = (bf16[1088,256]{1,0:T(8,128)(2,1)S(1)}, bf16[1088,256]{1,0:T(8,128)(2,1)S(1)}, u32[]{:S(2)}, u32[]{:S(2)}) collective-permute-start(bf16[1088,256]{1,0:T(8,128)(2,1)S(1)} %pad_maximum_fusion.near_ref), channel_id=1, source_target_pairs={{0,3},{1,0},{2,1},{3,2},{4,7},{5,4},{6,5},{7,6},{8,11},{9,8},{10,9... | collective-permute-start | bytes 1671176 | tf_op jit(solution)/shard_map/ppermute | solution.py:252
  37.5 8.8 %collective-permute-start.5 = (bf16[544,256]{1,0:T(8,128)(2,1)S(1)}, bf16[544,256]{1,0:T(8,128)(2,1)S(1)}, u32[]{:S(2)}, u32[]{:S(2)}) collective-permute-start(bf16[544,256]{1,0:T(8,128)(2,1)S(1)} %slice.72), channel_id=1, source_target_pairs={{0,1},{1,2},{2,3},{3,0},{4,5},{5,6},{6,7},{7,4},{8,9},{9,10},{10,1... | collective-permute-start | bytes 835592 | tf_op jit(solution)/shard_map/ppermute | solution.py:252
  39.0 7.3 %collective-permute-start.6 = (bf16[544,256]{1,0:T(8,128)(2,1)S(1)}, bf16[544,256]{1,0:T(8,128)(2,1)S(1)}, u32[]{:S(2)}, u32[]{:S(2)}) collective-permute-start(bf16[544,256]{1,0:T(8,128)(2,1)S(1)} %slice.73), channel_id=1, source_target_pairs={{0,3},{1,0},{2,1},{3,2},{4,7},{5,4},{6,5},{7,6},{8,11},{9,8},{10,9... | collective-permute-start | bytes 835592 | tf_op jit(solution)/shard_map/ppermute | solution.py:252
  40.9 44.1 %collective-permute-start.7 = (bf16[3072,256]{1,0:T(8,128)(2,1)}, bf16[3072,256]{1,0:T(8,128)(2,1)S(1)}, u32[]{:S(2)}, u32[]{:S(2)}) collective-permute-start(bf16[3072,256]{1,0:T(8,128)(2,1)} %shard_map.86), channel_id=1, source_target_pairs={{0,64},{16,80},{32,96},{48,112},{64,128},{80,144},{96,160},{112,17... | collective-permute-start | bytes 4718600 | tf_op jit(solution)/shard_map/ppermute | solution.py:292
  42.5 42.6 %collective-permute-start.8 = (bf16[3072,256]{1,0:T(8,128)(2,1)}, bf16[3072,256]{1,0:T(8,128)(2,1)S(1)}, u32[]{:S(2)}, u32[]{:S(2)}) collective-permute-start(bf16[3072,256]{1,0:T(8,128)(2,1)} %shard_map.87), channel_id=1, source_target_pairs={{0,192},{16,208},{32,224},{48,240},{64,0},{80,16},{96,32},{112,48}... | collective-permute-start | bytes 4718600 | tf_op jit(solution)/shard_map/ppermute | solution.py:292
  85.0 17.4 %copy-start.12 = (bf16[512,256]{1,0:T(8,128)(2,1)S(1)}, bf16[512,256]{1,0:T(8,128)(2,1)}, u32[]{:S(2)}) copy-start(bf16[512,256]{1,0:T(8,128)(2,1)} %get-tuple-element.60) | copy-start | bytes 786436
  85.0 17.5 %copy-start = (bf16[3072,256]{1,0:T(8,128)(2,1)}, bf16[3072,256]{1,0:T(8,128)(2,1)S(1)}, u32[]{:S(2)}) copy-start(bf16[3072,256]{1,0:T(8,128)(2,1)S(1)} %collective-permute-done.7.b_ref) | copy-start | bytes 4718596
  85.0 17.5 %copy-start.1 = (bf16[3072,256]{1,0:T(8,128)(2,1)}, bf16[3072,256]{1,0:T(8,128)(2,1)S(1)}, u32[]{:S(2)}) copy-start(bf16[3072,256]{1,0:T(8,128)(2,1)S(1)} %collective-permute-done.8.c_ref) | copy-start | bytes 4718596
  85.1 14.3 %collective-permute-start.9 = (bf16[1024,256]{1,0:T(8,128)(2,1)}, bf16[1024,256]{1,0:T(8,128)(2,1)S(1)}, u32[]{:S(2)}, u32[]{:S(2)}) collective-permute-start(bf16[1024,256]{1,0:T(8,128)(2,1)} %get-tuple-element.61), channel_id=1, source_target_pairs={{0,1},{1,2},{2,3},{3,0},{4,5},{5,6},{6,7},{7,4},{8,9},{9,10},{10,1... | collective-permute-start | bytes 1572872 | tf_op jit(solution)/shard_map/ppermute | solution.py:252
  85.2 14.1 %collective-permute-start.10 = (bf16[1024,256]{1,0:T(8,128)(2,1)}, bf16[1024,256]{1,0:T(8,128)(2,1)S(1)}, u32[]{:S(2)}, u32[]{:S(2)}) collective-permute-start(bf16[1024,256]{1,0:T(8,128)(2,1)} %get-tuple-element.62), channel_id=1, source_target_pairs={{0,3},{1,0},{2,1},{3,2},{4,7},{5,4},{6,5},{7,6},{8,11},{9,8},{10,9... | collective-permute-start | bytes 1572872 | tf_op jit(solution)/shard_map/ppermute | solution.py:252
  88.4 21.8 %copy-start.11 = (bf16[1024,256]{1,0:T(8,128)(2,1)S(1)}, bf16[1024,256]{1,0:T(8,128)(2,1)}, u32[]{:S(2)}) copy-start(bf16[1024,256]{1,0:T(8,128)(2,1)} %get-tuple-element.59) | copy-start | bytes 1572868
  99.4 6.9 %collective-permute-start.13 = (bf16[512,256]{1,0:T(8,128)(2,1)S(1)}, bf16[512,256]{1,0:T(8,128)(2,1)S(1)}, u32[]{:S(2)}, u32[]{:S(2)}) collective-permute-start(bf16[512,256]{1,0:T(8,128)(2,1)S(1)} %add_convert_fusion.3), channel_id=1, source_target_pairs={{0,3},{1,0},{2,1},{3,2},{4,7},{5,4},{6,5},{7,6},{8,11},{9,8},{10,9... | collective-permute-start | bytes 786440 | tf_op jit(solution)/shard_map/ppermute | solution.py:252
  102.5 7.7 %collective-permute-start.11 = (bf16[512,256]{1,0:T(8,128)(2,1)S(1)}, bf16[512,256]{1,0:T(8,128)(2,1)S(1)}, u32[]{:S(2)}, u32[]{:S(2)}) collective-permute-start(bf16[512,256]{1,0:T(8,128)(2,1)S(1)} %add_convert_fusion.5), channel_id=1, source_target_pairs={{0,1},{1,2},{2,3},{3,0},{4,5},{5,6},{6,7},{7,4},{8,9},{9,10},{10,1... | collective-permute-start | bytes 786440 | tf_op jit(solution)/shard_map/ppermute | solution.py:252
  102.6 20.0 %collective-permute-start.16 = (bf16[1024,256]{1,0:T(8,128)(2,1)S(1)}, bf16[1024,256]{1,0:T(8,128)(2,1)S(1)}, u32[]{:S(2)}, u32[]{:S(2)}) collective-permute-start(bf16[1024,256]{1,0:T(8,128)(2,1)S(1)} %slice.75), channel_id=1, source_target_pairs={{0,64},{16,80},{32,96},{48,112},{64,128},{80,144},{96,160},{112,17... | collective-permute-start | bytes 1572872 | tf_op jit(solution)/shard_map/ppermute | solution.py:292
  103.8 18.9 %collective-permute-start.17 = (bf16[1024,256]{1,0:T(8,128)(2,1)S(1)}, bf16[1024,256]{1,0:T(8,128)(2,1)S(1)}, u32[]{:S(2)}, u32[]{:S(2)}) collective-permute-start(bf16[1024,256]{1,0:T(8,128)(2,1)S(1)} %slice.76), channel_id=1, source_target_pairs={{0,192},{16,208},{32,224},{48,240},{64,0},{80,16},{96,32},{112,48}... | collective-permute-start | bytes 1572872 | tf_op jit(solution)/shard_map/ppermute | solution.py:292
  110.4 8.0 %collective-permute-start.12 = (bf16[256,256]{1,0:T(8,128)(2,1)S(1)}, bf16[256,256]{1,0:T(8,128)(2,1)S(1)}, u32[]{:S(2)}, u32[]{:S(2)}) collective-permute-start(bf16[256,256]{1,0:T(8,128)(2,1)S(1)} %get-tuple-element.81), channel_id=1, source_target_pairs={{0,12},{1,13},{2,14},{3,15},{4,0},{5,1},{6,2},{7,3},{8,4},{9,5},{1... | collective-permute-start | bytes 393224 | tf_op jit(solution)/shard_map/ppermute | solution.py:259
  111.3 11.3 %collective-permute-start.14 = (bf16[256,256]{1,0:T(8,128)(2,1)S(1)}, bf16[256,256]{1,0:T(8,128)(2,1)S(1)}, u32[]{:S(2)}, u32[]{:S(2)}) collective-permute-start(bf16[256,256]{1,0:T(8,128)(2,1)S(1)} %get-tuple-element.80), channel_id=1, source_target_pairs={{0,8},{1,9},{2,10},{3,11},{4,12},{5,13},{6,14},{7,15},{8,0},{9,1},... | collective-permute-start | bytes 393224 | tf_op jit(solution)/shard_map/ppermute | solution.py:259
  115.2 7.4 %collective-permute-start.15 = (bf16[256,256]{1,0:T(8,128)(2,1)S(1)}, bf16[256,256]{1,0:T(8,128)(2,1)S(1)}, u32[]{:S(2)}, u32[]{:S(2)}) collective-permute-start(bf16[256,256]{1,0:T(8,128)(2,1)S(1)} %get-tuple-element.79), channel_id=1, source_target_pairs={{0,4},{1,5},{2,6},{3,7},{4,8},{5,9},{6,10},{7,11},{8,12},{9,13},{1... | collective-permute-start | bytes 393224 | tf_op jit(solution)/shard_map/ppermute | solution.py:259
  122.8 6.3 %collective-permute-start.18 = (bf16[256,256]{1,0:T(8,128)(2,1)S(1)}, bf16[256,256]{1,0:T(8,128)(2,1)S(1)}, u32[]{:S(2)}, u32[]{:S(2)}) collective-permute-start(bf16[256,256]{1,0:T(8,128)(2,1)S(1)} %add_convert_fusion.7.g0), channel_id=1, source_target_pairs={{0,64},{16,80},{32,96},{48,112},{64,128},{80,144},{96,160},{112,17... | collective-permute-start | bytes 393224 | tf_op jit(solution)/shard_map/ppermute | solution.py:292
  124.5 5.0 %collective-permute-start.19 = (bf16[256,256]{1,0:T(8,128)(2,1)S(1)}, bf16[256,256]{1,0:T(8,128)(2,1)S(1)}, u32[]{:S(2)}, u32[]{:S(2)}) collective-permute-start(bf16[256,256]{1,0:T(8,128)(2,1)S(1)} %add_convert_fusion.7.g0), channel_id=1, source_target_pairs={{0,192},{16,208},{32,224},{48,240},{64,0},{80,16},{96,32},{112,48}... | collective-permute-start | bytes 393224 | tf_op jit(solution)/shard_map/ppermute | solution.py:292
  126.1 6.5 %collective-permute-start.20 = (bf16[256,256]{1,0:T(8,128)(2,1)S(1)}, bf16[256,256]{1,0:T(8,128)(2,1)S(1)}, u32[]{:S(2)}, u32[]{:S(2)}) collective-permute-start(bf16[256,256]{1,0:T(8,128)(2,1)S(1)} %add_convert_fusion.7.g0), channel_id=1, source_target_pairs={{0,128},{16,144},{32,160},{48,176},{64,192},{80,208},{96,224},{112... | collective-permute-start | bytes 393224 | tf_op jit(solution)/shard_map/ppermute | solution.py:292
  137.2 4.0 %collective-permute-start.21 = (bf16[1024,256]{1,0:T(8,128)(2,1)}, bf16[1024,256]{1,0:T(8,128)(2,1)S(1)}, u32[]{:S(2)}, u32[]{:S(2)}) collective-permute-start(bf16[1024,256]{1,0:T(8,128)(2,1)} %shard_map.91), channel_id=1, source_target_pairs={{0,16},{16,0},{32,48},{48,32},{64,80},{80,64},{96,112},{112,96},{1... | collective-permute-start | bytes 1572872 | tf_op jit(solution)/shard_map/ppermute | solution.py:463
  142.4 8.8 %collective-permute-start.22 = (bf16[512,256]{1,0:T(8,128)(2,1)S(1)}, bf16[512,256]{1,0:T(8,128)(2,1)S(1)}, u32[]{:S(2)}, u32[]{:S(2)}) collective-permute-start(bf16[512,256]{1,0:T(8,128)(2,1)S(1)} %slice.100), channel_id=1, source_target_pairs={{0,1},{1,0},{2,3},{3,2},{4,5},{5,4},{6,7},{7,6},{8,9},{9,8},{10,11... | collective-permute-start | bytes 786440 | tf_op jit(solution)/shard_map/ppermute | solution.py:264
  151.3 6.4 %collective-permute-start.23 = (bf16[256,256]{1,0:T(8,128)(2,1)S(1)}, bf16[256,256]{1,0:T(8,128)(2,1)S(1)}, u32[]{:S(2)}, u32[]{:S(2)}) collective-permute-start(bf16[256,256]{1,0:T(8,128)(2,1)S(1)} %slice.103), channel_id=1, source_target_pairs={{0,3},{1,2},{2,1},{3,0},{4,7},{5,6},{6,5},{7,4},{8,11},{9,10},{10,... | collective-permute-start | bytes 393224 | tf_op jit(solution)/shard_map/ppermute | solution.py:264
  157.8 4.4 %collective-permute-start.24 = (bf16[128,256]{1,0:T(8,128)(2,1)S(1)}, bf16[128,256]{1,0:T(8,128)(2,1)S(1)}, u32[]{:S(2)}, u32[]{:S(2)}) collective-permute-start(bf16[128,256]{1,0:T(8,128)(2,1)S(1)} %slice.105), channel_id=1, source_target_pairs={{0,4},{1,5},{2,6},{3,7},{4,0},{5,1},{6,2},{7,3},{8,12},{9,13},{10,... | collective-permute-start | bytes 196616 | tf_op jit(solution)/shard_map/ppermute | solution.py:275
  162.2 5.8 %collective-permute-start.25 = (bf16[64,256]{1,0:T(8,128)(2,1)S(1)}, bf16[64,256]{1,0:T(8,128)(2,1)S(1)}, u32[]{:S(2)}, u32[]{:S(2)}) collective-permute-start(bf16[64,256]{1,0:T(8,128)(2,1)S(1)} %slice.107), channel_id=1, source_target_pairs={{0,12},{1,13},{2,14},{3,15},{4,8},{5,9},{6,10},{7,11},{8,4},{9,5},... | collective-permute-start | bytes 98312 | tf_op jit(solution)/shard_map/ppermute | solution.py:275
  168.0 5.0 %collective-permute-start.26 = (bf16[32,256]{1,0:T(8,128)(2,1)S(1)}, bf16[32,256]{1,0:T(8,128)(2,1)S(1)}, u32[]{:S(2)}, u32[]{:S(2)}) collective-permute-start(bf16[32,256]{1,0:T(8,128)(2,1)S(1)} %slice.109), channel_id=1, source_target_pairs={{0,44},{1,45},{2,46},{3,47},{4,40},{5,41},{6,42},{7,43},{8,36},{9,... | collective-permute-start | bytes 49160 | tf_op jit(solution)/shard_map/ppermute | solution.py:275
  (14 other events, 82.9 us)
Sparse Core Ops, SparseCore 0:
  25.2 80.8 all-gather.1
